TPU v7x, 512 devices: a whole 4x4x16 slice. The times are simulated.
512 devices in a mesh: wide: 64 (over z, x), narrow: 8 (over y, core).
Axes of the slice: x: 4, y: 4, z: 16, core: 2. Of those that a mesh axis runs over, the one named last changes fastest.
Arguments:
- fine_state: bfloat16 [524288, 256], P(('wide', 'narrow')), may hold values from -6 to 6
- l2_state: bfloat16 [16384, 256], P('wide'), may hold values from -3 to 3
- l3_state: bfloat16 [4096, 256], replicated, may hold values from -3 to 3
- boundary: int32 [8192], P(('wide', 'narrow')), may hold values from 0 to 1023
- senders: int32 [1048576], P(('wide', 'narrow')), may hold values from 0 to 1407
- receivers: int32 [1048576], P(('wide', 'narrow')), may hold values from 0 to 1024
- up_parent: int32 [524288], P(('wide', 'narrow')), may hold values from 0 to 255
- l2_parent: int32 [16384], P('wide'), may hold values from 0 to 4095, as said below
- msg_in: bfloat16 [512, 256], replicated, may hold values from -0.25 to 0.25
- msg_out: bfloat16 [256, 256], replicated, may hold values from -0.375 to 0.375
- fine_gain: float32 [256], replicated, may hold values from 0.1 to 1.9
- up_weight: bfloat16 [256, 256], replicated, may hold values from -0.375 to 0.375
- l2_gain: float32 [256], replicated, may hold values from 0.1 to 1.9
- l3_gain: float32 [256], replicated, may hold values from 0.1 to 1.9
- l3_w1: bfloat16 [256, 256], replicated, may hold values from -0.375 to 0.375
- l3_w2: bfloat16 [256, 256], replicated, may hold values from -0.375 to 0.375
- down_weight: bfloat16 [256, 256], replicated, may hold values from -0.375 to 0.375
- fine_down: bfloat16 [256, 256], replicated, may hold values from -0.375 to 0.375
Outputs:
- fine_out: bfloat16 [524288, 256], P(('wide', 'narrow'))
- l2_down: bfloat16 [16384, 256], P('wide')
Inputs may be any that keep to these rules, and one draw needn't show every extreme that they name: `boundary`: local fine node indices. `senders`: index into the device's pool of 1408 rows. `receivers`: 1024 marks a padding slot. `up_parent`: index among the 256 level-2 nodes of the device's patch. `l2_parent`: the parent of a level-2 node of patch w lies in one of the level-3 blocks w - 1, w, w + 1 (modulo 64), block b being nodes b * 64 to b * 64 + 63.
All inputs are finite; a program needn't handle non-finite values.
Results may differ from a plain program's by a relative error of at most 0.014.
Values may be sent and summed in bfloat16 or wider, within the bound.
No kernel may reach another device: no remote copies, remote signals or barrier semaphores. Data moves between devices by JAX's collectives and lax.ppermute only.
A program may use at most 64 MiB of HBM per device.

v0:
```python
import jax
import jax.numpy as jnp
from jax import lax
from jax.sharding import PartitionSpec as P


def extended(cells, sides, width):
    for axis, dim in sides:
        count = lax.axis_size(axis)
        head = lax.slice_in_dim(cells, 0, width, axis=dim)
        tail = lax.slice_in_dim(cells, cells.shape[dim] - width, cells.shape[dim], axis=dim)
        cells = jnp.concatenate(
            [
                lax.ppermute(tail, axis, [(i, (i + 1) % count) for i in range(count)]),
                cells,
                lax.ppermute(head, axis, [((i + 1) % count, i) for i in range(count)]),
            ],
            axis=dim,
        )
    return cells


def passed_along(value, axis, steps):
    count = lax.axis_size(axis)
    pairs = [(source, (source + steps) % count) for source in range(count)]
    return lax.ppermute(value, axis, pairs)


def rms_scale(values, gain):
    return values * lax.rsqrt(jnp.mean(values * values, axis=-1, keepdims=True) + 1e-05) * gain


def one_hot_rows(index, count):
    return (index[:, None] == jnp.arange(count, dtype=jnp.int32)[None, :]).astype(jnp.bfloat16)


def coarse_update(coarse_sum, state_rows, l3_gain, l3_w1, l3_w2):
    l3_mid = (state_rows.astype(jnp.float32) + rms_scale(coarse_sum, l3_gain)).astype(jnp.bfloat16)
    l3_hidden = jax.nn.silu(jnp.dot(l3_mid, l3_w1, preferred_element_type=jnp.float32)).astype(
        jnp.bfloat16
    )
    return (
        l3_mid.astype(jnp.float32) + jnp.dot(l3_hidden, l3_w2, preferred_element_type=jnp.float32)
    ).astype(jnp.bfloat16)


def body(
    fine_state,
    l2_state,
    l3_state,
    boundary,
    senders,
    receivers,
    up_parent,
    l2_parent,
    msg_in,
    msg_out,
    fine_gain,
    up_weight,
    l2_gain,
    l3_gain,
    l3_w1,
    l3_w2,
    down_weight,
    fine_down,
):
    node_count = fine_state.shape[0]
    level_two = l2_state.shape[0]
    level_three = l3_state.shape[0]
    exported = jnp.take(fine_state, boundary, axis=0)
    patch = lax.all_gather(exported, "narrow", axis=0, tiled=True)
    beside_all = extended(patch, (("wide", 0),), patch.shape[0])
    pool = jnp.concatenate([fine_state, beside_all], axis=0)
    sender_rows = jnp.take(pool, senders, axis=0)
    receiver_rows = jnp.take(fine_state, jnp.minimum(receivers, node_count - 1), axis=0)
    joined = jnp.concatenate([sender_rows, receiver_rows], axis=1)
    edge_hidden = jax.nn.silu(jnp.dot(joined, msg_in, preferred_element_type=jnp.float32)).astype(
        jnp.bfloat16
    )
    message = jnp.dot(edge_hidden, msg_out, preferred_element_type=jnp.float32).astype(jnp.bfloat16)
    incidence = (receivers[None, :] == jnp.arange(node_count, dtype=jnp.int32)[:, None]).astype(
        jnp.bfloat16
    )
    fine_agg = jnp.dot(incidence, message, preferred_element_type=jnp.float32)
    fine_mid = (fine_state.astype(jnp.float32) + rms_scale(fine_agg, fine_gain)).astype(
        jnp.bfloat16
    )
    up_term = jnp.dot(fine_mid, up_weight, preferred_element_type=jnp.float32).astype(jnp.bfloat16)
    fine_parent = one_hot_rows(up_parent, level_two)
    partial_two = lax.dot_general(
        fine_parent, up_term, (((0,), (0,)), ((), ())), preferred_element_type=jnp.float32
    )
    l2_sum = lax.psum(partial_two, "narrow")
    l2_mid = (l2_state.astype(jnp.float32) + rms_scale(l2_sum, l2_gain)).astype(jnp.bfloat16)
    block_rows = level_three // lax.axis_size("wide")
    window_start = (lax.axis_index("wide") - 1) * block_rows
    local_parent = (l2_parent - window_start + level_three) % level_three
    coarse_parent = one_hot_rows(local_parent, 3 * block_rows)
    partial_three = lax.dot_general(
        coarse_parent, l2_mid, (((0,), (0,)), ((), ())), preferred_element_type=jnp.float32
    )
    from_behind = passed_along(partial_three[2 * block_rows :], "wide", 1)
    from_ahead = passed_along(partial_three[:block_rows], "wide", -1)
    own_sum = partial_three[block_rows : 2 * block_rows] + from_behind + from_ahead
    state_rows = lax.dynamic_slice_in_dim(
        l3_state, lax.axis_index("wide") * block_rows, block_rows, 0
    )
    new_rows = coarse_update(own_sum, state_rows, l3_gain, l3_w1, l3_w2)
    l3_new = extended(new_rows, (("wide", 0),), block_rows)
    picked = jnp.dot(coarse_parent, l3_new, preferred_element_type=jnp.float32).astype(jnp.bfloat16)
    l2_down = (
        l2_mid.astype(jnp.float32)
        + jnp.dot(picked, down_weight, preferred_element_type=jnp.float32)
    ).astype(jnp.bfloat16)
    picked_fine = jnp.dot(fine_parent, l2_down, preferred_element_type=jnp.float32).astype(
        jnp.bfloat16
    )
    fine_out = (
        fine_mid.astype(jnp.float32)
        + jnp.dot(picked_fine, fine_down, preferred_element_type=jnp.float32)
    ).astype(jnp.bfloat16)
    return (fine_out, l2_down)


def solution(mesh):
    return jax.shard_map(
        body,
        mesh=mesh,
        in_specs=(
            P(("wide", "narrow"), None),
            P("wide", None),
            P(),
            P(("wide", "narrow")),
            P(("wide", "narrow")),
            P(("wide", "narrow")),
            P(("wide", "narrow")),
            P("wide"),
            P(),
            P(),
            P(),
            P(),
            P(),
            P(),
            P(),
            P(),
            P(),
            P(),
        ),
        out_specs=(P(("wide", "narrow"), None), P("wide", None)),
        check_vma=False,
    )
```

profile of v0, /device:TPU:102, one launch (start us, length us, event | category | flops | bytes accessed | tf_op | source)
XLA Modules:
  0.0 175.8 jit_solution(6069404574955320261)
XLA Ops:
  7.2 0.0 copy-start
  7.2 0.0 all-reduce.2.cloned.1.call-start
  7.2 0.7 compare_select_fusion.2
  7.9 0.7 compare_and_fusion.2
  8.6 1.7 gather_fusion
  10.3 0.1 broadcast_select_fusion.2
  10.4 13.3 %all_gather.3 = bf16[128,256]{1,0:T(8,128)(2,1)S(1)} all-gather(bf16[16,256]{1,0:T(8,128)(2,1)S(1)} %broadcast_select_fusion.2), channel_id=1, replica_groups=mesh['wide'=64,'narrow'=8] {'narrow'}, dimensions={0}, use_global_device_ids=true | all-gather | bytes 73728 | tf_op jit(solution)/shard_map/all_gather | solution.py:71
  23.6 4.9 %collective-permute-start = (bf16[128,256]{1,0:T(8,128)(2,1)S(1)}, bf16[128,256]{1,0:T(8,128)(2,1)S(1)}, u32[]{:S(2)}, u32[]{:S(2)}) collective-permute-start(bf16[128,256]{1,0:T(8,128)(2,1)S(1)} %all_gather.3), channel_id=1, source_target_pairs={{0,8},{8,16},{16,24},{24,32},{32,40},{40,48},{48,56},{56,64},{64,7... | collective-permute-start | bytes 196616 | tf_op jit(solution)/shard_map/ppermute | solution.py:14
  28.6 1.9 %collective-permute-start.1 = (bf16[128,256]{1,0:T(8,128)(2,1)S(1)}, bf16[128,256]{1,0:T(8,128)(2,1)S(1)}, u32[]{:S(2)}, u32[]{:S(2)}) collective-permute-start(bf16[128,256]{1,0:T(8,128)(2,1)S(1)} %all_gather.3), channel_id=1, source_target_pairs={{8,0},{16,8},{24,16},{32,24},{40,32},{48,40},{56,48},{64,56},{72,6... | collective-permute-start | bytes 196616 | tf_op jit(solution)/shard_map/ppermute | solution.py:16
  30.5 0.7 fusion.35
  31.2 0.7 compare_and_fusion
  31.9 0.7 fusion.34
  32.6 7.7 %gather_fusion.2 = bf16[2048,256]{1,0:T(8,128)(2,1)S(1)} fusion(bf16[1024,256]{1,0:T(8,128)(2,1)} %param.18, s32[2048]{0:T(1024)S(1)} %fusion.35), kind=kCustom, calls=%fused_computation.2 | custom fusion | bytes 2105344 | tf_op jit(solution)/shard_map/jit(_take)/gather | solution.py:75
  40.3 0.0 copy-start.4
  40.4 0.0 copy-start.1
  40.4 1.3 broadcast_select_fusion
  41.7 0.2 copy.20
  41.9 0.1 pad_maximum_fusion
  42.0 7.5 %gather_fusion.1 = bf16[2048,256]{1,0:T(8,128)(2,1)S(1)} fusion(bf16[1408,256]{1,0:T(8,128)(2,1)S(1)} %pad_maximum_fusion, s32[2048]{0:T(1024)S(1)} %fusion.34), kind=kCustom, calls=%fused_computation.1 | custom fusion | bytes 2105344 | tf_op jit(solution)/shard_map/jit(_take)/gather | solution.py:74
  49.5 1.2 broadcast_select_fusion.1
  50.7 0.1 copy-done.2
  50.8 0.1 copy-done.9
  50.9 3.4 %convolution_convert_fusion = bf16[2048,256]{1,0:T(8,128)(2,1)} fusion(bf16[256,256]{1,0:T(8,128)(2,1)S(1)} %copy-done.9, bf16[512,256]{1,0:T(8,128)(2,1)S(1)} %copy-done, bf16[2048,256]{1,0:T(8,128)(2,1)S(1)} %copy-done.2, bf16[2048,256]{1,0:T(8,128)(2,1)} %broadcast_select_fusion.1), kind=kOutput, calls=%fused_computation.6 | convolution fusion | flops 812646400 | bytes 3538944 | tf_op jit(solution)/shard_map/dot_general | solution.py:80
  54.3 3.2 %multiply_reduce_fusion = (f32[1024]{0:T(1024)S(1)}, f32[1024,256]{0,1:T(8,128)S(1)}) fusion(bf16[2048,256]{1,0:T(8,128)(2,1)} %convolution_convert_fusion, s32[2048]{0:T(1024)S(1)} %copy-done.5), kind=kOutput, calls=%fused_computation.24 | convolution fusion | flops 1076362240 | bytes 2109440 | tf_op jit(solution)/shard_map/dot_general | solution.py:84
  57.5 0.0 copy-start.15
  57.5 0.0 copy-start.8
  57.6 0.0 copy-start.3
  57.6 0.0 copy-start.7
  57.6 0.2 add_convert_fusion
  57.8 0.6 copy-done.10
  58.4 1.5 fusion.11
  59.9 0.0 all-reduce.2.cloned.1.call-update
  60.0 77.9 %all-reduce.2.cloned.1.call-done = f32[256,256]{1,0:T(8,128)} async-done(((f32[256,256]{1,0:T(8,128)}), f32[256,256]{1,0:T(8,128)}) %all-reduce.2.cloned.1.call-update) | async-done | bytes 262160 | tf_op jit(solution)/shard_map/psum | solution.py:93
  137.9 1.1 multiply_reduce_fusion.1
  139.0 1.1 add_convert_fusion.1
  140.0 0.3 fusion.18
  140.4 4.7 %collective-permute-start.2 = (f32[64,256]{1,0:T(8,128)S(1)}, f32[64,256]{1,0:T(8,128)S(1)}, u32[]{:S(2)}, u32[]{:S(2)}) collective-permute-start(f32[64,256]{1,0:T(8,128)S(1)} %get-tuple-element.4), channel_id=1, source_target_pairs={{0,8},{8,16},{16,24},{24,32},{32,40},{40,48},{48,56},{56,64},{64,7... | collective-permute-start | bytes 196616 | tf_op jit(solution)/shard_map/ppermute | solution.py:26
  145.0 1.9 %collective-permute-start.3 = (f32[64,256]{1,0:T(8,128)S(1)}, f32[64,256]{1,0:T(8,128)S(1)}, u32[]{:S(2)}, u32[]{:S(2)}) collective-permute-start(f32[64,256]{1,0:T(8,128)S(1)} %get-tuple-element.5), channel_id=1, source_target_pairs={{0,504},{8,0},{16,8},{24,16},{32,24},{40,32},{48,40},{56,48},{64,5... | collective-permute-start | bytes 196616 | tf_op jit(solution)/shard_map/ppermute | solution.py:26
  147.0 7.5 %collective-permute-done.3 = f32[64,256]{1,0:T(8,128)S(1)} collective-permute-done((f32[64,256]{1,0:T(8,128)S(1)}, f32[64,256]{1,0:T(8,128)S(1)}, u32[]{:S(2)}, u32[]{:S(2)}) %collective-permute-start.3) | collective-permute-done | bytes 65568 | tf_op jit(solution)/shard_map/ppermute | solution.py:26
  154.5 0.1 multiply_reduce_fusion.2
  154.7 1.2 fusion.13
  155.8 1.9 %collective-permute-start.4 = (bf16[64,256]{1,0:T(8,128)(2,1)S(1)}, bf16[64,256]{1,0:T(8,128)(2,1)S(1)}, u32[]{:S(2)}, u32[]{:S(2)}) collective-permute-start(bf16[64,256]{1,0:T(8,128)(2,1)S(1)} %fusion.13), channel_id=1, source_target_pairs={{0,8},{8,16},{16,24},{24,32},{32,40},{40,48},{48,56},{56,64},{64,7... | collective-permute-start | bytes 98312 | tf_op jit(solution)/shard_map/ppermute | solution.py:14
  157.8 3.9 %collective-permute-start.5 = (bf16[64,256]{1,0:T(8,128)(2,1)S(1)}, bf16[64,256]{1,0:T(8,128)(2,1)S(1)}, u32[]{:S(2)}, u32[]{:S(2)}) collective-permute-start(bf16[64,256]{1,0:T(8,128)(2,1)S(1)} %fusion.13), channel_id=1, source_target_pairs={{8,0},{16,8},{24,16},{32,24},{40,32},{48,40},{56,48},{64,56},{72,6... | collective-permute-start | bytes 98312 | tf_op jit(solution)/shard_map/ppermute | solution.py:16
  161.7 5.2 %collective-permute-done.5 = bf16[64,256]{1,0:T(8,128)(2,1)S(1)} collective-permute-done((bf16[64,256]{1,0:T(8,128)(2,1)S(1)}, bf16[64,256]{1,0:T(8,128)(2,1)S(1)}, u32[]{:S(2)}, u32[]{:S(2)}) %collective-permute-start.5) | collective-permute-done | bytes 32800 | tf_op jit(solution)/shard_map/ppermute | solution.py:16
  166.9 0.4 fusion.12
  167.3 0.0 copy-start.17
  167.3 0.6 fusion.10
  167.9 1.0 copy.22
  (36 shorter events, 0.1 us)
Async XLA Ops:
  7.2 43.6 %copy-start = (bf16[512,256]{1,0:T(8,128)(2,1)S(1)}, bf16[512,256]{1,0:T(8,128)(2,1)}, u32[]{:S(2)}) copy-start(bf16[512,256]{1,0:T(8,128)(2,1)} %param.26) | copy-start | bytes 786436
  7.2 130.7 %all-reduce.2.cloned.1.call-start = ((), (), s32[]{:S(2)}) async-start(), calls=%async_computation | async-start | bytes 524288 | tf_op jit(solution)/shard_map/psum | solution.py:93
  23.6 18.3 %collective-permute-start = (bf16[128,256]{1,0:T(8,128)(2,1)S(1)}, bf16[128,256]{1,0:T(8,128)(2,1)S(1)}, u32[]{:S(2)}, u32[]{:S(2)}) collective-permute-start(bf16[128,256]{1,0:T(8,128)(2,1)S(1)} %all_gather.3), channel_id=1, source_target_pairs={{0,8},{8,16},{16,24},{24,32},{32,40},{40,48},{48,56},{56,64},{64,7... | collective-permute-start | bytes 196616 | tf_op jit(solution)/shard_map/ppermute | solution.py:14
  28.6 13.3 %collective-permute-start.1 = (bf16[128,256]{1,0:T(8,128)(2,1)S(1)}, bf16[128,256]{1,0:T(8,128)(2,1)S(1)}, u32[]{:S(2)}, u32[]{:S(2)}) collective-permute-start(bf16[128,256]{1,0:T(8,128)(2,1)S(1)} %all_gather.3), channel_id=1, source_target_pairs={{8,0},{16,8},{24,16},{32,24},{40,32},{48,40},{56,48},{64,56},{72,6... | collective-permute-start | bytes 196616 | tf_op jit(solution)/shard_map/ppermute | solution.py:16
  40.3 1.3 copy-start.4
  40.4 1.3 copy-start.1
  49.5 1.3 copy-start.2
  49.5 1.4 copy-start.9
  50.9 3.4 %copy-start.5 = (s32[2048]{0:T(1024)S(1)}, s32[2048]{0:T(1024)}, u32[]{:S(2)}) copy-start(s32[2048]{0:T(1024)} %param.23) | copy-start | bytes 24580
  54.3 3.3 %copy-start.6 = (f32[256]{0:T(256)S(1)}, f32[256]{0:T(256)}, u32[]{:S(2)}) copy-start(f32[256]{0:T(256)} %param.28) | copy-start | bytes 3076
  57.5 0.9 copy-start.10
  57.5 0.9 copy-start.15
  57.5 2.4 %copy-start.8 = (s32[256]{0:T(256)S(1)}, s32[256]{0:T(256)}, u32[]{:S(2)}) copy-start(s32[256]{0:T(256)} %param.25) | copy-start | bytes 3076
  57.6 81.4 %copy-start.3 = (bf16[256,256]{1,0:T(8,128)(2,1)S(1)}, bf16[256,256]{1,0:T(8,128)(2,1)}, u32[]{:S(2)}) copy-start(bf16[256,256]{1,0:T(8,128)(2,1)} %param.19) | copy-start | bytes 393220
  57.6 81.4 %copy-start.7 = (f32[256]{0:T(256)S(1)}, f32[256]{0:T(256)}, u32[]{:S(2)}) copy-start(f32[256]{0:T(256)} %param.30) | copy-start | bytes 3076
  58.4 96.2 %copy-start.11 = (bf16[256,256]{1,0:T(8,128)(2,1)S(1)}, bf16[256,256]{1,0:T(8,128)(2,1)}, u32[]{:S(2)}) copy-start(bf16[256,256]{1,0:T(8,128)(2,1)} %param.33) | copy-start | bytes 393220
  58.4 96.2 %copy-start.12 = (bf16[256,256]{1,0:T(8,128)(2,1)S(1)}, bf16[256,256]{1,0:T(8,128)(2,1)}, u32[]{:S(2)}) copy-start(bf16[256,256]{1,0:T(8,128)(2,1)} %param.32) | copy-start | bytes 393220
  58.4 96.3 %copy-start.16 = (f32[256]{0:T(256)S(1)}, f32[256]{0:T(256)}, u32[]{:S(2)}) copy-start(f32[256]{0:T(256)} %param.31) | copy-start | bytes 3076
  58.4 108.5 %copy-start.13 = (bf16[256,256]{1,0:T(8,128)(2,1)S(1)}, bf16[256,256]{1,0:T(8,128)(2,1)}, u32[]{:S(2)}) copy-start(bf16[256,256]{1,0:T(8,128)(2,1)} %param.34) | copy-start | bytes 393220
  58.4 108.9 %copy-start.14 = (bf16[256,256]{1,0:T(8,128)(2,1)S(1)}, bf16[256,256]{1,0:T(8,128)(2,1)}, u32[]{:S(2)}) copy-start(bf16[256,256]{1,0:T(8,128)(2,1)} %param.35) | copy-start | bytes 393220
  140.4 6.6 %collective-permute-start.2 = (f32[64,256]{1,0:T(8,128)S(1)}, f32[64,256]{1,0:T(8,128)S(1)}, u32[]{:S(2)}, u32[]{:S(2)}) collective-permute-start(f32[64,256]{1,0:T(8,128)S(1)} %get-tuple-element.4), channel_id=1, source_target_pairs={{0,8},{8,16},{16,24},{24,32},{32,40},{40,48},{48,56},{56,64},{64,7... | collective-permute-start | bytes 196616 | tf_op jit(solution)/shard_map/ppermute | solution.py:26
  145.0 9.5 %collective-permute-start.3 = (f32[64,256]{1,0:T(8,128)S(1)}, f32[64,256]{1,0:T(8,128)S(1)}, u32[]{:S(2)}, u32[]{:S(2)}) collective-permute-start(f32[64,256]{1,0:T(8,128)S(1)} %get-tuple-element.5), channel_id=1, source_target_pairs={{0,504},{8,0},{16,8},{24,16},{32,24},{40,32},{48,40},{56,48},{64,5... | collective-permute-start | bytes 196616 | tf_op jit(solution)/shard_map/ppermute | solution.py:26
  155.8 5.9 %collective-permute-start.4 = (bf16[64,256]{1,0:T(8,128)(2,1)S(1)}, bf16[64,256]{1,0:T(8,128)(2,1)S(1)}, u32[]{:S(2)}, u32[]{:S(2)}) collective-permute-start(bf16[64,256]{1,0:T(8,128)(2,1)S(1)} %fusion.13), channel_id=1, source_target_pairs={{0,8},{8,16},{16,24},{24,32},{32,40},{40,48},{48,56},{56,64},{64,7... | collective-permute-start | bytes 98312 | tf_op jit(solution)/shard_map/ppermute | solution.py:14
  157.8 9.1 %collective-permute-start.5 = (bf16[64,256]{1,0:T(8,128)(2,1)S(1)}, bf16[64,256]{1,0:T(8,128)(2,1)S(1)}, u32[]{:S(2)}, u32[]{:S(2)}) collective-permute-start(bf16[64,256]{1,0:T(8,128)(2,1)S(1)} %fusion.13), channel_id=1, source_target_pairs={{8,0},{16,8},{24,16},{32,24},{40,32},{48,40},{56,48},{64,56},{72,6... | collective-permute-start | bytes 98312 | tf_op jit(solution)/shard_map/ppermute | solution.py:16
  167.3 1.6 copy-start.17
Sparse Core Ops, SparseCore 0:
  60.1 77.7 all-reduce.1
where the time goes:
time: 177 us; the launch traced here: 176 us
  waiting for transfers between devices  90.6 us (51%)
  starting transfers between devices  19.3 us (11%)
  local copies, waits for them, and re-layouts  19 us (11%)
  between operations  14.4 us (8%)
  blocking collectives  13.3 us (8%)
  matrix products  10.6 us (6%)
  other arithmetic  8.6 us (5%)
    psum x1, waiting for transfers between devices, body(): l2_sum = lax.psum(partial_two, 'narrow')  77.9 us
    all_gather x1, blocking collectives, body(): patch = lax.all_gather(exported, 'narrow', axis=0, tiled=True)  13.3 us
    gather x1, local copies, waits for them, and re-layouts, body(): jnp.take(fine_state, jnp.minimum(receivers, node_count - 1), axis=0)  7.75 us
    ppermute x2, waiting for transfers between devices, passed_along(): return lax.ppermute(value, axis, pairs)  7.54 us
    gather x1, local copies, waits for them, and re-layouts, body(): sender_rows = jnp.take(pool, senders, axis=0)  7.5 us
    ppermute x2, starting transfers between devices, extended(): lax.ppermute(tail, axis, [(i, (i + 1) % count) for i in range(count)])  6.86 us
    ppermute x2, starting transfers between devices, passed_along(): return lax.ppermute(value, axis, pairs)  6.58 us
    ppermute x2, starting transfers between devices, extended(): lax.ppermute(head, axis, [((i + 1) % count, i) for i in range(count)])  5.84 us
  transfers between devices with their start and end apart: 7, of which 3 were waited for; matrix products, arithmetic and copies ran while one was open for 6% of the time, Pallas kernels for 0%

commit v1 on v0

v1 whole, which is shorter than its diff:
```python
import functools

import jax
import jax.numpy as jnp
from jax import lax
from jax.experimental import pallas as pl
from jax.experimental.pallas import tpu as pltpu
from jax.sharding import PartitionSpec as P

F32 = jnp.float32
BF16 = jnp.bfloat16
LANES = 128
EDGE_BLOCK = 512


def dot(a, b):
    return jnp.dot(a, b, preferred_element_type=F32)


def rms_scale(values, gain):
    return values * lax.rsqrt(jnp.mean(values * values, axis=-1, keepdims=True) + 1e-05) * gain


def silu(x):
    half = 0.5 * x
    return half + half * jnp.tanh(half)


def column_parts(index):
    low = (index & (LANES - 1)).astype(F32)
    high = (index >> 7).astype(F32)
    return low.T, high.T


def lane_select(low_col, high_col):
    lane = lax.broadcasted_iota(jnp.int32, (LANES, LANES), 1).astype(F32)
    low = jnp.broadcast_to(low_col, (LANES, LANES))
    hot = jnp.where(low == lane, 1.0, 0.0).astype(BF16)
    high = jnp.broadcast_to(high_col, (LANES, LANES)).astype(BF16)
    return hot, high


def row_select(index_row):
    sub = lax.broadcasted_iota(jnp.int32, (LANES, LANES), 0)
    hot = jnp.where((index_row & (LANES - 1)) == sub, 1.0, 0.0).astype(BF16)
    high = jnp.broadcast_to((index_row >> 7).astype(F32), (LANES, LANES)).astype(BF16)
    return hot, high


def pick(hot, high, tile):
    return jnp.where(high == jnp.asarray(tile, BF16), hot, jnp.zeros_like(hot))


def fetch(pairs, sems):
    copies = [pltpu.make_async_copy(a, b, sems.at[k]) for k, (a, b) in enumerate(pairs)]
    for copy in copies:
        copy.start()
    for copy in copies:
        copy.wait()


def gathered(index_ref, proj, hot, out_ref, before_ref=None):
    tiles = proj.shape[0] // LANES
    low, high = column_parts(index_ref[...])
    for block in range(out_ref.shape[0] // EDGE_BLOCK):
        for part in range(EDGE_BLOCK // LANES):
            j = block * (EDGE_BLOCK // LANES) + part
            span = slice(j * LANES, (j + 1) * LANES)
            hot_j, high_j = lane_select(low[:, j : j + 1], high[:, j : j + 1])
            for t in range(tiles):
                hot[span, t * LANES : (t + 1) * LANES] = pick(hot_j, high_j, t)
        span = slice(block * EDGE_BLOCK, (block + 1) * EDGE_BLOCK)
        rows = dot(hot[span], proj[...])
        out_ref[span] = rows if before_ref is None else rows + before_ref[span]


def receiver_kernel(fs_hbm, recv_hbm, w_in_hbm, pre_ref, fs, recv, w_in, proj, hot, sems):
    width = fs.shape[1]
    fetch([(fs_hbm, fs), (recv_hbm, recv), (w_in_hbm.at[pl.ds(width, width)], w_in)], sems)
    proj[...] = dot(fs[...], w_in[...]).astype(BF16)
    gathered(recv, proj, hot, pre_ref)


def sender_kernel(
    before_ref, fs_hbm, send_hbm, w_in_hbm, l3_hbm, pre_ref, l3_rows_ref, fs, send, w_in, proj, hot, sems
):
    width = fs.shape[1]
    wide = lax.axis_index("wide")
    count = lax.axis_size("wide")
    rows = l3_rows_ref.shape[0] // 3
    pairs = [(fs_hbm, fs), (send_hbm, send), (w_in_hbm.at[pl.ds(0, width)], w_in)]
    for k in range(3):
        block = lax.rem(wide + (k + count - 1), count)
        pairs.append(
            (
                l3_hbm.at[pl.ds(pl.multiple_of(block * rows, rows), rows)],
                l3_rows_ref.at[pl.ds(k * rows, rows)],
            )
        )
    fetch(pairs, sems)
    proj[...] = dot(fs[...], w_in[...]).astype(BF16)
    gathered(send, proj, hot, pre_ref, before_ref)


def fine_kernel(
    pre_ref, around_ref, fs_ref, send_ref, recv_ref, par_ref, w_in_ref, w_out_ref, gain_ref,
    mid_ref, keep_ref, give_ref, hidden, hot, inc, sums,
):
    nodes, width = fs_ref.shape
    edges = pre_ref.shape[0]
    tiles = nodes // LANES
    extra = around_ref.shape[0] // LANES
    proj = dot(around_ref[...], w_in_ref[:width]).astype(BF16)
    send_low, send_high = column_parts(send_ref[...])
    for block in range(edges // EDGE_BLOCK):
        for part in range(EDGE_BLOCK // LANES):
            j = block * (EDGE_BLOCK // LANES) + part
            span = slice(j * LANES, (j + 1) * LANES)
            hot_s, high_s = lane_select(send_low[:, j : j + 1], send_high[:, j : j + 1])
            for t in range(extra):
                hot[span, t * LANES : (t + 1) * LANES] = pick(hot_s, high_s, tiles + t)
            hot_r, high_r = row_select(recv_ref[j : j + 1])
            for t in range(tiles):
                inc[t * LANES : (t + 1) * LANES, span] = pick(hot_r, high_r, t)
        span = slice(block * EDGE_BLOCK, (block + 1) * EDGE_BLOCK)
        hidden[span] = silu(pre_ref[span] + dot(hot[span], proj)).astype(BF16)
    for block in range(nodes // EDGE_BLOCK):
        span = slice(block * EDGE_BLOCK, (block + 1) * EDGE_BLOCK)
        agg = dot(dot(inc[span], hidden[...]).astype(BF16), w_out_ref[...])
        mid_ref[span] = (fs_ref[span].astype(F32) + rms_scale(agg, gain_ref[...])).astype(BF16)
    total = jnp.zeros(sums.shape, F32)
    for j in range(tiles):
        hot_p, high_p = row_select(par_ref[j : j + 1])
        upper = jnp.concatenate([pick(hot_p, high_p, t) for t in range(sums.shape[0] // LANES)], axis=0)
        total = total + dot(upper, mid_ref[j * LANES : (j + 1) * LANES])
    sums[...] = total
    half = keep_ref.shape[0]
    core = lax.rem(lax.axis_index("narrow"), 2)
    keep_ref[...] = sums[pl.ds(pl.multiple_of(core * half, half), half)]
    give_ref[...] = sums[pl.ds(pl.multiple_of((1 - core) * half, half), half)].astype(BF16)


def add_kernel(a_ref, b_ref, out_ref):
    out_ref[...] = (a_ref[...].astype(F32) + b_ref[...].astype(F32)).astype(BF16)


def level_two_kernel(a_ref, b_ref, state_ref, w_up_ref, gain_ref, out_ref):
    rows = out_ref.shape[0]
    core = lax.rem(lax.axis_index("narrow"), 2)
    total = a_ref[...].astype(F32) + b_ref[...].astype(F32)
    level = dot(total.astype(BF16), w_up_ref[...])
    state = state_ref[pl.ds(pl.multiple_of(core * rows, rows), rows)].astype(F32)
    out_ref[...] = (state + rms_scale(level, gain_ref[...])).astype(BF16)


def coarse_parent(parent_ref, rows, level_three):
    start = (lax.axis_index("wide") - 1) * rows
    local = (parent_ref[...] - start) & (level_three - 1)
    sub = lax.broadcasted_iota(jnp.int32, (3 * rows, LANES), 0)
    return jnp.concatenate(
        [jnp.where(local[j : j + 1] == sub, 1.0, 0.0) for j in range(parent_ref.shape[0])], axis=1
    )


def window_kernel(level_three, mine_ref, other_ref, parent_ref, own_ref, piece_ref, mid_ref):
    half = mine_ref.shape[0]
    rows = piece_ref.shape[0]
    narrow = lax.axis_index("narrow")
    core = lax.rem(narrow, 2)
    chip = narrow // 2
    mid_ref[pl.ds(pl.multiple_of(core * half, half), half)] = mine_ref[...]
    mid_ref[pl.ds(pl.multiple_of((1 - core) * half, half), half)] = other_ref[...]
    upper = coarse_parent(parent_ref, rows, level_three).astype(BF16)
    own_ref[...] = dot(upper, mid_ref[...])
    block = jnp.where(chip == 0, 1 + core, jnp.where(chip == 1, core, jnp.where(chip == 2, 2, 0)))
    piece_ref[...] = own_ref[pl.ds(pl.multiple_of(block * rows, rows), rows)].astype(BF16)


def down_kernel(
    level_three, own_ref, pieces_ref, l3_rows_ref, gain_ref,
    w1_ref, w2_ref, w_down_ref, w_fine_ref, parent_ref, mid_ref, par_ref, fine_ref,
    fine_out_ref, down_ref,
):
    rows = pieces_ref.shape[1]
    own = own_ref[...]
    piece = [pieces_ref[k].astype(F32) for k in (0, 1, 2, 3, 4, 6)]
    total = jnp.concatenate(
        [
            own[:rows] + piece[0] + piece[4],
            own[rows : 2 * rows] + piece[1] + piece[2],
            own[2 * rows :] + piece[3] + piece[5],
        ],
        axis=0,
    )
    mid3 = (l3_rows_ref[...].astype(F32) + rms_scale(total, gain_ref[...])).astype(BF16)
    hidden = silu(dot(mid3, w1_ref[...])).astype(BF16)
    new = (mid3.astype(F32) + dot(hidden, w2_ref[...])).astype(BF16)
    lower = coarse_parent(parent_ref, rows, level_three).T.astype(BF16)
    picked = dot(lower, new).astype(BF16)
    down = (mid_ref[...].astype(F32) + dot(picked, w_down_ref[...])).astype(BF16)
    down_ref[...] = down
    fine = dot(down, w_fine_ref[...]).astype(BF16)
    par_low, par_high = column_parts(par_ref[...])
    for j in range(par_ref.shape[0]):
        hot, high = lane_select(par_low[:, j : j + 1], par_high[:, j : j + 1])
        lower = jnp.concatenate([pick(hot, high, t) for t in range(fine.shape[0] // LANES)], axis=1)
        span = slice(j * LANES, (j + 1) * LANES)
        fine_out_ref[span] = (fine_ref[span].astype(F32) + dot(lower, fine)).astype(BF16)


def passed_along(value, steps):
    count = lax.axis_size("wide")
    return lax.ppermute(value, "wide", [(k, (k + steps) % count) for k in range(count)])


def swapped(value, partner):
    count = lax.axis_size("narrow")
    return lax.ppermute(value, "narrow", [(k, partner(k)) for k in range(count)])


def served(value):
    wide, narrow = lax.axis_size("wide"), lax.axis_size("narrow")
    steps = (1, -1, 2, -2)
    pairs = [
        (w * narrow + n, (w + steps[n // 2]) % wide * narrow + n)
        for w in range(wide)
        for n in range(narrow)
    ]
    return lax.ppermute(value, ("wide", "narrow"), pairs)


def call(kernel, out, scratch=(), vmem=48, hbm=(), nargs=0, flops=0, moved=0):
    specs = [
        pl.BlockSpec(memory_space=pltpu.HBM if k in hbm else pltpu.VMEM) for k in range(nargs)
    ]
    outs = [jax.ShapeDtypeStruct(shape, dtype) for shape, dtype in out]
    return pl.pallas_call(
        kernel,
        out_shape=outs,
        in_specs=specs,
        out_specs=[pl.BlockSpec(memory_space=pltpu.VMEM) for _ in outs],
        scratch_shapes=list(scratch),
        compiler_params=pltpu.CompilerParams(vmem_limit_bytes=vmem * 2**20),
        cost_estimate=pl.CostEstimate(flops=flops, bytes_accessed=moved, transcendentals=0),
    )


def body(
    fine_state, l2_state, l3_state, boundary, senders, receivers, up_parent, l2_parent, msg_in,
    msg_out, fine_gain, up_weight, l2_gain, l3_gain, l3_w1, l3_w2, down_weight, fine_down,
):
    nodes, width = fine_state.shape
    edges = senders.shape[0]
    level_two = l2_state.shape[0]
    level_three = l3_state.shape[0]
    rows = level_three // lax.axis_size("wide")
    n_narrow = lax.axis_size("narrow")
    send = senders.reshape(-1, LANES)
    recv = receivers.reshape(-1, LANES)
    par = up_parent.reshape(-1, LANES)
    parent = l2_parent.reshape(-1, LANES)
    fine_gain, l2_gain, l3_gain = (g.reshape(1, width) for g in (fine_gain, l2_gain, l3_gain))

    hot = (boundary[:, None] == jnp.arange(nodes, dtype=jnp.int32)[None, :]).astype(BF16)
    exported = dot(hot, fine_state).astype(BF16)
    behind, ahead = passed_along(exported, 1), passed_along(exported, -1)
    scratch = [
        pltpu.VMEM((nodes, width), BF16),
        pltpu.VMEM(send.shape, jnp.int32),
        pltpu.VMEM((width, width), BF16),
        pltpu.VMEM((nodes, width), BF16),
        pltpu.VMEM((edges, nodes), BF16),
        pltpu.SemaphoreType.DMA((6,)),
    ]
    (pre_recv,) = call(
        receiver_kernel, [((edges, width), F32)], scratch, hbm=(0, 1, 2), nargs=3,
        flops=2_000_000_000, moved=2_000_000,
    )(fine_state, recv, msg_in)
    behind, ahead, pre_recv = lax.optimization_barrier((behind, ahead, pre_recv))
    window = jnp.concatenate([behind, exported, ahead], axis=0)
    window = jnp.broadcast_to(window[None], (n_narrow,) + window.shape)
    window = lax.all_to_all(window, "narrow", 0, 0, tiled=True)
    bnd = boundary.shape[0]
    around = window.reshape(n_narrow, 3, bnd, width).transpose(1, 0, 2, 3).reshape(-1, width)

    pre, l3_rows = call(
        sender_kernel, [((edges, width), F32), ((3 * rows, width), BF16)], scratch,
        hbm=(1, 2, 3, 4), nargs=5, flops=2_000_000_000, moved=2_000_000,
    )(pre_recv, fine_state, send, msg_in, l3_state)

    half = level_two // 2
    fine_mid, keep, give = call(
        fine_kernel,
        [((nodes, width), BF16), ((half, width), F32), ((half, width), BF16)],
        [
            pltpu.VMEM((edges, width), BF16),
            pltpu.VMEM((edges, around.shape[0]), BF16),
            pltpu.VMEM((nodes, edges), BF16),
            pltpu.VMEM((level_two, width), F32),
        ],
        nargs=9, flops=3_000_000_000, moved=4_000_000,
    )(pre, around, fine_state, send, recv, par, msg_in, msg_out, fine_gain)

    half_out = [((half, width), BF16)]
    (chip_sum,) = call(add_kernel, half_out, nargs=2)(keep, swapped(give, lambda k: k ^ 1))
    (pair_sum,) = call(add_kernel, half_out, nargs=2)(chip_sum, swapped(chip_sum, lambda k: k ^ 2))
    (half_mid,) = call(level_two_kernel, half_out, nargs=5)(
        pair_sum, swapped(pair_sum, lambda k: (n_narrow // 2 - 1 - k // 2) * 2 + k % 2),
        l2_state, up_weight, l2_gain,
    )
    own, piece, l2_mid = call(
        functools.partial(window_kernel, level_three),
        [((3 * rows, width), F32), ((rows, width), BF16), ((level_two, width), BF16)],
        nargs=3,
    )(half_mid, swapped(half_mid, lambda k: k ^ 1), parent)
    piece = served(piece)
    pieces = jnp.broadcast_to(piece[None], (n_narrow,) + piece.shape)
    pieces = lax.all_to_all(pieces, "narrow", 0, 0, tiled=True)

    fine_out, l2_down = call(
        functools.partial(down_kernel, level_three),
        [((nodes, width), BF16), ((level_two, width), BF16)],
        nargs=12,
    )(
        own, pieces, l3_rows, l3_gain, l3_w1, l3_w2, down_weight, fine_down,
        parent, l2_mid, par, fine_mid,
    )
    return (fine_out, l2_down)


def solution(mesh):
    both = P(("wide", "narrow"))
    return jax.shard_map(
        body,
        mesh=mesh,
        in_specs=(
            P(("wide", "narrow"), None),
            P("wide", None),
            P(),
            both,
            both,
            both,
            both,
            P("wide"),
        )
        + (P(),) * 10,
        out_specs=(P(("wide", "narrow"), None), P("wide", None)),
        check_vma=False,
    )
```

time: 177 us -> 84.8 us (0.48)
  the two profiles are of different devices: /device:TPU:102 before, /device:TPU:1 now
where the time goes in v1:
time: 84.8 us; the launch traced here: 84.2 us
  starting transfers between devices  37 us (44%)
  waiting for transfers between devices  16.5 us (19%)
  Pallas kernels  11.7 us (14%)
  blocking collectives  10.4 us (12%)
  local copies, waits for them, and re-layouts  6.43 us (8%)
  matrix products  1.27 us (1%)
  between operations  0.92 us (1%)
    ppermute x2, starting transfers between devices, passed_along(): lax.ppermute(value, 'wide', [(k, (k + steps) % count) for k in range(coun...  16.1 us
    ppermute x4, starting transfers between devices, swapped(): lax.ppermute(value, 'narrow', [(k, partner(k)) for k in range(count)])  12.4 us
    all_to_all x1, blocking collectives, body(): pieces = lax.all_to_all(pieces, 'narrow', 0, 0, tiled=True)  10.4 us
    ppermute x4, waiting for transfers between devices, swapped(): lax.ppermute(value, 'narrow', [(k, partner(k)) for k in range(count)])  7.99 us
    all_to_all x1, starting transfers between devices, body(): window = lax.all_to_all(window, 'narrow', 0, 0, tiled=True)  6.57 us
    ppermute x1, waiting for transfers between devices, served(): return lax.ppermute(value, ('wide', 'narrow'), pairs)  6.05 us
    unnamed x42, local copies, waits for them, and re-layouts  5.7 us
    pallas_call x1, Pallas kernels, body(): call(fine_kernel, [((nodes, width), BF16), ((half, width), F32), ((half,...  4.19 us
  transfers between devices with their start and end apart: 8, of which 7 were waited for; matrix products, arithmetic and copies ran while one was open for 0% of the time, Pallas kernels for 6%

profile of v1, /device:TPU:1, one launch (start us, length us, event | category | flops | bytes accessed | tf_op | source)
XLA Modules:
  0.0 84.2 jit_solution(13464518068334871545)
XLA Ops:
  0.6 1.3 %convolution_convert_fusion = bf16[16,256]{1,0:T(8,128)(2,1)S(1)} fusion(bf16[1024,256]{1,0:T(8,128)(2,1)} %fs_ref.1, s32[16]{0:T(128)} %param.21), kind=kOutput, calls=%fused_computation | convolution fusion | flops 8409088 | bytes 532544 | tf_op jit(solution)/shard_map/dot_general | solution.py:17
  1.9 14.2 %collective-permute-start.1 = (bf16[16,256]{1,0:T(8,128)(2,1)S(1)}, bf16[16,256]{1,0:T(8,128)(2,1)S(1)}, u32[]{:S(2)}, u32[]{:S(2)}) collective-permute-start(bf16[16,256]{1,0:T(8,128)(2,1)S(1)} %convolution_convert_fusion), channel_id=1, source_target_pairs={{0,504},{8,0},{16,8},{24,16},{32,24},{40,32},{48,40},{56,48},{64,5... | collective-permute-start | bytes 24584 | tf_op jit(solution)/shard_map/ppermute | solution.py:213
  16.1 1.9 %collective-permute-start = (bf16[16,256]{1,0:T(8,128)(2,1)S(1)}, bf16[16,256]{1,0:T(8,128)(2,1)S(1)}, u32[]{:S(2)}, u32[]{:S(2)}) collective-permute-start(bf16[16,256]{1,0:T(8,128)(2,1)S(1)} %convolution_convert_fusion), channel_id=1, source_target_pairs={{0,8},{8,16},{16,24},{24,32},{32,40},{40,48},{48,56},{56,64},{64,7... | collective-permute-start | bytes 24584 | tf_op jit(solution)/shard_map/ppermute | solution.py:213
  18.0 0.0 copy-start
  18.0 1.0 %copy-done = bf16[1024,256]{1,0:T(8,128)(2,1)S(1)} copy-done((bf16[1024,256]{1,0:T(8,128)(2,1)S(1)}, bf16[1024,256]{1,0:T(8,128)(2,1)}, u32[]{:S(2)}) %copy-start) | copy-done | bytes 524312
  19.0 0.9 %copy-done.12 = bf16[512,256]{1,0:T(8,128)(2,1)S(1)} copy-done((bf16[512,256]{1,0:T(8,128)(2,1)S(1)}, bf16[512,256]{1,0:T(8,128)(2,1)}, u32[]{:S(2)}) %copy-start.12) | copy-done | bytes 262168
  20.0 0.7 copy-done.15
  20.7 2.1 %shard_map.185.before_ref = f32[2048,256]{1,0:T(8,128)S(1)} custom-call(bf16[1024,256]{1,0:T(8,128)(2,1)S(1)} %copy-done, s32[16,128]{1,0:T(8,128)S(1)} %bitcast.19, bf16[512,256]{1,0:T(8,128)(2,1)S(1)} %copy-done.12), custom_call_target="tpu_custom_call" | custom-call | flops 2000000000 | bytes 2000000 | tf_op jit(solution)/shard_map/pallas_call | solution.py:275
  22.8 0.0 collective-permute-done.1
  22.8 1.0 %collective-permute-done = bf16[16,256]{1,0:T(8,128)(2,1)S(1)} collective-permute-done((bf16[16,256]{1,0:T(8,128)(2,1)S(1)}, bf16[16,256]{1,0:T(8,128)(2,1)S(1)}, u32[]{:S(2)}, u32[]{:S(2)}) %collective-permute-start) | collective-permute-done | bytes 8224 | tf_op jit(solution)/shard_map/ppermute | solution.py:213
  23.8 0.7 broadcast_in_dim.4
  24.5 6.6 %all-to-all-start = ((bf16[8,48,256]{2,1,0:T(8,128)(2,1)}), bf16[8,48,256]{2,1,0:T(8,128)(2,1)S(1)}, u32[]{:S(2)}, u32[]{:S(2)}) async-start(bf16[8,48,256]{2,1,0:T(8,128)(2,1)} %broadcast_in_dim.4), calls=%async_computation | async-start | bytes 393216 | tf_op jit(solution)/shard_map/all_to_all | solution.py:282
  31.0 0.0 copy-done.1
  31.0 0.0 copy-done.13
  31.0 0.0 copy-done.17
  31.1 0.0 copy-start.8
  31.1 0.0 copy-start.14
  31.1 0.0 copy-start.16
  31.1 0.0 copy-start.18
  31.1 3.0 %shard_map.186 = (f32[2048,256]{1,0:T(8,128)S(1)}, bf16[192,256]{1,0:T(8,128)(2,1)S(1)}) custom-call(f32[2048,256]{1,0:T(8,128)S(1)} %shard_map.185.before_ref, bf16[1024,256]{1,0:T(8,128)(2,1)S(1)} %copy-done.1, s32[16,128]{1,0:T(8,128)S(1)} %bitcast.21, bf16[512,256]{1,0:T(8,128)(2,1)S(1)} %copy-done.13, bf16[4096,256]{1,0:T(8,128)(2,1)} %l3_hbm.1), custom_call_target="tpu_custom_call" | custom-call | flops 2000000000 | bytes 2000000 | tf_op jit(solution)/shard_map/pallas_call | solution.py:286
  34.1 0.0 copy-start.19
  34.1 1.4 %copy-done.19 = f32[2048,256]{1,0:T(8,128)} copy-done((f32[2048,256]{1,0:T(8,128)}, f32[2048,256]{1,0:T(8,128)S(1)}, u32[]{:S(2)}) %copy-start.19) | copy-done | bytes 2097176
  35.4 1.5 %all-to-all-done = bf16[8,48,256]{2,1,0:T(8,128)(2,1)S(1)} async-done(((bf16[8,48,256]{2,1,0:T(8,128)(2,1)}), bf16[8,48,256]{2,1,0:T(8,128)(2,1)S(1)}, u32[]{:S(2)}, u32[]{:S(2)}) %all-to-all-start) | async-done | bytes 196640 | tf_op jit(solution)/shard_map/all_to_all | solution.py:282
  36.9 0.0 copy-done.8
  37.0 1.6 %copy-done.20 = f32[2048,256]{1,0:T(8,128)S(1)} copy-done((f32[2048,256]{1,0:T(8,128)S(1)}, f32[2048,256]{1,0:T(8,128)}, u32[]{:S(2)}) %copy-start.20) | copy-done | bytes 2097176
  38.6 0.0 copy-start.4
  38.6 0.0 copy-start.5
  38.6 0.0 copy-start.6
  38.6 0.0 copy-start.7
  38.6 0.0 copy-start.11
  38.6 4.2 %shard_map.187 = (bf16[1024,256]{1,0:T(8,128)(2,1)S(1)}, f32[128,256]{1,0:T(8,128)S(1)}, bf16[128,256]{1,0:T(8,128)(2,1)S(1)}) custom-call(f32[2048,256]{1,0:T(8,128)S(1)} %copy-done.20, bf16[384,256]{1,0:T(8,128)(2,1)S(1)} %bitcast.12, bf16[1024,256]{1,0:T(8,128)(2,1)S(1)} %copy-done.1, s32[16,128]{1,0:T(8,128)S(1)} %bitcast.22, s32[16,128]{1,0:T(8,128)S(1)} %bitcast.20, ...), custom_call_target="tpu_custom_call" | custom-call | flops 3000000000 | bytes 4000000 | tf_op jit(solution)/shard_map/pallas_call | solution.py:292
  42.8 2.9 %collective-permute-start.2 = (bf16[128,256]{1,0:T(8,128)(2,1)S(1)}, bf16[128,256]{1,0:T(8,128)(2,1)S(1)}, u32[]{:S(2)}, u32[]{:S(2)}) collective-permute-start(bf16[128,256]{1,0:T(8,128)(2,1)S(1)} %get-tuple-element.18), channel_id=1, source_target_pairs={{0,1},{1,0},{2,3},{3,2},{4,5},{5,4},{6,7},{7,6},{8,9},{9,8},{10,11... | collective-permute-start | bytes 196616 | tf_op jit(solution)/shard_map/ppermute | solution.py:218
  45.7 0.9 %collective-permute-done.2.b_ref = bf16[128,256]{1,0:T(8,128)(2,1)S(1)} collective-permute-done((bf16[128,256]{1,0:T(8,128)(2,1)S(1)}, bf16[128,256]{1,0:T(8,128)(2,1)S(1)}, u32[]{:S(2)}, u32[]{:S(2)}) %collective-permute-start.2) | collective-permute-done | bytes 65568 | tf_op jit(solution)/shard_map/ppermute | solution.py:218
  46.6 2.2 %collective-permute-start.3 = (bf16[128,256]{1,0:T(8,128)(2,1)S(1)}, bf16[128,256]{1,0:T(8,128)(2,1)S(1)}, u32[]{:S(2)}, u32[]{:S(2)}) collective-permute-start(bf16[128,256]{1,0:T(8,128)(2,1)S(1)} %shard_map.188.a_ref), channel_id=1, source_target_pairs={{0,2},{1,3},{2,0},{3,1},{4,6},{5,7},{6,4},{7,5},{8,10},{9,11},{10,... | collective-permute-start | bytes 196616 | tf_op jit(solution)/shard_map/ppermute | solution.py:218
  48.8 2.8 %collective-permute-done.3.b_ref = bf16[128,256]{1,0:T(8,128)(2,1)S(1)} collective-permute-done((bf16[128,256]{1,0:T(8,128)(2,1)S(1)}, bf16[128,256]{1,0:T(8,128)(2,1)S(1)}, u32[]{:S(2)}, u32[]{:S(2)}) %collective-permute-start.3) | collective-permute-done | bytes 65568 | tf_op jit(solution)/shard_map/ppermute | solution.py:218
  51.6 2.8 %collective-permute-start.4 = (bf16[128,256]{1,0:T(8,128)(2,1)S(1)}, bf16[128,256]{1,0:T(8,128)(2,1)S(1)}, u32[]{:S(2)}, u32[]{:S(2)}) collective-permute-start(bf16[128,256]{1,0:T(8,128)(2,1)S(1)} %shard_map.189.a_ref), channel_id=1, source_target_pairs={{0,6},{1,7},{2,4},{3,5},{4,2},{5,3},{6,0},{7,1},{8,14},{9,15},{10,... | collective-permute-start | bytes 196616 | tf_op jit(solution)/shard_map/ppermute | solution.py:218
  54.4 3.4 %collective-permute-done.4.b_ref = bf16[128,256]{1,0:T(8,128)(2,1)S(1)} collective-permute-done((bf16[128,256]{1,0:T(8,128)(2,1)S(1)}, bf16[128,256]{1,0:T(8,128)(2,1)S(1)}, u32[]{:S(2)}, u32[]{:S(2)}) %collective-permute-start.4) | collective-permute-done | bytes 65568 | tf_op jit(solution)/shard_map/ppermute | solution.py:218
  57.9 0.0 copy-done.3
  57.9 0.3 shard_map.190.mine_ref
  58.1 4.6 %collective-permute-start.5 = (bf16[128,256]{1,0:T(8,128)(2,1)S(1)}, bf16[128,256]{1,0:T(8,128)(2,1)S(1)}, u32[]{:S(2)}, u32[]{:S(2)}) collective-permute-start(bf16[128,256]{1,0:T(8,128)(2,1)S(1)} %shard_map.190.mine_ref), channel_id=1, source_target_pairs={{0,1},{1,0},{2,3},{3,2},{4,5},{5,4},{6,7},{7,6},{8,9},{9,8},{10,11... | collective-permute-start | bytes 196616 | tf_op jit(solution)/shard_map/ppermute | solution.py:218
  62.7 0.9 %collective-permute-done.5.other_ref = bf16[128,256]{1,0:T(8,128)(2,1)S(1)} collective-permute-done((bf16[128,256]{1,0:T(8,128)(2,1)S(1)}, bf16[128,256]{1,0:T(8,128)(2,1)S(1)}, u32[]{:S(2)}, u32[]{:S(2)}) %collective-permute-start.5) | collective-permute-done | bytes 65568 | tf_op jit(solution)/shard_map/ppermute | solution.py:218
  63.6 0.2 shard_map.191
  63.8 1.9 %collective-permute-start.6 = (bf16[64,256]{1,0:T(8,128)(2,1)S(1)}, bf16[64,256]{1,0:T(8,128)(2,1)S(1)}, u32[]{:S(2)}, u32[]{:S(2)}) collective-permute-start(bf16[64,256]{1,0:T(8,128)(2,1)S(1)} %get-tuple-element.20), channel_id=1, source_target_pairs={{0,8},{1,9},{2,506},{3,507},{4,20},{5,21},{6,502},{7,503},{8,16},{... | collective-permute-start | bytes 98312 | tf_op jit(solution)/shard_map/ppermute | solution.py:229
  65.7 6.1 %collective-permute-done.6 = bf16[64,256]{1,0:T(8,128)(2,1)S(1)} collective-permute-done((bf16[64,256]{1,0:T(8,128)(2,1)S(1)}, bf16[64,256]{1,0:T(8,128)(2,1)S(1)}, u32[]{:S(2)}, u32[]{:S(2)}) %collective-permute-start.6) | collective-permute-done | bytes 32800 | tf_op jit(solution)/shard_map/ppermute | solution.py:229
  71.8 10.4 %all_to_all.10.pieces_ref = bf16[8,64,256]{2,1,0:T(8,128)(2,1)S(1)} all-to-all(bf16[8,64,256]{2,1,0:T(8,128)(2,1)S(1)} %broadcast_in_dim.5), channel_id=1, replica_groups=mesh['wide'=64,'narrow'=8] {'narrow'}, dimensions={0} | all-to-all | bytes 524288 | tf_op jit(solution)/shard_map/all_to_all | solution.py:318
  82.2 0.0 copy-done.4
  82.2 0.0 copy-done.6
  82.3 2.0 %shard_map.192 = (bf16[1024,256]{1,0:T(8,128)(2,1)}, bf16[256,256]{1,0:T(8,128)(2,1)}) custom-call(f32[192,256]{1,0:T(8,128)S(1)} %get-tuple-element.19.own_ref, bf16[8,64,256]{2,1,0:T(8,128)(2,1)S(1)} %all_to_all.10.pieces_ref, bf16[192,256]{1,0:T(8,128)(2,1)S(1)} %get-tuple-element.21.l3_rows_ref, f32[1,256]{1,0:T(1,128)S(1)} %bitcast.18, ...), custom_call_target="tpu_custom_call" | custom-call | tf_op jit(solution)/shard_map/pallas_call | solution.py:320
  (24 shorter events, 0.1 us)
Async XLA Ops:
  1.9 20.9 %collective-permute-start.1 = (bf16[16,256]{1,0:T(8,128)(2,1)S(1)}, bf16[16,256]{1,0:T(8,128)(2,1)S(1)}, u32[]{:S(2)}, u32[]{:S(2)}) collective-permute-start(bf16[16,256]{1,0:T(8,128)(2,1)S(1)} %convolution_convert_fusion), channel_id=1, source_target_pairs={{0,504},{8,0},{16,8},{24,16},{32,24},{40,32},{48,40},{56,48},{64,5... | collective-permute-start | bytes 24584 | tf_op jit(solution)/shard_map/ppermute | solution.py:213
  16.1 7.7 %collective-permute-start = (bf16[16,256]{1,0:T(8,128)(2,1)S(1)}, bf16[16,256]{1,0:T(8,128)(2,1)S(1)}, u32[]{:S(2)}, u32[]{:S(2)}) collective-permute-start(bf16[16,256]{1,0:T(8,128)(2,1)S(1)} %convolution_convert_fusion), channel_id=1, source_target_pairs={{0,8},{8,16},{16,24},{24,32},{32,40},{40,48},{48,56},{56,64},{64,7... | collective-permute-start | bytes 24584 | tf_op jit(solution)/shard_map/ppermute | solution.py:213
  18.0 1.0 %copy-start = (bf16[1024,256]{1,0:T(8,128)(2,1)S(1)}, bf16[1024,256]{1,0:T(8,128)(2,1)}, u32[]{:S(2)}) copy-start(bf16[1024,256]{1,0:T(8,128)(2,1)} %fs_ref.1) | copy-start | bytes 1572868
  19.0 0.9 %copy-start.12 = (bf16[512,256]{1,0:T(8,128)(2,1)S(1)}, bf16[512,256]{1,0:T(8,128)(2,1)}, u32[]{:S(2)}) copy-start(bf16[512,256]{1,0:T(8,128)(2,1)} %w_in_ref.1) | copy-start | bytes 786436
  20.0 0.7 copy-start.15
  20.7 10.4 %copy-start.1 = (bf16[1024,256]{1,0:T(8,128)(2,1)S(1)}, bf16[1024,256]{1,0:T(8,128)(2,1)}, u32[]{:S(2)}) copy-start(bf16[1024,256]{1,0:T(8,128)(2,1)} %fs_ref.1) | copy-start | bytes 1572868
  20.7 10.4 %copy-start.13 = (bf16[512,256]{1,0:T(8,128)(2,1)S(1)}, bf16[512,256]{1,0:T(8,128)(2,1)}, u32[]{:S(2)}) copy-start(bf16[512,256]{1,0:T(8,128)(2,1)} %w_in_ref.1) | copy-start | bytes 786436
  20.7 10.4 %copy-start.17 = (s32[2048]{0:T(1024)S(1)}, s32[2048]{0:T(1024)}, u32[]{:S(2)}) copy-start(s32[2048]{0:T(1024)} %param.22) | copy-start | bytes 24580
  24.5 12.5 %all-to-all-start = ((bf16[8,48,256]{2,1,0:T(8,128)(2,1)}), bf16[8,48,256]{2,1,0:T(8,128)(2,1)S(1)}, u32[]{:S(2)}, u32[]{:S(2)}) async-start(bf16[8,48,256]{2,1,0:T(8,128)(2,1)} %broadcast_in_dim.4), calls=%async_computation | async-start | bytes 393216 | tf_op jit(solution)/shard_map/all_to_all | solution.py:282
  31.1 5.9 %copy-start.8 = (s32[1024]{0:T(1024)S(1)}, s32[1024]{0:T(1024)}, u32[]{:S(2)}) copy-start(s32[1024]{0:T(1024)} %param.24) | copy-start | bytes 12292
  31.1 5.9 %copy-start.14 = (bf16[256,256]{1,0:T(8,128)(2,1)S(1)}, bf16[256,256]{1,0:T(8,128)(2,1)}, u32[]{:S(2)}) copy-start(bf16[256,256]{1,0:T(8,128)(2,1)} %w_out_ref.1) | copy-start | bytes 393220
  31.1 5.9 %copy-start.16 = (s32[2048]{0:T(1024)S(1)}, s32[2048]{0:T(1024)}, u32[]{:S(2)}) copy-start(s32[2048]{0:T(1024)} %param.23) | copy-start | bytes 24580
  31.1 5.9 %copy-start.18 = (f32[256]{0:T(256)S(1)}, f32[256]{0:T(256)}, u32[]{:S(2)}) copy-start(f32[256]{0:T(256)} %param.28) | copy-start | bytes 3076
  34.1 1.4 %copy-start.19 = (f32[2048,256]{1,0:T(8,128)}, f32[2048,256]{1,0:T(8,128)S(1)}, u32[]{:S(2)}) copy-start(f32[2048,256]{1,0:T(8,128)S(1)} %get-tuple-element.14.pre_ref) | copy-start | bytes 6291460
  37.0 1.6 %copy-start.20 = (f32[2048,256]{1,0:T(8,128)S(1)}, f32[2048,256]{1,0:T(8,128)}, u32[]{:S(2)}) copy-start(f32[2048,256]{1,0:T(8,128)} %copy-done.19) | copy-start | bytes 6291460
  38.6 19.3 %copy-start.2 = (bf16[256,256]{1,0:T(8,128)(2,1)S(1)}, bf16[256,256]{1,0:T(8,128)(2,1)}, u32[]{:S(2)}) copy-start(bf16[256,256]{1,0:T(8,128)(2,1)} %state_ref.1) | copy-start | bytes 393220
  38.6 19.3 %copy-start.3 = (bf16[256,256]{1,0:T(8,128)(2,1)S(1)}, bf16[256,256]{1,0:T(8,128)(2,1)}, u32[]{:S(2)}) copy-start(bf16[256,256]{1,0:T(8,128)(2,1)} %w_up_ref.1) | copy-start | bytes 393220
  38.6 19.3 %copy-start.10 = (f32[256]{0:T(256)S(1)}, f32[256]{0:T(256)}, u32[]{:S(2)}) copy-start(f32[256]{0:T(256)} %param.30) | copy-start | bytes 3076
  38.6 25.0 %copy-start.9 = (s32[256]{0:T(256)S(1)}, s32[256]{0:T(256)}, u32[]{:S(2)}) copy-start(s32[256]{0:T(256)} %param.25) | copy-start | bytes 3076
  38.6 43.6 %copy-start.4 = (bf16[256,256]{1,0:T(8,128)(2,1)S(1)}, bf16[256,256]{1,0:T(8,128)(2,1)}, u32[]{:S(2)}) copy-start(bf16[256,256]{1,0:T(8,128)(2,1)} %w1_ref.1) | copy-start | bytes 393220
  38.6 43.6 %copy-start.5 = (bf16[256,256]{1,0:T(8,128)(2,1)S(1)}, bf16[256,256]{1,0:T(8,128)(2,1)}, u32[]{:S(2)}) copy-start(bf16[256,256]{1,0:T(8,128)(2,1)} %w2_ref.1) | copy-start | bytes 393220
  38.6 43.6 %copy-start.6 = (bf16[256,256]{1,0:T(8,128)(2,1)S(1)}, bf16[256,256]{1,0:T(8,128)(2,1)}, u32[]{:S(2)}) copy-start(bf16[256,256]{1,0:T(8,128)(2,1)} %w_down_ref.1) | copy-start | bytes 393220
  38.6 43.6 %copy-start.7 = (bf16[256,256]{1,0:T(8,128)(2,1)S(1)}, bf16[256,256]{1,0:T(8,128)(2,1)}, u32[]{:S(2)}) copy-start(bf16[256,256]{1,0:T(8,128)(2,1)} %w_fine_ref.1) | copy-start | bytes 393220
  38.6 43.6 %copy-start.11 = (f32[256]{0:T(256)S(1)}, f32[256]{0:T(256)}, u32[]{:S(2)}) copy-start(f32[256]{0:T(256)} %param.31) | copy-start | bytes 3076
  42.8 3.7 %collective-permute-start.2 = (bf16[128,256]{1,0:T(8,128)(2,1)S(1)}, bf16[128,256]{1,0:T(8,128)(2,1)S(1)}, u32[]{:S(2)}, u32[]{:S(2)}) collective-permute-start(bf16[128,256]{1,0:T(8,128)(2,1)S(1)} %get-tuple-element.18), channel_id=1, source_target_pairs={{0,1},{1,0},{2,3},{3,2},{4,5},{5,4},{6,7},{7,6},{8,9},{9,8},{10,11... | collective-permute-start | bytes 196616 | tf_op jit(solution)/shard_map/ppermute | solution.py:218
  46.6 5.0 %collective-permute-start.3 = (bf16[128,256]{1,0:T(8,128)(2,1)S(1)}, bf16[128,256]{1,0:T(8,128)(2,1)S(1)}, u32[]{:S(2)}, u32[]{:S(2)}) collective-permute-start(bf16[128,256]{1,0:T(8,128)(2,1)S(1)} %shard_map.188.a_ref), channel_id=1, source_target_pairs={{0,2},{1,3},{2,0},{3,1},{4,6},{5,7},{6,4},{7,5},{8,10},{9,11},{10,... | collective-permute-start | bytes 196616 | tf_op jit(solution)/shard_map/ppermute | solution.py:218
  51.6 6.2 %collective-permute-start.4 = (bf16[128,256]{1,0:T(8,128)(2,1)S(1)}, bf16[128,256]{1,0:T(8,128)(2,1)S(1)}, u32[]{:S(2)}, u32[]{:S(2)}) collective-permute-start(bf16[128,256]{1,0:T(8,128)(2,1)S(1)} %shard_map.189.a_ref), channel_id=1, source_target_pairs={{0,6},{1,7},{2,4},{3,5},{4,2},{5,3},{6,0},{7,1},{8,14},{9,15},{10,... | collective-permute-start | bytes 196616 | tf_op jit(solution)/shard_map/ppermute | solution.py:218
  58.1 5.4 %collective-permute-start.5 = (bf16[128,256]{1,0:T(8,128)(2,1)S(1)}, bf16[128,256]{1,0:T(8,128)(2,1)S(1)}, u32[]{:S(2)}, u32[]{:S(2)}) collective-permute-start(bf16[128,256]{1,0:T(8,128)(2,1)S(1)} %shard_map.190.mine_ref), channel_id=1, source_target_pairs={{0,1},{1,0},{2,3},{3,2},{4,5},{5,4},{6,7},{7,6},{8,9},{9,8},{10,11... | collective-permute-start | bytes 196616 | tf_op jit(solution)/shard_map/ppermute | solution.py:218
  63.8 8.0 %collective-permute-start.6 = (bf16[64,256]{1,0:T(8,128)(2,1)S(1)}, bf16[64,256]{1,0:T(8,128)(2,1)S(1)}, u32[]{:S(2)}, u32[]{:S(2)}) collective-permute-start(bf16[64,256]{1,0:T(8,128)(2,1)S(1)} %get-tuple-element.20), channel_id=1, source_target_pairs={{0,8},{1,9},{2,506},{3,507},{4,20},{5,21},{6,502},{7,503},{8,16},{... | collective-permute-start | bytes 98312 | tf_op jit(solution)/shard_map/ppermute | solution.py:229

commit v2 on v1

--- a/solution.py
+++ b/solution.py
@@ -82,7 +82,8 @@
 
 
 def sender_kernel(
-    before_ref, fs_hbm, send_hbm, w_in_hbm, l3_hbm, pre_ref, l3_rows_ref, fs, send, w_in, proj, hot, sems
+    before_ref, fs_hbm, send_hbm, w_in_hbm, l3_hbm, recv_ref, pre_ref, l3_rows_ref, inc_ref,
+    fs, send, w_in, proj, hot, sems,
 ):
     width = fs.shape[1]
     wide = lax.axis_index("wide")
@@ -100,11 +101,15 @@
     fetch(pairs, sems)
     proj[...] = dot(fs[...], w_in[...]).astype(BF16)
     gathered(send, proj, hot, pre_ref, before_ref)
+    for j in range(recv_ref.shape[0]):
+        hot_r, high_r = row_select(recv_ref[j : j + 1])
+        for t in range(inc_ref.shape[0] // LANES):
+            inc_ref[t * LANES : (t + 1) * LANES, j * LANES : (j + 1) * LANES] = pick(hot_r, high_r, t)
 
 
 def fine_kernel(
-    pre_ref, around_ref, fs_ref, send_ref, recv_ref, par_ref, w_in_ref, w_out_ref, gain_ref,
-    mid_ref, keep_ref, give_ref, hidden, hot, inc, sums,
+    pre_ref, around_ref, fs_ref, send_ref, inc_ref, par_ref, w_in_ref, w_out_ref, gain_ref,
+    mid_ref, part_ref, hidden, hot,
 ):
     nodes, width = fs_ref.shape
     edges = pre_ref.shape[0]
@@ -119,38 +124,35 @@
             hot_s, high_s = lane_select(send_low[:, j : j + 1], send_high[:, j : j + 1])
             for t in range(extra):
                 hot[span, t * LANES : (t + 1) * LANES] = pick(hot_s, high_s, tiles + t)
-            hot_r, high_r = row_select(recv_ref[j : j + 1])
-            for t in range(tiles):
-                inc[t * LANES : (t + 1) * LANES, span] = pick(hot_r, high_r, t)
         span = slice(block * EDGE_BLOCK, (block + 1) * EDGE_BLOCK)
         hidden[span] = silu(pre_ref[span] + dot(hot[span], proj)).astype(BF16)
     for block in range(nodes // EDGE_BLOCK):
         span = slice(block * EDGE_BLOCK, (block + 1) * EDGE_BLOCK)
-        agg = dot(dot(inc[span], hidden[...]).astype(BF16), w_out_ref[...])
+        agg = dot(dot(inc_ref[span], hidden[...]).astype(BF16), w_out_ref[...])
         mid_ref[span] = (fs_ref[span].astype(F32) + rms_scale(agg, gain_ref[...])).astype(BF16)
-    total = jnp.zeros(sums.shape, F32)
+    total = jnp.zeros(part_ref.shape, F32)
     for j in range(tiles):
         hot_p, high_p = row_select(par_ref[j : j + 1])
-        upper = jnp.concatenate([pick(hot_p, high_p, t) for t in range(sums.shape[0] // LANES)], axis=0)
+        upper = jnp.concatenate(
+            [pick(hot_p, high_p, t) for t in range(part_ref.shape[0] // LANES)], axis=0
+        )
         total = total + dot(upper, mid_ref[j * LANES : (j + 1) * LANES])
-    sums[...] = total
-    half = keep_ref.shape[0]
-    core = lax.rem(lax.axis_index("narrow"), 2)
-    keep_ref[...] = sums[pl.ds(pl.multiple_of(core * half, half), half)]
-    give_ref[...] = sums[pl.ds(pl.multiple_of((1 - core) * half, half), half)].astype(BF16)
+    part_ref[...] = total.astype(BF16)
 
 
 def add_kernel(a_ref, b_ref, out_ref):
-    out_ref[...] = (a_ref[...].astype(F32) + b_ref[...].astype(F32)).astype(BF16)
-
-
-def level_two_kernel(a_ref, b_ref, state_ref, w_up_ref, gain_ref, out_ref):
-    rows = out_ref.shape[0]
-    core = lax.rem(lax.axis_index("narrow"), 2)
-    total = a_ref[...].astype(F32) + b_ref[...].astype(F32)
-    level = dot(total.astype(BF16), w_up_ref[...])
-    state = state_ref[pl.ds(pl.multiple_of(core * rows, rows), rows)].astype(F32)
-    out_ref[...] = (state + rms_scale(level, gain_ref[...])).astype(BF16)
+    total = (a_ref[...].astype(F32) + b_ref[...].astype(F32)).astype(BF16)
+    for k in range(out_ref.shape[0]):
+        out_ref[k] = total
+
+
+def copies_kernel(*refs):
+    out_ref = refs[-1]
+    for k in range(out_ref.shape[0]):
+        start = 0
+        for ref in refs[:-1]:
+            out_ref[k, start : start + ref.shape[0]] = ref[...]
+            start += ref.shape[0]
 
 
 def coarse_parent(parent_ref, rows, level_three):
@@ -162,18 +164,19 @@
     )
 
 
-def window_kernel(level_three, mine_ref, other_ref, parent_ref, own_ref, piece_ref, mid_ref):
-    half = mine_ref.shape[0]
-    rows = piece_ref.shape[0]
-    narrow = lax.axis_index("narrow")
-    core = lax.rem(narrow, 2)
-    chip = narrow // 2
-    mid_ref[pl.ds(pl.multiple_of(core * half, half), half)] = mine_ref[...]
-    mid_ref[pl.ds(pl.multiple_of((1 - core) * half, half), half)] = other_ref[...]
-    upper = coarse_parent(parent_ref, rows, level_three).astype(BF16)
-    own_ref[...] = dot(upper, mid_ref[...])
-    block = jnp.where(chip == 0, 1 + core, jnp.where(chip == 1, core, jnp.where(chip == 2, 2, 0)))
-    piece_ref[...] = own_ref[pl.ds(pl.multiple_of(block * rows, rows), rows)].astype(BF16)
+def window_kernel(
+    level_three, parts_ref, state_ref, w_up_ref, gain_ref, parent_ref, own_ref, piece_ref, mid_ref
+):
+    rows = own_ref.shape[0] // 3
+    total = parts_ref[0].astype(F32)
+    for k in range(1, parts_ref.shape[0]):
+        total = total + parts_ref[k].astype(F32)
+    level = dot(total.astype(BF16), w_up_ref[...])
+    mid = (state_ref[...].astype(F32) + rms_scale(level, gain_ref[...])).astype(BF16)
+    mid_ref[...] = mid
+    own_ref[...] = dot(coarse_parent(parent_ref, rows, level_three).astype(BF16), mid)
+    start = (1 - lax.rem(lax.axis_index("chip"), 2)) * rows
+    piece_ref[...] = own_ref[pl.ds(pl.multiple_of(start, rows), 2 * rows)].astype(BF16)
 
 
 def down_kernel(
@@ -181,14 +184,14 @@
     w1_ref, w2_ref, w_down_ref, w_fine_ref, parent_ref, mid_ref, par_ref, fine_ref,
     fine_out_ref, down_ref,
 ):
-    rows = pieces_ref.shape[1]
+    rows = own_ref.shape[0] // 3
     own = own_ref[...]
-    piece = [pieces_ref[k].astype(F32) for k in (0, 1, 2, 3, 4, 6)]
+    behind, ahead, behind2, ahead2 = (pieces_ref[k].astype(F32) for k in range(4))
     total = jnp.concatenate(
         [
-            own[:rows] + piece[0] + piece[4],
-            own[rows : 2 * rows] + piece[1] + piece[2],
-            own[2 * rows :] + piece[3] + piece[5],
+            own[:rows] + behind[:rows] + behind2[rows:],
+            own[rows : 2 * rows] + behind[rows:] + ahead[:rows],
+            own[2 * rows :] + ahead[rows:] + ahead2[:rows],
         ],
         axis=0,
     )
@@ -213,23 +216,21 @@
     return lax.ppermute(value, "wide", [(k, (k + steps) % count) for k in range(count)])
 
 
-def swapped(value, partner):
-    count = lax.axis_size("narrow")
-    return lax.ppermute(value, "narrow", [(k, partner(k)) for k in range(count)])
-
-
 def served(value):
-    wide, narrow = lax.axis_size("wide"), lax.axis_size("narrow")
+    wide, chips, cores = (lax.axis_size(name) for name in ("wide", "chip", "core"))
     steps = (1, -1, 2, -2)
-    pairs = [
-        (w * narrow + n, (w + steps[n // 2]) % wide * narrow + n)
-        for w in range(wide)
-        for n in range(narrow)
-    ]
-    return lax.ppermute(value, ("wide", "narrow"), pairs)
-
-
-def call(kernel, out, scratch=(), vmem=48, hbm=(), nargs=0, flops=0, moved=0):
+    pairs = []
+    for w in range(wide):
+        for chip in range(chips):
+            for core in range(cores):
+                here = chip * cores + core
+                pairs.append(
+                    (w * chips * cores + here, (w + steps[chip]) % wide * chips * cores + here)
+                )
+    return lax.ppermute(value, ("wide", "chip", "core"), pairs)
+
+
+def call(kernel, out, scratch=(), vmem=24, hbm=(), nargs=0, flops=0, moved=0):
     specs = [
         pl.BlockSpec(memory_space=pltpu.HBM if k in hbm else pltpu.VMEM) for k in range(nargs)
     ]
@@ -254,7 +255,7 @@
     level_two = l2_state.shape[0]
     level_three = l3_state.shape[0]
     rows = level_three // lax.axis_size("wide")
-    n_narrow = lax.axis_size("narrow")
+    chips, cores = lax.axis_size("chip"), lax.axis_size("core")
     send = senders.reshape(-1, LANES)
     recv = receivers.reshape(-1, LANES)
     par = up_parent.reshape(-1, LANES)
@@ -277,45 +278,36 @@
         flops=2_000_000_000, moved=2_000_000,
     )(fine_state, recv, msg_in)
     behind, ahead, pre_recv = lax.optimization_barrier((behind, ahead, pre_recv))
-    window = jnp.concatenate([behind, exported, ahead], axis=0)
-    window = jnp.broadcast_to(window[None], (n_narrow,) + window.shape)
-    window = lax.all_to_all(window, "narrow", 0, 0, tiled=True)
+    (window,) = call(
+        copies_kernel, [((chips * cores, 3 * boundary.shape[0], width), BF16)], nargs=3
+    )(behind, exported, ahead)
+    window = lax.all_to_all(window, ("chip", "core"), 0, 0, tiled=True)
     bnd = boundary.shape[0]
-    around = window.reshape(n_narrow, 3, bnd, width).transpose(1, 0, 2, 3).reshape(-1, width)
-
-    pre, l3_rows = call(
-        sender_kernel, [((edges, width), F32), ((3 * rows, width), BF16)], scratch,
-        hbm=(1, 2, 3, 4), nargs=5, flops=2_000_000_000, moved=2_000_000,
-    )(pre_recv, fine_state, send, msg_in, l3_state)
-
-    half = level_two // 2
-    fine_mid, keep, give = call(
+    around = window.reshape(chips * cores, 3, bnd, width).transpose(1, 0, 2, 3).reshape(-1, width)
+
+    pre, l3_rows, incidence = call(
+        sender_kernel,
+        [((edges, width), F32), ((3 * rows, width), BF16), ((nodes, edges), BF16)], scratch,
+        hbm=(1, 2, 3, 4), nargs=6, flops=2_000_000_000, moved=2_000_000,
+    )(pre_recv, fine_state, send, msg_in, l3_state, recv)
+
+    fine_mid, part = call(
         fine_kernel,
-        [((nodes, width), BF16), ((half, width), F32), ((half, width), BF16)],
-        [
-            pltpu.VMEM((edges, width), BF16),
-            pltpu.VMEM((edges, around.shape[0]), BF16),
-            pltpu.VMEM((nodes, edges), BF16),
-            pltpu.VMEM((level_two, width), F32),
-        ],
+        [((nodes, width), BF16), ((level_two, width), BF16)],
+        [pltpu.VMEM((edges, width), BF16), pltpu.VMEM((edges, around.shape[0]), BF16)],
         nargs=9, flops=3_000_000_000, moved=4_000_000,
-    )(pre, around, fine_state, send, recv, par, msg_in, msg_out, fine_gain)
-
-    half_out = [((half, width), BF16)]
-    (chip_sum,) = call(add_kernel, half_out, nargs=2)(keep, swapped(give, lambda k: k ^ 1))
-    (pair_sum,) = call(add_kernel, half_out, nargs=2)(chip_sum, swapped(chip_sum, lambda k: k ^ 2))
-    (half_mid,) = call(level_two_kernel, half_out, nargs=5)(
-        pair_sum, swapped(pair_sum, lambda k: (n_narrow // 2 - 1 - k // 2) * 2 + k % 2),
-        l2_state, up_weight, l2_gain,
-    )
+    )(pre, around, fine_state, send, incidence, par, msg_in, msg_out, fine_gain)
+
+    other = lax.ppermute(part, "core", [(0, 1), (1, 0)])
+    (chip_sums,) = call(add_kernel, [((chips, level_two, width), BF16)], nargs=2)(part, other)
+    chip_sums = lax.all_to_all(chip_sums, "chip", 0, 0, tiled=True)
     own, piece, l2_mid = call(
         functools.partial(window_kernel, level_three),
-        [((3 * rows, width), F32), ((rows, width), BF16), ((level_two, width), BF16)],
-        nargs=3,
-    )(half_mid, swapped(half_mid, lambda k: k ^ 1), parent)
-    piece = served(piece)
-    pieces = jnp.broadcast_to(piece[None], (n_narrow,) + piece.shape)
-    pieces = lax.all_to_all(pieces, "narrow", 0, 0, tiled=True)
+        [((3 * rows, width), F32), ((2 * rows, width), BF16), ((level_two, width), BF16)],
+        nargs=5,
+    )(chip_sums, l2_state, up_weight, l2_gain, parent)
+    (pieces,) = call(copies_kernel, [((chips, 2 * rows, width), BF16)], nargs=1)(served(piece))
+    pieces = lax.all_to_all(pieces, "chip", 0, 0, tiled=True)
 
     fine_out, l2_down = call(
         functools.partial(down_kernel, level_three),
@@ -329,21 +321,13 @@
 
 
 def solution(mesh):
-    both = P(("wide", "narrow"))
+    wide, narrow = mesh.devices.shape
+    mesh = jax.sharding.Mesh(mesh.devices.reshape(wide, narrow // 2, 2), ("wide", "chip", "core"))
+    every = ("wide", "chip", "core")
     return jax.shard_map(
         body,
         mesh=mesh,
-        in_specs=(
-            P(("wide", "narrow"), None),
-            P("wide", None),
-            P(),
-            both,
-            both,
-            both,
-            both,
-            P("wide"),
-        )
-        + (P(),) * 10,
-        out_specs=(P(("wide", "narrow"), None), P("wide", None)),
+        in_specs=(P(every, None), P("wide", None), P()) + (P(every),) * 4 + (P("wide"),) + (P(),) * 10,
+        out_specs=(P(every, None), P("wide", None)),
         check_vma=False,
     )

time: 84.8 us -> 83.6 us (0.986)
  the two profiles are of different devices: /device:TPU:1 before, /device:TPU:8 now
where the time goes in v2:
time: 83.6 us; the launch traced here: 83 us
  starting transfers between devices  26.6 us (32%)
  blocking collectives  25.3 us (30%)
  local copies, waits for them, and re-layouts  12.8 us (15%)
  Pallas kernels  12.7 us (15%)
  waiting for transfers between devices  3.41 us (4%)
  matrix products  1.27 us (2%)
  between operations  0.9 us (1%)
    ppermute x2, starting transfers between devices, passed_along(): lax.ppermute(value, 'wide', [(k, (k + steps) % count) for k in range(coun...  15.5 us
    all_to_all x1, blocking collectives, body(): chip_sums = lax.all_to_all(chip_sums, 'chip', 0, 0, tiled=True)  12.9 us
    unnamed x52, local copies, waits for them, and re-layouts  12.8 us
    all_to_all x1, blocking collectives, body(): pieces = lax.all_to_all(pieces, 'chip', 0, 0, tiled=True)  12.4 us
    all_to_all x1, starting transfers between devices, body(): window = lax.all_to_all(window, ('chip', 'core'), 0, 0, tiled=True)  4.92 us
    pallas_call x1, Pallas kernels, body(): call(fine_kernel, [((nodes, width), BF16), ((level_two, width), BF16)], [...  4.02 us
    ppermute x1, starting transfers between devices, served(): return lax.ppermute(value, ('wide', 'chip', 'core'), pairs)  3.92 us
    pallas_call x1, Pallas kernels, body(): call(sender_kernel, [((edges, width), F32), ((3 * rows, width), BF16), ((...  3.36 us
  transfers between devices with their start and end apart: 5, of which 2 were waited for; matrix products, arithmetic and copies ran while one was open for 0% of the time, Pallas kernels for 7%

profile of v2, /device:TPU:8, one launch (start us, length us, event | category | flops | bytes accessed | tf_op | source)
XLA Modules:
  0.0 83.0 jit_solution(239614436323120539)
XLA Ops:
  0.6 1.3 %convolution_convert_fusion.refs_1_ = bf16[16,256]{1,0:T(8,128)(2,1)S(1)} fusion(bf16[1024,256]{1,0:T(8,128)(2,1)} %fs_ref.1, s32[16]{0:T(128)} %param.21), kind=kOutput, calls=%fused_computation | convolution fusion | flops 8409088 | bytes 532544 | tf_op jit(solution)/shard_map/dot_general | solution.py:17
  1.9 3.4 %collective-permute-start = (bf16[16,256]{1,0:T(8,128)(2,1)S(1)}, bf16[16,256]{1,0:T(8,128)(2,1)S(1)}, u32[]{:S(2)}, u32[]{:S(2)}) collective-permute-start(bf16[16,256]{1,0:T(8,128)(2,1)S(1)} %convolution_convert_fusion.refs_1_), channel_id=1, source_target_pairs={{0,8},{8,16},{16,24},{24,32},{32,40},{40,48},{48,56},{56,64},{64,7... | collective-permute-start | bytes 24584 | tf_op jit(solution)/shard_map/ppermute | solution.py:216
  5.3 12.1 %collective-permute-start.1 = (bf16[16,256]{1,0:T(8,128)(2,1)S(1)}, bf16[16,256]{1,0:T(8,128)(2,1)S(1)}, u32[]{:S(2)}, u32[]{:S(2)}) collective-permute-start(bf16[16,256]{1,0:T(8,128)(2,1)S(1)} %convolution_convert_fusion.refs_1_), channel_id=1, source_target_pairs={{0,504},{8,0},{16,8},{24,16},{32,24},{40,32},{48,40},{56,48},{64,5... | collective-permute-start | bytes 24584 | tf_op jit(solution)/shard_map/ppermute | solution.py:216
  17.4 0.0 copy-start
  17.4 1.0 %copy-done = bf16[1024,256]{1,0:T(8,128)(2,1)S(1)} copy-done((bf16[1024,256]{1,0:T(8,128)(2,1)S(1)}, bf16[1024,256]{1,0:T(8,128)(2,1)}, u32[]{:S(2)}) %copy-start) | copy-done | bytes 524312
  18.5 0.9 %copy-done.13 = bf16[512,256]{1,0:T(8,128)(2,1)S(1)} copy-done((bf16[512,256]{1,0:T(8,128)(2,1)S(1)}, bf16[512,256]{1,0:T(8,128)(2,1)}, u32[]{:S(2)}) %copy-start.13) | copy-done | bytes 262168
  19.4 0.7 copy-done.16
  20.1 0.0 copy-start.18
  20.1 2.1 %shard_map.185.before_ref = f32[2048,256]{1,0:T(8,128)S(1)} custom-call(bf16[1024,256]{1,0:T(8,128)(2,1)S(1)} %copy-done, s32[16,128]{1,0:T(8,128)S(1)} %bitcast.19, bf16[512,256]{1,0:T(8,128)(2,1)S(1)} %copy-done.13), custom_call_target="tpu_custom_call" | custom-call | flops 2000000000 | bytes 2000000 | tf_op jit(solution)/shard_map/pallas_call | solution.py:276
  22.3 0.0 copy-start.22
  22.3 1.3 %copy-done.22 = f32[2048,256]{1,0:T(8,128)} copy-done((f32[2048,256]{1,0:T(8,128)}, f32[2048,256]{1,0:T(8,128)S(1)}, u32[]{:S(2)}) %copy-start.22) | copy-done | bytes 2097176
  23.6 0.0 collective-permute-done.refs_0_
  23.6 0.0 collective-permute-done.1.refs_2_
  23.6 0.7 shard_map.187
  24.3 4.9 %all-to-all-start = ((bf16[8,48,256]{2,1,0:T(8,128)(2,1)}), bf16[8,48,256]{2,1,0:T(8,128)(2,1)S(1)}, u32[]{:S(2)}, u32[]{:S(2)}) async-start(bf16[8,48,256]{2,1,0:T(8,128)(2,1)} %shard_map.187), calls=%async_computation | async-start | bytes 393216 | tf_op jit(solution)/shard_map/all_to_all | solution.py:284
  29.2 0.0 copy-done.1
  29.2 0.0 copy-done.12
  29.3 0.0 copy-done.14
  29.3 0.0 copy-done.17
  29.3 0.0 copy-done.18
  29.3 0.0 copy-start.23
  29.3 1.6 %copy-done.23 = f32[2048,256]{1,0:T(8,128)S(1)} copy-done((f32[2048,256]{1,0:T(8,128)S(1)}, f32[2048,256]{1,0:T(8,128)}, u32[]{:S(2)}) %copy-start.23) | copy-done | bytes 2097176
  30.9 3.4 %shard_map.186 = (f32[2048,256]{1,0:T(8,128)S(1)}, bf16[192,256]{1,0:T(8,128)(2,1)S(1)}, bf16[1024,2048]{1,0:T(8,128)(2,1)S(1)}) custom-call(f32[2048,256]{1,0:T(8,128)S(1)} %copy-done.23, bf16[1024,256]{1,0:T(8,128)(2,1)S(1)} %copy-done.1, s32[16,128]{1,0:T(8,128)S(1)} %bitcast.21, bf16[512,256]{1,0:T(8,128)(2,1)S(1)} %copy-done.14, ...), custom_call_target="tpu_custom_call" | custom-call | flops 2000000000 | bytes 2000000 | tf_op jit(solution)/shard_map/pallas_call | solution.py:288
  34.2 0.0 copy-start.20
  34.3 1.9 %copy-done.20 = bf16[1024,2048]{1,0:T(8,128)(2,1)} copy-done((bf16[1024,2048]{1,0:T(8,128)(2,1)}, bf16[1024,2048]{1,0:T(8,128)(2,1)S(1)}, u32[]{:S(2)}) %copy-start.20) | copy-done | bytes 4194328
  36.2 1.4 %copy-done.24 = f32[2048,256]{1,0:T(8,128)} copy-done((f32[2048,256]{1,0:T(8,128)}, f32[2048,256]{1,0:T(8,128)S(1)}, u32[]{:S(2)}) %copy-start.24) | copy-done | bytes 2097176
  37.6 0.0 all-to-all-done
  37.6 0.0 copy-done.8
  37.6 0.0 copy-done.15
  37.6 0.0 copy-done.19
  37.6 2.2 %copy-done.21 = bf16[1024,2048]{1,0:T(8,128)(2,1)S(1)} copy-done((bf16[1024,2048]{1,0:T(8,128)(2,1)S(1)}, bf16[1024,2048]{1,0:T(8,128)(2,1)}, u32[]{:S(2)}) %copy-start.21) | copy-done | bytes 4194328
  39.8 1.6 %copy-done.25 = f32[2048,256]{1,0:T(8,128)S(1)} copy-done((f32[2048,256]{1,0:T(8,128)S(1)}, f32[2048,256]{1,0:T(8,128)}, u32[]{:S(2)}) %copy-start.25) | copy-done | bytes 2097176
  41.4 4.0 %shard_map.188 = (bf16[1024,256]{1,0:T(8,128)(2,1)S(1)}, bf16[256,256]{1,0:T(8,128)(2,1)S(1)}) custom-call(f32[2048,256]{1,0:T(8,128)S(1)} %copy-done.25, bf16[384,256]{1,0:T(8,128)(2,1)S(1)} %bitcast.12, bf16[1024,256]{1,0:T(8,128)(2,1)S(1)} %copy-done.1, s32[16,128]{1,0:T(8,128)S(1)} %bitcast.22, bf16[1024,2048]{1,0:T(8,128)(2,1)S(1)} %copy-done.21, ...), custom_call_target="tpu_custom_call" | custom-call | flops 3000000000 | bytes 4000000 | tf_op jit(solution)/shard_map/pallas_call | solution.py:294
  45.5 0.0 copy-start.4
  45.5 0.0 copy-start.5
  45.5 0.0 copy-start.6
  45.5 0.0 copy-start.7
  45.5 0.0 copy-start.11
  45.5 2.2 %collective-permute-start.2 = (bf16[256,256]{1,0:T(8,128)(2,1)S(1)}, bf16[256,256]{1,0:T(8,128)(2,1)S(1)}, u32[]{:S(2)}, u32[]{:S(2)}) collective-permute-start(bf16[256,256]{1,0:T(8,128)(2,1)S(1)} %get-tuple-element.18.a_ref), channel_id=1, source_target_pairs={{0,1},{1,0},{2,3},{3,2},{4,5},{5,4},{6,7},{7,6},{8,9},{9,8},{10,11... | collective-permute-start | bytes 393224 | tf_op jit(solution)/shard_map/ppermute | solution.py:301
  47.7 1.2 %collective-permute-done.2.b_ref = bf16[256,256]{1,0:T(8,128)(2,1)S(1)} collective-permute-done((bf16[256,256]{1,0:T(8,128)(2,1)S(1)}, bf16[256,256]{1,0:T(8,128)(2,1)S(1)}, u32[]{:S(2)}, u32[]{:S(2)}) %collective-permute-start.2) | collective-permute-done | bytes 131104 | tf_op jit(solution)/shard_map/ppermute | solution.py:301
  48.9 12.9 %all_to_all.15.parts_ref = bf16[4,256,256]{2,1,0:T(8,128)(2,1)S(1)} all-to-all(bf16[4,256,256]{2,1,0:T(8,128)(2,1)S(1)} %shard_map.189), channel_id=1, replica_groups=mesh['wide'=64,'chip'=4,'core'=2] {'chip'}, dimensions={0} | all-to-all | bytes 1048576 | tf_op jit(solution)/shard_map/all_to_all | solution.py:303
  61.9 0.0 copy-done.3
  61.9 0.5 shard_map.190
  62.4 3.9 %collective-permute-start.3 = (bf16[128,256]{1,0:T(8,128)(2,1)S(1)}, bf16[128,256]{1,0:T(8,128)(2,1)S(1)}, u32[]{:S(2)}, u32[]{:S(2)}) collective-permute-start(bf16[128,256]{1,0:T(8,128)(2,1)S(1)} %get-tuple-element.20), channel_id=1, source_target_pairs={{0,8},{1,9},{2,506},{3,507},{4,20},{5,21},{6,502},{7,503},{8,16},{... | collective-permute-start | bytes 196616 | tf_op jit(solution)/shard_map/ppermute | solution.py:230
  66.3 2.2 %collective-permute-done.3.refs_0_ = bf16[128,256]{1,0:T(8,128)(2,1)S(1)} collective-permute-done((bf16[128,256]{1,0:T(8,128)(2,1)S(1)}, bf16[128,256]{1,0:T(8,128)(2,1)S(1)}, u32[]{:S(2)}, u32[]{:S(2)}) %collective-permute-start.3) | collective-permute-done | bytes 65568 | tf_op jit(solution)/shard_map/ppermute | solution.py:230
  68.6 12.4 %all_to_all.16.pieces_ref = bf16[4,128,256]{2,1,0:T(8,128)(2,1)S(1)} all-to-all(bf16[4,128,256]{2,1,0:T(8,128)(2,1)S(1)} %shard_map.191), channel_id=1, replica_groups=mesh['wide'=64,'chip'=4,'core'=2] {'chip'}, dimensions={0} | all-to-all | bytes 524288 | tf_op jit(solution)/shard_map/all_to_all | solution.py:310
  81.0 0.0 copy-done.5
  81.0 2.0 %shard_map.192 = (bf16[1024,256]{1,0:T(8,128)(2,1)}, bf16[256,256]{1,0:T(8,128)(2,1)}) custom-call(f32[192,256]{1,0:T(8,128)S(1)} %get-tuple-element.19.own_ref, bf16[4,128,256]{2,1,0:T(8,128)(2,1)S(1)} %all_to_all.16.pieces_ref, bf16[192,256]{1,0:T(8,128)(2,1)S(1)} %get-tuple-element.21.l3_rows_ref, f32[1,256]{1,0:T(1,128)S(1)} %bitcast.18, ...), custom_call_target="tpu_custom_call" | custom-call | tf_op jit(solution)/shard_map/pallas_call | solution.py:312
  (26 shorter events, 0.1 us)
Async XLA Ops:
  1.9 21.7 %collective-permute-start = (bf16[16,256]{1,0:T(8,128)(2,1)S(1)}, bf16[16,256]{1,0:T(8,128)(2,1)S(1)}, u32[]{:S(2)}, u32[]{:S(2)}) collective-permute-start(bf16[16,256]{1,0:T(8,128)(2,1)S(1)} %convolution_convert_fusion.refs_1_), channel_id=1, source_target_pairs={{0,8},{8,16},{16,24},{24,32},{32,40},{40,48},{48,56},{56,64},{64,7... | collective-permute-start | bytes 24584 | tf_op jit(solution)/shard_map/ppermute | solution.py:216
  5.3 18.3 %collective-permute-start.1 = (bf16[16,256]{1,0:T(8,128)(2,1)S(1)}, bf16[16,256]{1,0:T(8,128)(2,1)S(1)}, u32[]{:S(2)}, u32[]{:S(2)}) collective-permute-start(bf16[16,256]{1,0:T(8,128)(2,1)S(1)} %convolution_convert_fusion.refs_1_), channel_id=1, source_target_pairs={{0,504},{8,0},{16,8},{24,16},{32,24},{40,32},{48,40},{56,48},{64,5... | collective-permute-start | bytes 24584 | tf_op jit(solution)/shard_map/ppermute | solution.py:216
  17.4 1.0 %copy-start = (bf16[1024,256]{1,0:T(8,128)(2,1)S(1)}, bf16[1024,256]{1,0:T(8,128)(2,1)}, u32[]{:S(2)}) copy-start(bf16[1024,256]{1,0:T(8,128)(2,1)} %fs_ref.1) | copy-start | bytes 1572868
  18.5 0.9 %copy-start.13 = (bf16[512,256]{1,0:T(8,128)(2,1)S(1)}, bf16[512,256]{1,0:T(8,128)(2,1)}, u32[]{:S(2)}) copy-start(bf16[512,256]{1,0:T(8,128)(2,1)} %w_in_ref.1) | copy-start | bytes 786436
  19.4 0.7 copy-start.16
  20.1 9.1 %copy-start.1 = (bf16[1024,256]{1,0:T(8,128)(2,1)S(1)}, bf16[1024,256]{1,0:T(8,128)(2,1)}, u32[]{:S(2)}) copy-start(bf16[1024,256]{1,0:T(8,128)(2,1)} %fs_ref.1) | copy-start | bytes 1572868
  20.1 9.1 %copy-start.12 = (bf16[4096,256]{1,0:T(8,128)(2,1)S(1)}, bf16[4096,256]{1,0:T(8,128)(2,1)}, u32[]{:S(2)}) copy-start(bf16[4096,256]{1,0:T(8,128)(2,1)} %l3_hbm.1) | copy-start | bytes 6291460
  20.1 9.1 %copy-start.14 = (bf16[512,256]{1,0:T(8,128)(2,1)S(1)}, bf16[512,256]{1,0:T(8,128)(2,1)}, u32[]{:S(2)}) copy-start(bf16[512,256]{1,0:T(8,128)(2,1)} %w_in_ref.1) | copy-start | bytes 786436
  20.1 9.1 %copy-start.17 = (s32[2048]{0:T(1024)S(1)}, s32[2048]{0:T(1024)}, u32[]{:S(2)}) copy-start(s32[2048]{0:T(1024)} %param.23) | copy-start | bytes 24580
  20.1 9.1 %copy-start.18 = (s32[2048]{0:T(1024)S(1)}, s32[2048]{0:T(1024)}, u32[]{:S(2)}) copy-start(s32[2048]{0:T(1024)} %param.22) | copy-start | bytes 24580
  22.3 1.4 %copy-start.22 = (f32[2048,256]{1,0:T(8,128)}, f32[2048,256]{1,0:T(8,128)S(1)}, u32[]{:S(2)}) copy-start(f32[2048,256]{1,0:T(8,128)S(1)} %shard_map.185.before_ref) | copy-start | bytes 6291460
  24.3 13.3 %all-to-all-start = ((bf16[8,48,256]{2,1,0:T(8,128)(2,1)}), bf16[8,48,256]{2,1,0:T(8,128)(2,1)S(1)}, u32[]{:S(2)}, u32[]{:S(2)}) async-start(bf16[8,48,256]{2,1,0:T(8,128)(2,1)} %shard_map.187), calls=%async_computation | async-start | bytes 393216 | tf_op jit(solution)/shard_map/all_to_all | solution.py:284
  29.3 1.6 %copy-start.23 = (f32[2048,256]{1,0:T(8,128)S(1)}, f32[2048,256]{1,0:T(8,128)}, u32[]{:S(2)}) copy-start(f32[2048,256]{1,0:T(8,128)} %copy-done.22) | copy-start | bytes 6291460
  30.9 6.7 %copy-start.8 = (s32[1024]{0:T(1024)S(1)}, s32[1024]{0:T(1024)}, u32[]{:S(2)}) copy-start(s32[1024]{0:T(1024)} %param.24) | copy-start | bytes 12292
  30.9 6.7 %copy-start.15 = (bf16[256,256]{1,0:T(8,128)(2,1)S(1)}, bf16[256,256]{1,0:T(8,128)(2,1)}, u32[]{:S(2)}) copy-start(bf16[256,256]{1,0:T(8,128)(2,1)} %w_out_ref.1) | copy-start | bytes 393220
  30.9 6.7 %copy-start.19 = (f32[256]{0:T(256)S(1)}, f32[256]{0:T(256)}, u32[]{:S(2)}) copy-start(f32[256]{0:T(256)} %param.28) | copy-start | bytes 3076
  34.2 2.0 %copy-start.20 = (bf16[1024,2048]{1,0:T(8,128)(2,1)}, bf16[1024,2048]{1,0:T(8,128)(2,1)S(1)}, u32[]{:S(2)}) copy-start(bf16[1024,2048]{1,0:T(8,128)(2,1)S(1)} %get-tuple-element.17.inc_ref) | copy-start | bytes 12582916
  36.2 1.4 %copy-start.24 = (f32[2048,256]{1,0:T(8,128)}, f32[2048,256]{1,0:T(8,128)S(1)}, u32[]{:S(2)}) copy-start(f32[2048,256]{1,0:T(8,128)S(1)} %get-tuple-element.14.pre_ref) | copy-start | bytes 6291460
  37.6 2.2 %copy-start.21 = (bf16[1024,2048]{1,0:T(8,128)(2,1)S(1)}, bf16[1024,2048]{1,0:T(8,128)(2,1)}, u32[]{:S(2)}) copy-start(bf16[1024,2048]{1,0:T(8,128)(2,1)} %copy-done.20) | copy-start | bytes 12582916
  39.8 1.6 %copy-start.25 = (f32[2048,256]{1,0:T(8,128)S(1)}, f32[2048,256]{1,0:T(8,128)}, u32[]{:S(2)}) copy-start(f32[2048,256]{1,0:T(8,128)} %copy-done.24) | copy-start | bytes 6291460
  41.4 20.5 %copy-start.2 = (bf16[256,256]{1,0:T(8,128)(2,1)S(1)}, bf16[256,256]{1,0:T(8,128)(2,1)}, u32[]{:S(2)}) copy-start(bf16[256,256]{1,0:T(8,128)(2,1)} %state_ref.1) | copy-start | bytes 393220
  41.4 20.5 %copy-start.3 = (bf16[256,256]{1,0:T(8,128)(2,1)S(1)}, bf16[256,256]{1,0:T(8,128)(2,1)}, u32[]{:S(2)}) copy-start(bf16[256,256]{1,0:T(8,128)(2,1)} %w_up_ref.1) | copy-start | bytes 393220
  41.4 20.5 %copy-start.9 = (s32[256]{0:T(256)S(1)}, s32[256]{0:T(256)}, u32[]{:S(2)}) copy-start(s32[256]{0:T(256)} %param.25) | copy-start | bytes 3076
  41.4 20.5 %copy-start.10 = (f32[256]{0:T(256)S(1)}, f32[256]{0:T(256)}, u32[]{:S(2)}) copy-start(f32[256]{0:T(256)} %param.30) | copy-start | bytes 3076
  45.5 35.5 %copy-start.4 = (bf16[256,256]{1,0:T(8,128)(2,1)S(1)}, bf16[256,256]{1,0:T(8,128)(2,1)}, u32[]{:S(2)}) copy-start(bf16[256,256]{1,0:T(8,128)(2,1)} %w1_ref.1) | copy-start | bytes 393220
  45.5 35.5 %copy-start.5 = (bf16[256,256]{1,0:T(8,128)(2,1)S(1)}, bf16[256,256]{1,0:T(8,128)(2,1)}, u32[]{:S(2)}) copy-start(bf16[256,256]{1,0:T(8,128)(2,1)} %w2_ref.1) | copy-start | bytes 393220
  45.5 35.5 %copy-start.6 = (bf16[256,256]{1,0:T(8,128)(2,1)S(1)}, bf16[256,256]{1,0:T(8,128)(2,1)}, u32[]{:S(2)}) copy-start(bf16[256,256]{1,0:T(8,128)(2,1)} %w_down_ref.1) | copy-start | bytes 393220
  45.5 35.5 %copy-start.7 = (bf16[256,256]{1,0:T(8,128)(2,1)S(1)}, bf16[256,256]{1,0:T(8,128)(2,1)}, u32[]{:S(2)}) copy-start(bf16[256,256]{1,0:T(8,128)(2,1)} %w_fine_ref.1) | copy-start | bytes 393220
  45.5 35.5 %copy-start.11 = (f32[256]{0:T(256)S(1)}, f32[256]{0:T(256)}, u32[]{:S(2)}) copy-start(f32[256]{0:T(256)} %param.31) | copy-start | bytes 3076
  45.5 3.4 %collective-permute-start.2 = (bf16[256,256]{1,0:T(8,128)(2,1)S(1)}, bf16[256,256]{1,0:T(8,128)(2,1)S(1)}, u32[]{:S(2)}, u32[]{:S(2)}) collective-permute-start(bf16[256,256]{1,0:T(8,128)(2,1)S(1)} %get-tuple-element.18.a_ref), channel_id=1, source_target_pairs={{0,1},{1,0},{2,3},{3,2},{4,5},{5,4},{6,7},{7,6},{8,9},{9,8},{10,11... | collective-permute-start | bytes 393224 | tf_op jit(solution)/shard_map/ppermute | solution.py:301
  62.4 6.2 %collective-permute-start.3 = (bf16[128,256]{1,0:T(8,128)(2,1)S(1)}, bf16[128,256]{1,0:T(8,128)(2,1)S(1)}, u32[]{:S(2)}, u32[]{:S(2)}) collective-permute-start(bf16[128,256]{1,0:T(8,128)(2,1)S(1)} %get-tuple-element.20), channel_id=1, source_target_pairs={{0,8},{1,9},{2,506},{3,507},{4,20},{5,21},{6,502},{7,503},{8,16},{... | collective-permute-start | bytes 196616 | tf_op jit(solution)/shard_map/ppermute | solution.py:230

commit v3 on v2

--- a/solution.py
+++ b/solution.py
@@ -51,84 +51,73 @@
     return jnp.where(high == jnp.asarray(tile, BF16), hot, jnp.zeros_like(hot))
 
 
-def fetch(pairs, sems):
-    copies = [pltpu.make_async_copy(a, b, sems.at[k]) for k, (a, b) in enumerate(pairs)]
+def project_kernel(fs_ref, w_in_ref, send_ref, recv_ref, l3_hbm, proj_ref, cols_ref, l3_rows_ref, sems):
+    nodes, width = fs_ref.shape
+    wide = lax.axis_index("wide")
+    count = lax.axis_size("wide")
+    rows = l3_rows_ref.shape[0] // 3
+    copies = []
+    for k in range(3):
+        block = lax.rem(wide + (k + count - 1), count)
+        copies.append(
+            pltpu.make_async_copy(
+                l3_hbm.at[pl.ds(pl.multiple_of(block * rows, rows), rows)],
+                l3_rows_ref.at[pl.ds(k * rows, rows)],
+                sems.at[k],
+            )
+        )
     for copy in copies:
         copy.start()
+    proj_ref[:nodes] = dot(fs_ref[...], w_in_ref[:width]).astype(BF16)
+    proj_ref[nodes:] = dot(fs_ref[...], w_in_ref[width:]).astype(BF16)
+    index = jnp.concatenate([send_ref[...], recv_ref[...]], axis=0)
+    cols_ref[0], cols_ref[1] = column_parts(index)
     for copy in copies:
         copy.wait()
 
 
-def gathered(index_ref, proj, hot, out_ref, before_ref=None):
-    tiles = proj.shape[0] // LANES
-    low, high = column_parts(index_ref[...])
-    for block in range(out_ref.shape[0] // EDGE_BLOCK):
+def gather_kernel(proj_ref, cols_ref, pre_ref, hot):
+    edges = pre_ref.shape[0]
+    nodes = proj_ref.shape[0] // 2
+    groups = edges // LANES
+    for block in range(edges // EDGE_BLOCK):
         for part in range(EDGE_BLOCK // LANES):
             j = block * (EDGE_BLOCK // LANES) + part
             span = slice(j * LANES, (j + 1) * LANES)
-            hot_j, high_j = lane_select(low[:, j : j + 1], high[:, j : j + 1])
-            for t in range(tiles):
-                hot[span, t * LANES : (t + 1) * LANES] = pick(hot_j, high_j, t)
+            for side in range(2):
+                k = side * groups + j
+                hot_j, high_j = lane_select(cols_ref[0, :, k : k + 1], cols_ref[1, :, k : k + 1])
+                for t in range(nodes // LANES):
+                    start = side * nodes + t * LANES
+                    hot[span, start : start + LANES] = pick(hot_j, high_j, t)
         span = slice(block * EDGE_BLOCK, (block + 1) * EDGE_BLOCK)
-        rows = dot(hot[span], proj[...])
-        out_ref[span] = rows if before_ref is None else rows + before_ref[span]
-
-
-def receiver_kernel(fs_hbm, recv_hbm, w_in_hbm, pre_ref, fs, recv, w_in, proj, hot, sems):
-    width = fs.shape[1]
-    fetch([(fs_hbm, fs), (recv_hbm, recv), (w_in_hbm.at[pl.ds(width, width)], w_in)], sems)
-    proj[...] = dot(fs[...], w_in[...]).astype(BF16)
-    gathered(recv, proj, hot, pre_ref)
-
-
-def sender_kernel(
-    before_ref, fs_hbm, send_hbm, w_in_hbm, l3_hbm, recv_ref, pre_ref, l3_rows_ref, inc_ref,
-    fs, send, w_in, proj, hot, sems,
-):
-    width = fs.shape[1]
-    wide = lax.axis_index("wide")
-    count = lax.axis_size("wide")
-    rows = l3_rows_ref.shape[0] // 3
-    pairs = [(fs_hbm, fs), (send_hbm, send), (w_in_hbm.at[pl.ds(0, width)], w_in)]
-    for k in range(3):
-        block = lax.rem(wide + (k + count - 1), count)
-        pairs.append(
-            (
-                l3_hbm.at[pl.ds(pl.multiple_of(block * rows, rows), rows)],
-                l3_rows_ref.at[pl.ds(k * rows, rows)],
-            )
-        )
-    fetch(pairs, sems)
-    proj[...] = dot(fs[...], w_in[...]).astype(BF16)
-    gathered(send, proj, hot, pre_ref, before_ref)
-    for j in range(recv_ref.shape[0]):
-        hot_r, high_r = row_select(recv_ref[j : j + 1])
-        for t in range(inc_ref.shape[0] // LANES):
-            inc_ref[t * LANES : (t + 1) * LANES, j * LANES : (j + 1) * LANES] = pick(hot_r, high_r, t)
+        pre_ref[span] = dot(hot[span], proj_ref[...]).astype(BF16)
 
 
 def fine_kernel(
-    pre_ref, around_ref, fs_ref, send_ref, inc_ref, par_ref, w_in_ref, w_out_ref, gain_ref,
-    mid_ref, part_ref, hidden, hot,
+    pre_ref, around_ref, fs_ref, cols_ref, recv_ref, par_ref, w_in_ref, w_out_ref, gain_ref,
+    mid_ref, part_ref, hidden, hot, inc,
 ):
     nodes, width = fs_ref.shape
     edges = pre_ref.shape[0]
     tiles = nodes // LANES
     extra = around_ref.shape[0] // LANES
     proj = dot(around_ref[...], w_in_ref[:width]).astype(BF16)
-    send_low, send_high = column_parts(send_ref[...])
     for block in range(edges // EDGE_BLOCK):
         for part in range(EDGE_BLOCK // LANES):
             j = block * (EDGE_BLOCK // LANES) + part
             span = slice(j * LANES, (j + 1) * LANES)
-            hot_s, high_s = lane_select(send_low[:, j : j + 1], send_high[:, j : j + 1])
+            hot_s, high_s = lane_select(cols_ref[0, :, j : j + 1], cols_ref[1, :, j : j + 1])
             for t in range(extra):
                 hot[span, t * LANES : (t + 1) * LANES] = pick(hot_s, high_s, tiles + t)
+            hot_r, high_r = row_select(recv_ref[j : j + 1])
+            for t in range(tiles):
+                inc[t * LANES : (t + 1) * LANES, span] = pick(hot_r, high_r, t)
         span = slice(block * EDGE_BLOCK, (block + 1) * EDGE_BLOCK)
-        hidden[span] = silu(pre_ref[span] + dot(hot[span], proj)).astype(BF16)
+        hidden[span] = silu(pre_ref[span].astype(F32) + dot(hot[span], proj)).astype(BF16)
     for block in range(nodes // EDGE_BLOCK):
         span = slice(block * EDGE_BLOCK, (block + 1) * EDGE_BLOCK)
-        agg = dot(dot(inc_ref[span], hidden[...]).astype(BF16), w_out_ref[...])
+        agg = dot(dot(inc[span], hidden[...]).astype(BF16), w_out_ref[...])
         mid_ref[span] = (fs_ref[span].astype(F32) + rms_scale(agg, gain_ref[...])).astype(BF16)
     total = jnp.zeros(part_ref.shape, F32)
     for j in range(tiles):
@@ -265,19 +254,13 @@
     hot = (boundary[:, None] == jnp.arange(nodes, dtype=jnp.int32)[None, :]).astype(BF16)
     exported = dot(hot, fine_state).astype(BF16)
     behind, ahead = passed_along(exported, 1), passed_along(exported, -1)
-    scratch = [
-        pltpu.VMEM((nodes, width), BF16),
-        pltpu.VMEM(send.shape, jnp.int32),
-        pltpu.VMEM((width, width), BF16),
-        pltpu.VMEM((nodes, width), BF16),
-        pltpu.VMEM((edges, nodes), BF16),
-        pltpu.SemaphoreType.DMA((6,)),
-    ]
-    (pre_recv,) = call(
-        receiver_kernel, [((edges, width), F32)], scratch, hbm=(0, 1, 2), nargs=3,
-        flops=2_000_000_000, moved=2_000_000,
-    )(fine_state, recv, msg_in)
-    behind, ahead, pre_recv = lax.optimization_barrier((behind, ahead, pre_recv))
+    proj, cols, l3_rows = call(
+        project_kernel,
+        [((2 * nodes, width), BF16), ((2, LANES, 2 * send.shape[0]), F32), ((3 * rows, width), BF16)],
+        [pltpu.SemaphoreType.DMA((3,))],
+        hbm=(4,), nargs=5, vmem=61, flops=500_000_000, moved=2_000_000,
+    )(fine_state, msg_in, send, recv, l3_state)
+    behind, ahead, proj = lax.optimization_barrier((behind, ahead, proj))
     (window,) = call(
         copies_kernel, [((chips * cores, 3 * boundary.shape[0], width), BF16)], nargs=3
     )(behind, exported, ahead)
@@ -285,18 +268,21 @@
     bnd = boundary.shape[0]
     around = window.reshape(chips * cores, 3, bnd, width).transpose(1, 0, 2, 3).reshape(-1, width)
 
-    pre, l3_rows, incidence = call(
-        sender_kernel,
-        [((edges, width), F32), ((3 * rows, width), BF16), ((nodes, edges), BF16)], scratch,
-        hbm=(1, 2, 3, 4), nargs=6, flops=2_000_000_000, moved=2_000_000,
-    )(pre_recv, fine_state, send, msg_in, l3_state, recv)
+    (pre,) = call(
+        gather_kernel, [((edges, width), BF16)], [pltpu.VMEM((edges, 2 * nodes), BF16)],
+        nargs=2, flops=4_000_000_000, moved=2_000_000,
+    )(proj, cols)
 
     fine_mid, part = call(
         fine_kernel,
         [((nodes, width), BF16), ((level_two, width), BF16)],
-        [pltpu.VMEM((edges, width), BF16), pltpu.VMEM((edges, around.shape[0]), BF16)],
+        [
+            pltpu.VMEM((edges, width), BF16),
+            pltpu.VMEM((edges, around.shape[0]), BF16),
+            pltpu.VMEM((nodes, edges), BF16),
+        ],
         nargs=9, flops=3_000_000_000, moved=4_000_000,
-    )(pre, around, fine_state, send, incidence, par, msg_in, msg_out, fine_gain)
+    )(pre, around, fine_state, cols, recv, par, msg_in, msg_out, fine_gain)
 
     other = lax.ppermute(part, "core", [(0, 1), (1, 0)])
     (chip_sums,) = call(add_kernel, [((chips, level_two, width), BF16)], nargs=2)(part, other)

time: 83.6 us -> 77.3 us (0.925)
  local copies, waits for them, and re-layouts: 12.8 us -> 2.23 us
  waiting for transfers between devices: 3.41 us -> 8.43 us
    unnamed x52 -> x38, local copies, waits for them, and re-layouts: 12.8 us -> 2.22 us
    ppermute x2, waiting for transfers between devices: 0.01 us -> 3.89 us  [passed_along(): lax.ppermute(value, 'wide', [(k, (k + steps) % count) for k in range(coun...]
  transfers between devices with their start and end apart: 5 -> 5, of which waited for: 2 -> 4; matrix products, arithmetic and copies ran while one was open for 0% -> 0% of each run, Pallas kernels for 7% -> 8%
where the time goes in v3:
time: 77.3 us; the launch traced here: 76.8 us
  starting transfers between devices  25.9 us (34%)
  blocking collectives  24.9 us (32%)
  Pallas kernels  13.2 us (17%)
  waiting for transfers between devices  8.43 us (11%)
  local copies, waits for them, and re-layouts  2.23 us (3%)
  matrix products  1.27 us (2%)
  between operations  0.92 us (1%)
    ppermute x2, starting transfers between devices, passed_along(): lax.ppermute(value, 'wide', [(k, (k + steps) % count) for k in range(coun...  15.5 us
    all_to_all x1, blocking collectives, body(): chip_sums = lax.all_to_all(chip_sums, 'chip', 0, 0, tiled=True)  12.5 us
    all_to_all x1, blocking collectives, body(): pieces = lax.all_to_all(pieces, 'chip', 0, 0, tiled=True)  12.4 us
    all_to_all x1, starting transfers between devices, body(): window = lax.all_to_all(window, ('chip', 'core'), 0, 0, tiled=True)  4.92 us
    pallas_call x1, Pallas kernels, body(): call(fine_kernel, [((nodes, width), BF16), ((level_two, width), BF16)], [...  4.19 us
    ppermute x2, waiting for transfers between devices, passed_along(): lax.ppermute(value, 'wide', [(k, (k + steps) % count) for k in range(coun...  3.89 us
    ppermute x1, starting transfers between devices, served(): return lax.ppermute(value, ('wide', 'chip', 'core'), pairs)  3.37 us
    pallas_call x1, Pallas kernels, body(): call(project_kernel, [((2 * nodes, width), BF16), ((2, LANES, 2 * send.sh...  3.04 us
  transfers between devices with their start and end apart: 5, of which 4 were waited for; matrix products, arithmetic and copies ran while one was open for 0% of the time, Pallas kernels for 8%

profile of v3, /device:TPU:8, one launch (start us, length us, event | category | flops | bytes accessed | tf_op | source)
XLA Modules:
  0.0 76.8 jit_solution(4836813808231753531)
XLA Ops:
  0.6 1.3 %convolution_convert_fusion.refs_1_ = bf16[16,256]{1,0:T(8,128)(2,1)S(1)} fusion(bf16[1024,256]{1,0:T(8,128)(2,1)} %fs_ref.3, s32[16]{0:T(128)} %param.21), kind=kOutput, calls=%fused_computation | convolution fusion | flops 8409088 | bytes 532544 | tf_op jit(solution)/shard_map/dot_general | solution.py:17
  1.9 13.6 %collective-permute-start.1 = (bf16[16,256]{1,0:T(8,128)(2,1)S(1)}, bf16[16,256]{1,0:T(8,128)(2,1)S(1)}, u32[]{:S(2)}, u32[]{:S(2)}) collective-permute-start(bf16[16,256]{1,0:T(8,128)(2,1)S(1)} %convolution_convert_fusion.refs_1_), channel_id=1, source_target_pairs={{0,504},{8,0},{16,8},{24,16},{32,24},{40,32},{48,40},{56,48},{64,5... | collective-permute-start | bytes 24584 | tf_op jit(solution)/shard_map/ppermute | solution.py:205
  15.5 1.9 %collective-permute-start = (bf16[16,256]{1,0:T(8,128)(2,1)S(1)}, bf16[16,256]{1,0:T(8,128)(2,1)S(1)}, u32[]{:S(2)}, u32[]{:S(2)}) collective-permute-start(bf16[16,256]{1,0:T(8,128)(2,1)S(1)} %convolution_convert_fusion.refs_1_), channel_id=1, source_target_pairs={{0,8},{8,16},{16,24},{24,32},{32,40},{40,48},{48,56},{56,64},{64,7... | collective-permute-start | bytes 24584 | tf_op jit(solution)/shard_map/ppermute | solution.py:205
  17.4 3.0 %shard_map.185 = (bf16[2048,256]{1,0:T(8,128)(2,1)}, f32[2,128,32]{2,1,0:T(8,128)}, bf16[192,256]{1,0:T(8,128)(2,1)}) custom-call(bf16[1024,256]{1,0:T(8,128)(2,1)} %fs_ref.3, bf16[512,256]{1,0:T(8,128)(2,1)} %w_in_ref.3, s32[16,128]{1,0:T(8,128)} %bitcast.23, s32[16,128]{1,0:T(8,128)} %bitcast.13, bf16[4096,256]{1,0:T(8,128)(2,1)} %l3_hbm.1), custom_call_target="tpu_custom_call" | custom-call | flops 500000000 | bytes 2000000 | tf_op jit(solution)/shard_map/pallas_call | solution.py:257
  20.5 0.0 collective-permute-done.1.refs_2_
  20.5 3.9 %collective-permute-done.refs_0_ = bf16[16,256]{1,0:T(8,128)(2,1)S(1)} collective-permute-done((bf16[16,256]{1,0:T(8,128)(2,1)S(1)}, bf16[16,256]{1,0:T(8,128)(2,1)S(1)}, u32[]{:S(2)}, u32[]{:S(2)}) %collective-permute-start) | collective-permute-done | bytes 8224 | tf_op jit(solution)/shard_map/ppermute | solution.py:205
  24.4 0.7 shard_map.187
  25.1 4.9 %all-to-all-start = ((bf16[8,48,256]{2,1,0:T(8,128)(2,1)}), bf16[8,48,256]{2,1,0:T(8,128)(2,1)S(1)}, u32[]{:S(2)}, u32[]{:S(2)}) async-start(bf16[8,48,256]{2,1,0:T(8,128)(2,1)} %shard_map.187), calls=%async_computation | async-start | bytes 393216 | tf_op jit(solution)/shard_map/all_to_all | solution.py:267
  30.0 1.2 %copy-done.14 = bf16[2048,256]{1,0:T(8,128)(2,1)S(1)} copy-done((bf16[2048,256]{1,0:T(8,128)(2,1)S(1)}, bf16[2048,256]{1,0:T(8,128)(2,1)}, u32[]{:S(2)}) %copy-start.14) | copy-done | bytes 1048600
  31.2 0.9 %copy-done.16 = f32[2,128,32]{2,1,0:T(8,128)S(1)} copy-done((f32[2,128,32]{2,1,0:T(8,128)S(1)}, f32[2,128,32]{2,1,0:T(8,128)}, u32[]{:S(2)}) %copy-start.16) | copy-done | bytes 32792
  32.1 0.0 copy-start.15
  32.1 0.0 copy-start.17
  32.1 0.0 copy-start.18
  32.2 2.7 %shard_map.186.pre_ref = bf16[2048,256]{1,0:T(8,128)(2,1)S(1)} custom-call(bf16[2048,256]{1,0:T(8,128)(2,1)S(1)} %copy-done.14, f32[2,128,32]{2,1,0:T(8,128)S(1)} %copy-done.16), custom_call_target="tpu_custom_call" | custom-call | flops 4000000000 | bytes 2000000 | tf_op jit(solution)/shard_map/pallas_call | solution.py:271
  34.9 0.5 all-to-all-done
  35.4 0.0 copy-done
  35.4 0.0 copy-done.1
  35.4 0.0 copy-done.9
  35.4 0.0 copy-done.10
  35.4 0.0 copy-done.15
  35.4 0.0 copy-done.17
  35.4 0.0 copy-done.18
  35.4 0.0 copy-start.2
  35.5 0.0 copy-start.3
  35.5 0.0 copy-start.11
  35.5 0.0 copy-start.12
  35.5 4.2 %shard_map.188 = (bf16[1024,256]{1,0:T(8,128)(2,1)S(1)}, bf16[256,256]{1,0:T(8,128)(2,1)S(1)}) custom-call(bf16[2048,256]{1,0:T(8,128)(2,1)S(1)} %shard_map.186.pre_ref, bf16[384,256]{1,0:T(8,128)(2,1)S(1)} %bitcast.12, bf16[1024,256]{1,0:T(8,128)(2,1)S(1)} %copy-done, f32[2,128,32]{2,1,0:T(8,128)S(1)} %copy-done.17, s32[16,128]{1,0:T(8,128)S(1)} %bitcast.14, ...), custom_call_target="tpu_custom_call" | custom-call | flops 3000000000 | bytes 4000000 | tf_op jit(solution)/shard_map/pallas_call | solution.py:276
  39.7 0.0 copy-start.4
  39.7 0.0 copy-start.5
  39.7 0.0 copy-start.6
  39.7 0.0 copy-start.7
  39.7 0.0 copy-start.8
  39.8 0.0 copy-start.13
  39.8 2.1 %collective-permute-start.2 = (bf16[256,256]{1,0:T(8,128)(2,1)S(1)}, bf16[256,256]{1,0:T(8,128)(2,1)S(1)}, u32[]{:S(2)}, u32[]{:S(2)}) collective-permute-start(bf16[256,256]{1,0:T(8,128)(2,1)S(1)} %get-tuple-element.18.a_ref), channel_id=1, source_target_pairs={{0,1},{1,0},{2,3},{3,2},{4,5},{5,4},{6,7},{7,6},{8,9},{9,8},{10,11... | collective-permute-start | bytes 393224 | tf_op jit(solution)/shard_map/ppermute | solution.py:287
  41.8 1.3 %collective-permute-done.2.b_ref = bf16[256,256]{1,0:T(8,128)(2,1)S(1)} collective-permute-done((bf16[256,256]{1,0:T(8,128)(2,1)S(1)}, bf16[256,256]{1,0:T(8,128)(2,1)S(1)}, u32[]{:S(2)}, u32[]{:S(2)}) %collective-permute-start.2) | collective-permute-done | bytes 131104 | tf_op jit(solution)/shard_map/ppermute | solution.py:287
  43.2 12.5 %all_to_all.15.parts_ref = bf16[4,256,256]{2,1,0:T(8,128)(2,1)S(1)} all-to-all(bf16[4,256,256]{2,1,0:T(8,128)(2,1)S(1)} %shard_map.189), channel_id=1, replica_groups=mesh['wide'=64,'chip'=4,'core'=2] {'chip'}, dimensions={0} | all-to-all | bytes 1048576 | tf_op jit(solution)/shard_map/all_to_all | solution.py:289
  55.7 0.0 copy-done.2
  55.7 0.0 copy-done.3
  55.7 0.0 copy-done.11
  55.7 0.0 copy-done.12
  55.7 0.5 shard_map.190
  56.2 3.4 %collective-permute-start.3 = (bf16[128,256]{1,0:T(8,128)(2,1)S(1)}, bf16[128,256]{1,0:T(8,128)(2,1)S(1)}, u32[]{:S(2)}, u32[]{:S(2)}) collective-permute-start(bf16[128,256]{1,0:T(8,128)(2,1)S(1)} %get-tuple-element.20), channel_id=1, source_target_pairs={{0,8},{1,9},{2,506},{3,507},{4,20},{5,21},{6,502},{7,503},{8,16},{... | collective-permute-start | bytes 196616 | tf_op jit(solution)/shard_map/ppermute | solution.py:219
  59.6 2.8 %collective-permute-done.3.refs_0_ = bf16[128,256]{1,0:T(8,128)(2,1)S(1)} collective-permute-done((bf16[128,256]{1,0:T(8,128)(2,1)S(1)}, bf16[128,256]{1,0:T(8,128)(2,1)S(1)}, u32[]{:S(2)}, u32[]{:S(2)}) %collective-permute-start.3) | collective-permute-done | bytes 65568 | tf_op jit(solution)/shard_map/ppermute | solution.py:219
  62.4 12.4 %all_to_all.16.pieces_ref = bf16[4,128,256]{2,1,0:T(8,128)(2,1)S(1)} all-to-all(bf16[4,128,256]{2,1,0:T(8,128)(2,1)S(1)} %shard_map.191), channel_id=1, replica_groups=mesh['wide'=64,'chip'=4,'core'=2] {'chip'}, dimensions={0} | all-to-all | bytes 524288 | tf_op jit(solution)/shard_map/all_to_all | solution.py:296
  74.8 0.0 copy-done.4
  74.8 0.0 copy-done.5
  74.8 0.0 copy-done.6
  74.8 2.0 %shard_map.192 = (bf16[1024,256]{1,0:T(8,128)(2,1)}, bf16[256,256]{1,0:T(8,128)(2,1)}) custom-call(f32[192,256]{1,0:T(8,128)S(1)} %get-tuple-element.19.own_ref, bf16[4,128,256]{2,1,0:T(8,128)(2,1)S(1)} %all_to_all.16.pieces_ref, bf16[192,256]{1,0:T(8,128)(2,1)S(1)} %copy-done.8, f32[1,256]{1,0:T(1,128)S(1)} %bitcast.20, bf16[256,256]{1,0:T(8,128)(2,1)S(1)} %copy-done.4, ...), custom_call_target="tpu_custom_call" | custom-call | tf_op jit(solution)/shard_map/pallas_call | solution.py:298
  (12 shorter events, 0.1 us)
Async XLA Ops:
  1.9 18.6 %collective-permute-start.1 = (bf16[16,256]{1,0:T(8,128)(2,1)S(1)}, bf16[16,256]{1,0:T(8,128)(2,1)S(1)}, u32[]{:S(2)}, u32[]{:S(2)}) collective-permute-start(bf16[16,256]{1,0:T(8,128)(2,1)S(1)} %convolution_convert_fusion.refs_1_), channel_id=1, source_target_pairs={{0,504},{8,0},{16,8},{24,16},{32,24},{40,32},{48,40},{56,48},{64,5... | collective-permute-start | bytes 24584 | tf_op jit(solution)/shard_map/ppermute | solution.py:205
  15.5 8.9 %collective-permute-start = (bf16[16,256]{1,0:T(8,128)(2,1)S(1)}, bf16[16,256]{1,0:T(8,128)(2,1)S(1)}, u32[]{:S(2)}, u32[]{:S(2)}) collective-permute-start(bf16[16,256]{1,0:T(8,128)(2,1)S(1)} %convolution_convert_fusion.refs_1_), channel_id=1, source_target_pairs={{0,8},{8,16},{16,24},{24,32},{32,40},{40,48},{48,56},{56,64},{64,7... | collective-permute-start | bytes 24584 | tf_op jit(solution)/shard_map/ppermute | solution.py:205
  25.1 10.3 %all-to-all-start = ((bf16[8,48,256]{2,1,0:T(8,128)(2,1)}), bf16[8,48,256]{2,1,0:T(8,128)(2,1)S(1)}, u32[]{:S(2)}, u32[]{:S(2)}) async-start(bf16[8,48,256]{2,1,0:T(8,128)(2,1)} %shard_map.187), calls=%async_computation | async-start | bytes 393216 | tf_op jit(solution)/shard_map/all_to_all | solution.py:267
  30.0 1.2 %copy-start.14 = (bf16[2048,256]{1,0:T(8,128)(2,1)S(1)}, bf16[2048,256]{1,0:T(8,128)(2,1)}, u32[]{:S(2)}) copy-start(bf16[2048,256]{1,0:T(8,128)(2,1)} %get-tuple-element.14.proj_ref) | copy-start | bytes 3145732
  31.2 0.9 %copy-start.16 = (f32[2,128,32]{2,1,0:T(8,128)S(1)}, f32[2,128,32]{2,1,0:T(8,128)}, u32[]{:S(2)}) copy-start(f32[2,128,32]{2,1,0:T(8,128)} %get-tuple-element.15.cols_ref) | copy-start | bytes 98308
  32.1 3.3 %copy-start = (bf16[1024,256]{1,0:T(8,128)(2,1)S(1)}, bf16[1024,256]{1,0:T(8,128)(2,1)}, u32[]{:S(2)}) copy-start(bf16[1024,256]{1,0:T(8,128)(2,1)} %fs_ref.3) | copy-start | bytes 1572868
  32.1 3.3 %copy-start.1 = (bf16[512,256]{1,0:T(8,128)(2,1)S(1)}, bf16[512,256]{1,0:T(8,128)(2,1)}, u32[]{:S(2)}) copy-start(bf16[512,256]{1,0:T(8,128)(2,1)} %w_in_ref.3) | copy-start | bytes 786436
  32.1 3.3 %copy-start.9 = (s32[2048]{0:T(1024)S(1)}, s32[2048]{0:T(1024)}, u32[]{:S(2)}) copy-start(s32[2048]{0:T(1024)} %param.23) | copy-start | bytes 24580
  32.1 3.3 %copy-start.10 = (s32[1024]{0:T(1024)S(1)}, s32[1024]{0:T(1024)}, u32[]{:S(2)}) copy-start(s32[1024]{0:T(1024)} %param.24) | copy-start | bytes 12292
  32.1 3.3 %copy-start.15 = (bf16[256,256]{1,0:T(8,128)(2,1)S(1)}, bf16[256,256]{1,0:T(8,128)(2,1)}, u32[]{:S(2)}) copy-start(bf16[256,256]{1,0:T(8,128)(2,1)} %w_out_ref.1) | copy-start | bytes 393220
  32.1 3.3 %copy-start.17 = (f32[2,128,32]{2,1,0:T(8,128)S(1)}, f32[2,128,32]{2,1,0:T(8,128)}, u32[]{:S(2)}) copy-start(f32[2,128,32]{2,1,0:T(8,128)} %get-tuple-element.15.cols_ref) | copy-start | bytes 98308
  32.1 3.3 %copy-start.18 = (f32[256]{0:T(256)S(1)}, f32[256]{0:T(256)}, u32[]{:S(2)}) copy-start(f32[256]{0:T(256)} %param.28) | copy-start | bytes 3076
  35.4 20.2 %copy-start.2 = (bf16[256,256]{1,0:T(8,128)(2,1)S(1)}, bf16[256,256]{1,0:T(8,128)(2,1)}, u32[]{:S(2)}) copy-start(bf16[256,256]{1,0:T(8,128)(2,1)} %state_ref.1) | copy-start | bytes 393220
  35.5 20.2 %copy-start.3 = (bf16[256,256]{1,0:T(8,128)(2,1)S(1)}, bf16[256,256]{1,0:T(8,128)(2,1)}, u32[]{:S(2)}) copy-start(bf16[256,256]{1,0:T(8,128)(2,1)} %w_up_ref.1) | copy-start | bytes 393220
  35.5 20.2 %copy-start.11 = (s32[256]{0:T(256)S(1)}, s32[256]{0:T(256)}, u32[]{:S(2)}) copy-start(s32[256]{0:T(256)} %param.25) | copy-start | bytes 3076
  35.5 20.2 %copy-start.12 = (f32[256]{0:T(256)S(1)}, f32[256]{0:T(256)}, u32[]{:S(2)}) copy-start(f32[256]{0:T(256)} %param.30) | copy-start | bytes 3076
  39.7 35.1 %copy-start.4 = (bf16[256,256]{1,0:T(8,128)(2,1)S(1)}, bf16[256,256]{1,0:T(8,128)(2,1)}, u32[]{:S(2)}) copy-start(bf16[256,256]{1,0:T(8,128)(2,1)} %w1_ref.1) | copy-start | bytes 393220
  39.7 35.1 %copy-start.5 = (bf16[256,256]{1,0:T(8,128)(2,1)S(1)}, bf16[256,256]{1,0:T(8,128)(2,1)}, u32[]{:S(2)}) copy-start(bf16[256,256]{1,0:T(8,128)(2,1)} %w2_ref.1) | copy-start | bytes 393220
  39.7 35.1 %copy-start.6 = (bf16[256,256]{1,0:T(8,128)(2,1)S(1)}, bf16[256,256]{1,0:T(8,128)(2,1)}, u32[]{:S(2)}) copy-start(bf16[256,256]{1,0:T(8,128)(2,1)} %w_down_ref.1) | copy-start | bytes 393220
  39.7 35.1 %copy-start.7 = (bf16[256,256]{1,0:T(8,128)(2,1)S(1)}, bf16[256,256]{1,0:T(8,128)(2,1)}, u32[]{:S(2)}) copy-start(bf16[256,256]{1,0:T(8,128)(2,1)} %w_fine_ref.1) | copy-start | bytes 393220
  39.7 35.0 %copy-start.8 = (bf16[192,256]{1,0:T(8,128)(2,1)S(1)}, bf16[192,256]{1,0:T(8,128)(2,1)}, u32[]{:S(2)}) copy-start(bf16[192,256]{1,0:T(8,128)(2,1)} %get-tuple-element.21.l3_rows_ref) | copy-start | bytes 294916
  39.8 35.0 %copy-start.13 = (f32[256]{0:T(256)S(1)}, f32[256]{0:T(256)}, u32[]{:S(2)}) copy-start(f32[256]{0:T(256)} %param.31) | copy-start | bytes 3076
  39.8 3.4 %collective-permute-start.2 = (bf16[256,256]{1,0:T(8,128)(2,1)S(1)}, bf16[256,256]{1,0:T(8,128)(2,1)S(1)}, u32[]{:S(2)}, u32[]{:S(2)}) collective-permute-start(bf16[256,256]{1,0:T(8,128)(2,1)S(1)} %get-tuple-element.18.a_ref), channel_id=1, source_target_pairs={{0,1},{1,0},{2,3},{3,2},{4,5},{5,4},{6,7},{7,6},{8,9},{9,8},{10,11... | collective-permute-start | bytes 393224 | tf_op jit(solution)/shard_map/ppermute | solution.py:287
  56.2 6.2 %collective-permute-start.3 = (bf16[128,256]{1,0:T(8,128)(2,1)S(1)}, bf16[128,256]{1,0:T(8,128)(2,1)S(1)}, u32[]{:S(2)}, u32[]{:S(2)}) collective-permute-start(bf16[128,256]{1,0:T(8,128)(2,1)S(1)} %get-tuple-element.20), channel_id=1, source_target_pairs={{0,8},{1,9},{2,506},{3,507},{4,20},{5,21},{6,502},{7,503},{8,16},{... | collective-permute-start | bytes 196616 | tf_op jit(solution)/shard_map/ppermute | solution.py:219

commit v4 on v3

v4 whole, which is shorter than its diff:
```python
import functools

import jax
import jax.numpy as jnp
from jax import lax
from jax.experimental import pallas as pl
from jax.experimental.pallas import tpu as pltpu
from jax.sharding import PartitionSpec as P

F32 = jnp.float32
BF16 = jnp.bfloat16
LANES = 128
EDGE_BLOCK = 512


def dot(a, b):
    return jnp.dot(a, b, preferred_element_type=F32)


def rms_scale(values, gain):
    return values * lax.rsqrt(jnp.mean(values * values, axis=-1, keepdims=True) + 1e-05) * gain


def silu(x):
    half = 0.5 * x
    return half + half * jnp.tanh(half)


def column_parts(index):
    low = (index & (LANES - 1)).astype(F32)
    high = (index >> 7).astype(F32)
    return low.T, high.T


def lane_select(low_col, high_col):
    lane = lax.broadcasted_iota(jnp.int32, (LANES, LANES), 1).astype(F32)
    low = jnp.broadcast_to(low_col, (LANES, LANES))
    hot = jnp.where(low == lane, 1.0, 0.0).astype(BF16)
    high = jnp.broadcast_to(high_col, (LANES, LANES)).astype(BF16)
    return hot, high


def row_select(index_row):
    sub = lax.broadcasted_iota(jnp.int32, (LANES, LANES), 0)
    hot = jnp.where((index_row & (LANES - 1)) == sub, 1.0, 0.0).astype(BF16)
    high = jnp.broadcast_to((index_row >> 7).astype(F32), (LANES, LANES)).astype(BF16)
    return hot, high


def pick(hot, high, tile):
    return jnp.where(high == jnp.asarray(tile, BF16), hot, jnp.zeros_like(hot))


def gather_kernel(fs_ref, w_in_ref, send_ref, recv_ref, l3_hbm, pre_ref, l3_rows_ref, proj, hot, sems):
    nodes, width = fs_ref.shape
    edges = pre_ref.shape[0]
    wide = lax.axis_index("wide")
    count = lax.axis_size("wide")
    rows = l3_rows_ref.shape[0] // 3
    copies = []
    for k in range(3):
        block = lax.rem(wide + (k + count - 1), count)
        copies.append(
            pltpu.make_async_copy(
                l3_hbm.at[pl.ds(pl.multiple_of(block * rows, rows), rows)],
                l3_rows_ref.at[pl.ds(k * rows, rows)],
                sems.at[k],
            )
        )
    for copy in copies:
        copy.start()
    proj[:nodes] = dot(fs_ref[...], w_in_ref[:width]).astype(BF16)
    proj[nodes:] = dot(fs_ref[...], w_in_ref[width:]).astype(BF16)
    columns = [column_parts(send_ref[...]), column_parts(recv_ref[...])]
    for block in range(edges // EDGE_BLOCK):
        for part in range(EDGE_BLOCK // LANES):
            j = block * (EDGE_BLOCK // LANES) + part
            span = slice(j * LANES, (j + 1) * LANES)
            for side, (low, high) in enumerate(columns):
                hot_j, high_j = lane_select(low[:, j : j + 1], high[:, j : j + 1])
                for t in range(nodes // LANES):
                    start = side * nodes + t * LANES
                    hot[span, start : start + LANES] = pick(hot_j, high_j, t)
        span = slice(block * EDGE_BLOCK, (block + 1) * EDGE_BLOCK)
        pre_ref[span] = dot(hot[span], proj[...]).astype(BF16)
    for copy in copies:
        copy.wait()


def chip_rows_kernel(mine_ref, other_ref, out_ref):
    rows = mine_ref.shape[0]
    core = lax.axis_index("core")
    first = jnp.where(core == 0, mine_ref[...], other_ref[...])
    last = jnp.where(core == 0, other_ref[...], mine_ref[...])
    for k in range(out_ref.shape[0]):
        out_ref[k, :rows] = first
        out_ref[k, rows:] = last


def neighbour_kernel(pair_ref, out_ref):
    out_ref[...] = pair_ref[1 - pair_slot()]


def fine_kernel(
    pre_ref, pair_ref, far_ref, fs_ref, send_ref, recv_ref, par_ref, w_in_ref, w_out_ref, gain_ref,
    mid_ref, keep_ref, give_ref, around, hidden, hot, inc, sums,
):
    nodes, width = fs_ref.shape
    edges = pre_ref.shape[0]
    tiles = nodes // LANES
    bound = far_ref.shape[0]
    extra = 3 * bound // LANES
    slot = pair_slot()
    ahead = lax.rem(lax.axis_index("wide") + lax.axis_index("core"), 2) == 0
    near_at, far_at = jnp.where(ahead, 2 * bound, 0), jnp.where(ahead, 0, 2 * bound)
    around[pl.ds(pl.multiple_of(near_at, bound), bound)] = pair_ref[1 - slot]
    around[bound : 2 * bound] = pair_ref[slot]
    around[pl.ds(pl.multiple_of(far_at, bound), bound)] = far_ref[...]
    proj = dot(around[...], w_in_ref[:width]).astype(BF16)
    send_low, send_high = column_parts(send_ref[...])
    for block in range(edges // EDGE_BLOCK):
        for part in range(EDGE_BLOCK // LANES):
            j = block * (EDGE_BLOCK // LANES) + part
            span = slice(j * LANES, (j + 1) * LANES)
            hot_s, high_s = lane_select(send_low[:, j : j + 1], send_high[:, j : j + 1])
            for t in range(extra):
                hot[span, t * LANES : (t + 1) * LANES] = pick(hot_s, high_s, tiles + t)
            hot_r, high_r = row_select(recv_ref[j : j + 1])
            for t in range(tiles):
                inc[t * LANES : (t + 1) * LANES, span] = pick(hot_r, high_r, t)
        span = slice(block * EDGE_BLOCK, (block + 1) * EDGE_BLOCK)
        hidden[span] = silu(pre_ref[span].astype(F32) + dot(hot[span], proj)).astype(BF16)
    for block in range(nodes // EDGE_BLOCK):
        span = slice(block * EDGE_BLOCK, (block + 1) * EDGE_BLOCK)
        agg = dot(dot(inc[span], hidden[...]).astype(BF16), w_out_ref[...])
        mid_ref[span] = (fs_ref[span].astype(F32) + rms_scale(agg, gain_ref[...])).astype(BF16)
    total = jnp.zeros(sums.shape, F32)
    for j in range(tiles):
        hot_p, high_p = row_select(par_ref[j : j + 1])
        upper = jnp.concatenate(
            [pick(hot_p, high_p, t) for t in range(sums.shape[0] // LANES)], axis=0
        )
        total = total + dot(upper, mid_ref[j * LANES : (j + 1) * LANES])
    sums[...] = total
    half = keep_ref.shape[0]
    core = lax.axis_index("core")
    keep_ref[...] = sums[pl.ds(pl.multiple_of(core * half, half), half)].astype(BF16)
    give_ref[...] = sums[pl.ds(pl.multiple_of((1 - core) * half, half), half)].astype(BF16)


def add_kernel(a_ref, b_ref, out_ref):
    total = (a_ref[...].astype(F32) + b_ref[...].astype(F32)).astype(BF16)
    for k in range(out_ref.shape[0]):
        out_ref[k] = total


def level_two_kernel(parts_ref, state_ref, w_up_ref, gain_ref, out_ref):
    rows = out_ref.shape[0]
    total = parts_ref[0].astype(F32)
    for k in range(1, parts_ref.shape[0]):
        total = total + parts_ref[k].astype(F32)
    level = dot(total.astype(BF16), w_up_ref[...])
    start = pl.multiple_of(lax.axis_index("core") * rows, rows)
    state = state_ref[pl.ds(start, rows)].astype(F32)
    out_ref[...] = (state + rms_scale(level, gain_ref[...])).astype(BF16)


def coarse_parent(parent_ref, rows, level_three):
    start = (lax.axis_index("wide") - 1) * rows
    local = (parent_ref[...] - start) & (level_three - 1)
    sub = lax.broadcasted_iota(jnp.int32, (3 * rows, LANES), 0)
    return jnp.concatenate(
        [jnp.where(local[j : j + 1] == sub, 1.0, 0.0) for j in range(parent_ref.shape[0])], axis=1
    )


def window_kernel(level_three, mine_ref, other_ref, parent_ref, own_ref, pieces_ref, mid_ref, padded):
    rows = own_ref.shape[0] // 3
    core = lax.axis_index("core")
    mid = jnp.concatenate(
        [
            jnp.where(core == 0, mine_ref[...], other_ref[...]),
            jnp.where(core == 0, other_ref[...], mine_ref[...]),
        ],
        axis=0,
    )
    mid_ref[...] = mid
    own = dot(coarse_parent(parent_ref, rows, level_three).astype(BF16), mid)
    own_ref[...] = own
    padded[...] = jnp.zeros_like(padded)
    padded[rows : 4 * rows] = own.astype(BF16)
    here = quad_slot()
    for there in range(pieces_ref.shape[0]):
        step = there - here
        start = jnp.where(
            step == 1, 2, jnp.where(step == 2, 3, jnp.where(step == -1, 1, jnp.where(step == -2, 0, 5)))
        )
        start = jnp.where((core == 1) & ((here >= 2) == (there >= 2)), 5, start)
        pieces_ref[there] = padded[pl.ds(pl.multiple_of(start * rows, rows), 2 * rows)]


def collect_kernel(pieces_ref, out_ref, sums):
    rows = out_ref.shape[0] // 3
    sums[...] = jnp.zeros_like(sums)
    here = quad_slot()
    for there in range(pieces_ref.shape[0]):
        start = pl.multiple_of(jnp.where(there < here, 0, rows), rows)
        sums[pl.ds(start, 2 * rows)] += pieces_ref[there].astype(F32)
    out_ref[...] = sums[...].astype(BF16)


def down_kernel(
    level_three, own_ref, mine_ref, other_ref, l3_rows_ref, gain_ref,
    w1_ref, w2_ref, w_down_ref, w_fine_ref, parent_ref, mid_ref, par_ref, fine_ref,
    fine_out_ref, down_ref,
):
    rows = own_ref.shape[0] // 3
    total = own_ref[...] + (mine_ref[...].astype(F32) + other_ref[...].astype(F32))
    mid3 = (l3_rows_ref[...].astype(F32) + rms_scale(total, gain_ref[...])).astype(BF16)
    hidden = silu(dot(mid3, w1_ref[...])).astype(BF16)
    new = (mid3.astype(F32) + dot(hidden, w2_ref[...])).astype(BF16)
    lower = coarse_parent(parent_ref, rows, level_three).T.astype(BF16)
    picked = dot(lower, new).astype(BF16)
    down = (mid_ref[...].astype(F32) + dot(picked, w_down_ref[...])).astype(BF16)
    down_ref[...] = down
    fine = dot(down, w_fine_ref[...]).astype(BF16)
    par_low, par_high = column_parts(par_ref[...])
    for j in range(par_ref.shape[0]):
        hot, high = lane_select(par_low[:, j : j + 1], par_high[:, j : j + 1])
        lower = jnp.concatenate([pick(hot, high, t) for t in range(fine.shape[0] // LANES)], axis=1)
        span = slice(j * LANES, (j + 1) * LANES)
        fine_out_ref[span] = (fine_ref[span].astype(F32) + dot(lower, fine)).astype(BF16)


def pair_slot():
    return lax.rem(lax.axis_index("wide") + lax.axis_index("core"), 2)


def quad_slot():
    return lax.rem(lax.axis_index("wide") + 2 * lax.axis_index("core"), 4)


def device_of(wide, chip, core):
    sizes = [lax.axis_size(name) for name in ("wide", "chip", "core")]
    return (wide % sizes[0] * sizes[1] + chip) * sizes[2] + core


def exchanged(value, groups):
    return lax.all_to_all(
        value, ("wide", "chip", "core"), 0, 0, tiled=True, axis_index_groups=groups
    )


def core_swapped(value):
    return lax.ppermute(value, "core", [(0, 1), (1, 0)])


def call(kernel, out, scratch=(), vmem=24, hbm=(), nargs=0, flops=0, moved=0):
    specs = [
        pl.BlockSpec(memory_space=pltpu.HBM if k in hbm else pltpu.VMEM) for k in range(nargs)
    ]
    outs = [jax.ShapeDtypeStruct(shape, dtype) for shape, dtype in out]
    return pl.pallas_call(
        kernel,
        out_shape=outs,
        in_specs=specs,
        out_specs=[pl.BlockSpec(memory_space=pltpu.VMEM) for _ in outs],
        scratch_shapes=list(scratch),
        compiler_params=pltpu.CompilerParams(vmem_limit_bytes=vmem * 2**20),
        cost_estimate=pl.CostEstimate(flops=flops, bytes_accessed=moved, transcendentals=0),
    )


def body(
    fine_state, l2_state, l3_state, boundary, senders, receivers, up_parent, l2_parent, msg_in,
    msg_out, fine_gain, up_weight, l2_gain, l3_gain, l3_w1, l3_w2, down_weight, fine_down,
):
    nodes, width = fine_state.shape
    edges = senders.shape[0]
    level_two = l2_state.shape[0]
    level_three = l3_state.shape[0]
    wide = lax.axis_size("wide")
    rows = level_three // wide
    chips, cores = lax.axis_size("chip"), lax.axis_size("core")
    send = senders.reshape(-1, LANES)
    recv = receivers.reshape(-1, LANES)
    par = up_parent.reshape(-1, LANES)
    parent = l2_parent.reshape(-1, LANES)
    fine_gain, l2_gain, l3_gain = (g.reshape(1, width) for g in (fine_gain, l2_gain, l3_gain))

    hot = (boundary[:, None] == jnp.arange(nodes, dtype=jnp.int32)[None, :]).astype(BF16)
    exported = dot(hot, fine_state).astype(BF16)
    bound = chips * cores * boundary.shape[0]
    pairs = [
        [device_of(first + core + step, chip, core) for step in range(2) for chip in range(chips)]
        for core in range(cores)
        for first in range(0, wide, 2)
    ]
    quads = [
        [device_of(first + 2 * core + step, chip, core) for step in range(4)]
        for core in range(cores)
        for chip in range(chips)
        for first in range(0, wide, 4)
    ]

    (chip_rows,) = call(
        chip_rows_kernel, [((2 * chips, cores * boundary.shape[0], width), BF16)], nargs=2
    )(exported, core_swapped(exported))
    chip_rows, local_state = lax.optimization_barrier((chip_rows, fine_state))
    pair = exchanged(chip_rows, pairs).reshape(2, bound, width)

    pre, l3_rows = call(
        gather_kernel,
        [((edges, width), BF16), ((3 * rows, width), BF16)],
        [
            pltpu.VMEM((2 * nodes, width), BF16),
            pltpu.VMEM((edges, 2 * nodes), BF16),
            pltpu.SemaphoreType.DMA((3,)),
        ],
        hbm=(4,), nargs=5, vmem=61, flops=5_000_000_000, moved=2_000_000,
    )(local_state, msg_in, send, recv, l3_state)
    pair, pre = lax.optimization_barrier((pair, pre))
    (near,) = call(neighbour_kernel, [((bound, width), BF16)], nargs=1)(pair)
    far = core_swapped(near)

    half = level_two // 2
    fine_mid, keep, give = call(
        fine_kernel,
        [((nodes, width), BF16), ((half, width), BF16), ((half, width), BF16)],
        [
            pltpu.VMEM((3 * bound, width), BF16),
            pltpu.VMEM((edges, width), BF16),
            pltpu.VMEM((edges, 3 * bound), BF16),
            pltpu.VMEM((nodes, edges), BF16),
            pltpu.VMEM((level_two, width), F32),
        ],
        nargs=10, flops=3_000_000_000, moved=4_000_000,
    )(pre, pair, far, fine_state, send, recv, par, msg_in, msg_out, fine_gain)

    (chip_sums,) = call(add_kernel, [((chips, half, width), BF16)], nargs=2)(keep, core_swapped(give))
    chip_sums = lax.all_to_all(chip_sums, "chip", 0, 0, tiled=True)
    (half_mid,) = call(level_two_kernel, [((half, width), BF16)], nargs=4)(
        chip_sums, l2_state, up_weight, l2_gain
    )
    own, pieces, l2_mid = call(
        functools.partial(window_kernel, level_three),
        [((3 * rows, width), F32), ((4, 2 * rows, width), BF16), ((level_two, width), BF16)],
        [pltpu.VMEM((7 * rows, width), BF16)],
        nargs=3,
    )(half_mid, core_swapped(half_mid), parent)
    (mine,) = call(
        collect_kernel, [((3 * rows, width), BF16)], [pltpu.VMEM((3 * rows, width), F32)], nargs=1
    )(exchanged(pieces, quads))

    fine_out, l2_down = call(
        functools.partial(down_kernel, level_three),
        [((nodes, width), BF16), ((level_two, width), BF16)],
        nargs=13,
    )(
        own, mine, core_swapped(mine), l3_rows, l3_gain, l3_w1, l3_w2, down_weight, fine_down,
        parent, l2_mid, par, fine_mid,
    )
    return (fine_out, l2_down)


def solution(mesh):
    wide, narrow = mesh.devices.shape
    mesh = jax.sharding.Mesh(mesh.devices.reshape(wide, narrow // 2, 2), ("wide", "chip", "core"))
    every = ("wide", "chip", "core")
    return jax.shard_map(
        body,
        mesh=mesh,
        in_specs=(P(every, None), P("wide", None), P()) + (P(every),) * 4 + (P("wide"),) + (P(),) * 10,
        out_specs=(P(every, None), P("wide", None)),
        check_vma=False,
    )
```

time: 77.3 us -> 70.6 us (0.913)
  the two profiles are of different devices: /device:TPU:8 before, /device:TPU:1 now
where the time goes in v4:
time: 70.6 us; the launch traced here: 70.1 us
  starting transfers between devices  29.3 us (42%)
  blocking collectives  19.5 us (28%)
  Pallas kernels  12.9 us (18%)
  waiting for transfers between devices  4.91 us (7%)
  local copies, waits for them, and re-layouts  1.31 us (2%)
  matrix products  1.27 us (2%)
  between operations  0.89 us (1%)
    ppermute x5, starting transfers between devices, core_swapped(): return lax.ppermute(value, 'core', [(0, 1), (1, 0)])  19.1 us
    all_to_all x1, starting transfers between devices, exchanged(): lax.all_to_all(value, ('wide', 'chip', 'core'), 0, 0, tiled=True, axis_in...  10.2 us
    all_to_all x1, blocking collectives, body(): chip_sums = lax.all_to_all(chip_sums, 'chip', 0, 0, tiled=True)  10.1 us
    all_to_all x1, blocking collectives, exchanged(): lax.all_to_all(value, ('wide', 'chip', 'core'), 0, 0, tiled=True, axis_in...  9.43 us
    pallas_call x1, Pallas kernels, body(): call(gather_kernel, [((edges, width), BF16), ((3 * rows, width), BF16)],...  5.45 us
    ppermute x5, waiting for transfers between devices, core_swapped(): return lax.ppermute(value, 'core', [(0, 1), (1, 0)])  4.91 us
    pallas_call x1, Pallas kernels, body(): call(fine_kernel, [((nodes, width), BF16), ((half, width), BF16), ((half,...  4.23 us
    pallas_call x1, Pallas kernels, body(): call(functools.partial(down_kernel, level_three), [((nodes, width), BF16)...  1.97 us
  transfers between devices with their start and end apart: 6, of which 5 were waited for; matrix products, arithmetic and copies ran while one was open for 0% of the time, Pallas kernels for 8%

profile of v4, /device:TPU:1, one launch (start us, length us, event | category | flops | bytes accessed | tf_op | source)
XLA Modules:
  0.0 70.1 jit_solution(10929649874947589776)
XLA Ops:
  0.6 1.3 %convolution_convert_fusion.mine_ref = bf16[16,256]{1,0:T(8,128)(2,1)S(1)} fusion(bf16[1024,256]{1,0:T(8,128)(2,1)} %fs_ref.2, s32[16]{0:T(128)} %param.21), kind=kOutput, calls=%fused_computation | convolution fusion | flops 8409088 | bytes 532544 | tf_op jit(solution)/shard_map/dot_general | solution.py:17
  1.9 8.8 %collective-permute-start = (bf16[16,256]{1,0:T(8,128)(2,1)S(1)}, bf16[16,256]{1,0:T(8,128)(2,1)S(1)}, u32[]{:S(2)}, u32[]{:S(2)}) collective-permute-start(bf16[16,256]{1,0:T(8,128)(2,1)S(1)} %convolution_convert_fusion.mine_ref), channel_id=1, source_target_pairs={{0,1},{1,0},{2,3},{3,2},{4,5},{5,4},{6,7},{7,6},{8,9},{9,8},{10,11... | collective-permute-start | bytes 24584 | tf_op jit(solution)/shard_map/ppermute | solution.py:255
  10.7 0.8 %collective-permute-done.other_ref = bf16[16,256]{1,0:T(8,128)(2,1)S(1)} collective-permute-done((bf16[16,256]{1,0:T(8,128)(2,1)S(1)}, bf16[16,256]{1,0:T(8,128)(2,1)S(1)}, u32[]{:S(2)}, u32[]{:S(2)}) %collective-permute-start) | collective-permute-done | bytes 8224 | tf_op jit(solution)/shard_map/ppermute | solution.py:255
  11.5 0.7 shard_map.185
  12.2 10.2 %all-to-all-start = ((bf16[8,32,256]{2,1,0:T(8,128)(2,1)}), bf16[8,32,256]{2,1,0:T(8,128)(2,1)S(1)}, u32[]{:S(2)}, u32[]{:S(2)}) async-start(bf16[8,32,256]{2,1,0:T(8,128)(2,1)} %shard_map.185), calls=%async_computation | async-start | bytes 262144 | tf_op jit(solution)/shard_map/all_to_all | solution.py:249
  22.4 0.0 copy-start.13
  22.4 0.0 copy-start.14
  22.4 0.0 copy-start.15
  22.4 0.0 copy-start.16
  22.5 5.5 %shard_map.186 = (bf16[2048,256]{1,0:T(8,128)(2,1)}, bf16[192,256]{1,0:T(8,128)(2,1)}) custom-call(bf16[1024,256]{1,0:T(8,128)(2,1)} %fs_ref.2, bf16[512,256]{1,0:T(8,128)(2,1)} %w_in_ref.3, s32[16,128]{1,0:T(8,128)} %bitcast.17, s32[16,128]{1,0:T(8,128)} %bitcast.19, bf16[4096,256]{1,0:T(8,128)(2,1)} %l3_hbm.1), custom_call_target="tpu_custom_call" | custom-call | flops 5000000000 | bytes 2000000 | tf_op jit(solution)/shard_map/pallas_call | solution.py:312
  27.9 0.0 all-to-all-done
  28.0 1.9 %collective-permute-start.1 = (bf16[128,256]{1,0:T(8,128)(2,1)S(1)}, bf16[128,256]{1,0:T(8,128)(2,1)S(1)}, u32[]{:S(2)}, u32[]{:S(2)}) collective-permute-start(bf16[128,256]{1,0:T(8,128)(2,1)S(1)} %shard_map.187), channel_id=1, source_target_pairs={{0,1},{1,0},{2,3},{3,2},{4,5},{5,4},{6,7},{7,6},{8,9},{9,8},{10,11... | collective-permute-start | bytes 196616 | tf_op jit(solution)/shard_map/ppermute | solution.py:255
  29.9 1.2 %collective-permute-done.1.far_ref = bf16[128,256]{1,0:T(8,128)(2,1)S(1)} collective-permute-done((bf16[128,256]{1,0:T(8,128)(2,1)S(1)}, bf16[128,256]{1,0:T(8,128)(2,1)S(1)}, u32[]{:S(2)}, u32[]{:S(2)}) %collective-permute-start.1) | collective-permute-done | bytes 65568 | tf_op jit(solution)/shard_map/ppermute | solution.py:255
  31.1 0.0 copy-done
  31.1 0.0 copy-done.8
  31.1 0.0 copy-done.12
  31.1 0.0 copy-done.13
  31.1 0.0 copy-done.14
  31.1 0.0 copy-done.15
  31.1 0.0 copy-done.16
  31.2 0.0 copy-start.17
  31.2 1.2 %copy-done.17 = bf16[2048,256]{1,0:T(8,128)(2,1)S(1)} copy-done((bf16[2048,256]{1,0:T(8,128)(2,1)S(1)}, bf16[2048,256]{1,0:T(8,128)(2,1)}, u32[]{:S(2)}) %copy-start.17) | copy-done | bytes 1048600
  32.4 4.2 %shard_map.188 = (bf16[1024,256]{1,0:T(8,128)(2,1)S(1)}, bf16[128,256]{1,0:T(8,128)(2,1)S(1)}, bf16[128,256]{1,0:T(8,128)(2,1)S(1)}) custom-call(bf16[2048,256]{1,0:T(8,128)(2,1)S(1)} %copy-done.17, bf16[2,128,256]{2,1,0:T(8,128)(2,1)S(1)} %bitcast.10, bf16[128,256]{1,0:T(8,128)(2,1)S(1)} %collective-permute-done.1.far_ref, bf16[1024,256]{1,0:T(8,128)(2,1)S(1)} %copy-done, ...), custom_call_target="tpu_custom_call" | custom-call | flops 3000000000 | bytes 4000000 | tf_op jit(solution)/shard_map/pallas_call | solution.py:327
  36.6 0.0 copy-start.1
  36.6 0.0 copy-start.2
  36.7 0.0 copy-start.3
  36.7 0.0 copy-start.4
  36.7 0.0 copy-start.7
  36.7 0.0 copy-start.11
  36.7 2.2 %collective-permute-start.2 = (bf16[128,256]{1,0:T(8,128)(2,1)S(1)}, bf16[128,256]{1,0:T(8,128)(2,1)S(1)}, u32[]{:S(2)}, u32[]{:S(2)}) collective-permute-start(bf16[128,256]{1,0:T(8,128)(2,1)S(1)} %get-tuple-element.20), channel_id=1, source_target_pairs={{0,1},{1,0},{2,3},{3,2},{4,5},{5,4},{6,7},{7,6},{8,9},{9,8},{10,11... | collective-permute-start | bytes 196616 | tf_op jit(solution)/shard_map/ppermute | solution.py:255
  38.9 1.1 %collective-permute-done.2.b_ref = bf16[128,256]{1,0:T(8,128)(2,1)S(1)} collective-permute-done((bf16[128,256]{1,0:T(8,128)(2,1)S(1)}, bf16[128,256]{1,0:T(8,128)(2,1)S(1)}, u32[]{:S(2)}, u32[]{:S(2)}) %collective-permute-start.2) | collective-permute-done | bytes 65568 | tf_op jit(solution)/shard_map/ppermute | solution.py:255
  40.0 10.1 %all_to_all.15.parts_ref = bf16[4,128,256]{2,1,0:T(8,128)(2,1)S(1)} all-to-all(bf16[4,128,256]{2,1,0:T(8,128)(2,1)S(1)} %shard_map.189), channel_id=1, replica_groups=mesh['wide'=64,'chip'=4,'core'=2] {'chip'}, dimensions={0} | all-to-all | bytes 524288 | tf_op jit(solution)/shard_map/all_to_all | solution.py:341
  50.1 0.0 copy-done.5
  50.1 0.0 copy-done.6
  50.1 0.0 copy-done.10
  50.1 0.3 shard_map.190.mine_ref
  50.4 3.2 %collective-permute-start.3 = (bf16[128,256]{1,0:T(8,128)(2,1)S(1)}, bf16[128,256]{1,0:T(8,128)(2,1)S(1)}, u32[]{:S(2)}, u32[]{:S(2)}) collective-permute-start(bf16[128,256]{1,0:T(8,128)(2,1)S(1)} %shard_map.190.mine_ref), channel_id=1, source_target_pairs={{0,1},{1,0},{2,3},{3,2},{4,5},{5,4},{6,7},{7,6},{8,9},{9,8},{10,11... | collective-permute-start | bytes 196616 | tf_op jit(solution)/shard_map/ppermute | solution.py:255
  53.6 0.9 %collective-permute-done.3.other_ref = bf16[128,256]{1,0:T(8,128)(2,1)S(1)} collective-permute-done((bf16[128,256]{1,0:T(8,128)(2,1)S(1)}, bf16[128,256]{1,0:T(8,128)(2,1)S(1)}, u32[]{:S(2)}, u32[]{:S(2)}) %collective-permute-start.3) | collective-permute-done | bytes 65568 | tf_op jit(solution)/shard_map/ppermute | solution.py:255
  54.5 0.0 copy-done.9
  54.5 0.2 shard_map.191
  54.7 9.4 %all_to_all.16.pieces_ref = bf16[4,128,256]{2,1,0:T(8,128)(2,1)S(1)} all-to-all(bf16[4,128,256]{2,1,0:T(8,128)(2,1)S(1)} %get-tuple-element.22), channel_id=1, replica_groups={{0,8,16,24},{32,40,48,56},{64,72,80,88},{96,104,112,120},{128,136,144,1..., dimensions={0} | all-to-all | bytes 524288 | tf_op jit(solution)/shard_map/all_to_all | solution.py:249
  64.1 0.1 shard_map.192.mine_ref
  64.2 3.0 %collective-permute-start.4 = (bf16[192,256]{1,0:T(8,128)(2,1)S(1)}, bf16[192,256]{1,0:T(8,128)(2,1)S(1)}, u32[]{:S(2)}, u32[]{:S(2)}) collective-permute-start(bf16[192,256]{1,0:T(8,128)(2,1)S(1)} %shard_map.192.mine_ref), channel_id=1, source_target_pairs={{0,1},{1,0},{2,3},{3,2},{4,5},{5,4},{6,7},{7,6},{8,9},{9,8},{10,11... | collective-permute-start | bytes 294920 | tf_op jit(solution)/shard_map/ppermute | solution.py:255
  67.2 0.9 %collective-permute-done.4.other_ref = bf16[192,256]{1,0:T(8,128)(2,1)S(1)} collective-permute-done((bf16[192,256]{1,0:T(8,128)(2,1)S(1)}, bf16[192,256]{1,0:T(8,128)(2,1)S(1)}, u32[]{:S(2)}, u32[]{:S(2)}) %collective-permute-start.4) | collective-permute-done | bytes 98336 | tf_op jit(solution)/shard_map/ppermute | solution.py:255
  68.1 0.0 copy-done.1
  68.2 0.0 copy-done.2
  68.2 0.0 copy-done.4
  68.2 2.0 %shard_map.193 = (bf16[1024,256]{1,0:T(8,128)(2,1)}, bf16[256,256]{1,0:T(8,128)(2,1)}) custom-call(f32[192,256]{1,0:T(8,128)S(1)} %get-tuple-element.21.own_ref, bf16[192,256]{1,0:T(8,128)(2,1)S(1)} %shard_map.192.mine_ref, bf16[192,256]{1,0:T(8,128)(2,1)S(1)} %collective-permute-done.4.other_ref, bf16[192,256]{1,0:T(8,128)(2,1)S(1)} %copy-done.7, ...), custom_call_target="tpu_custom_call" | custom-call | tf_op jit(solution)/shard_map/pallas_call | solution.py:355
  (12 shorter events, 0.1 us)
Async XLA Ops:
  1.9 9.6 %collective-permute-start = (bf16[16,256]{1,0:T(8,128)(2,1)S(1)}, bf16[16,256]{1,0:T(8,128)(2,1)S(1)}, u32[]{:S(2)}, u32[]{:S(2)}) collective-permute-start(bf16[16,256]{1,0:T(8,128)(2,1)S(1)} %convolution_convert_fusion.mine_ref), channel_id=1, source_target_pairs={{0,1},{1,0},{2,3},{3,2},{4,5},{5,4},{6,7},{7,6},{8,9},{9,8},{10,11... | collective-permute-start | bytes 24584 | tf_op jit(solution)/shard_map/ppermute | solution.py:255
  12.2 15.7 %all-to-all-start = ((bf16[8,32,256]{2,1,0:T(8,128)(2,1)}), bf16[8,32,256]{2,1,0:T(8,128)(2,1)S(1)}, u32[]{:S(2)}, u32[]{:S(2)}) async-start(bf16[8,32,256]{2,1,0:T(8,128)(2,1)} %shard_map.185), calls=%async_computation | async-start | bytes 262144 | tf_op jit(solution)/shard_map/all_to_all | solution.py:249
  22.4 8.7 %copy-start = (bf16[1024,256]{1,0:T(8,128)(2,1)S(1)}, bf16[1024,256]{1,0:T(8,128)(2,1)}, u32[]{:S(2)}) copy-start(bf16[1024,256]{1,0:T(8,128)(2,1)} %fs_ref.2) | copy-start | bytes 1572868
  22.4 8.7 %copy-start.8 = (s32[1024]{0:T(1024)S(1)}, s32[1024]{0:T(1024)}, u32[]{:S(2)}) copy-start(s32[1024]{0:T(1024)} %param.24) | copy-start | bytes 12292
  22.4 8.7 %copy-start.12 = (bf16[512,256]{1,0:T(8,128)(2,1)S(1)}, bf16[512,256]{1,0:T(8,128)(2,1)}, u32[]{:S(2)}) copy-start(bf16[512,256]{1,0:T(8,128)(2,1)} %w_in_ref.3) | copy-start | bytes 786436
  22.4 8.7 %copy-start.13 = (bf16[256,256]{1,0:T(8,128)(2,1)S(1)}, bf16[256,256]{1,0:T(8,128)(2,1)}, u32[]{:S(2)}) copy-start(bf16[256,256]{1,0:T(8,128)(2,1)} %w_out_ref.1) | copy-start | bytes 393220
  22.4 8.7 %copy-start.14 = (s32[2048]{0:T(1024)S(1)}, s32[2048]{0:T(1024)}, u32[]{:S(2)}) copy-start(s32[2048]{0:T(1024)} %param.22) | copy-start | bytes 24580
  22.4 8.7 %copy-start.15 = (s32[2048]{0:T(1024)S(1)}, s32[2048]{0:T(1024)}, u32[]{:S(2)}) copy-start(s32[2048]{0:T(1024)} %param.23) | copy-start | bytes 24580
  22.4 8.7 %copy-start.16 = (f32[256]{0:T(256)S(1)}, f32[256]{0:T(256)}, u32[]{:S(2)}) copy-start(f32[256]{0:T(256)} %param.28) | copy-start | bytes 3076
  28.0 3.1 %collective-permute-start.1 = (bf16[128,256]{1,0:T(8,128)(2,1)S(1)}, bf16[128,256]{1,0:T(8,128)(2,1)S(1)}, u32[]{:S(2)}, u32[]{:S(2)}) collective-permute-start(bf16[128,256]{1,0:T(8,128)(2,1)S(1)} %shard_map.187), channel_id=1, source_target_pairs={{0,1},{1,0},{2,3},{3,2},{4,5},{5,4},{6,7},{7,6},{8,9},{9,8},{10,11... | collective-permute-start | bytes 196616 | tf_op jit(solution)/shard_map/ppermute | solution.py:255
  31.2 1.2 %copy-start.17 = (bf16[2048,256]{1,0:T(8,128)(2,1)S(1)}, bf16[2048,256]{1,0:T(8,128)(2,1)}, u32[]{:S(2)}) copy-start(bf16[2048,256]{1,0:T(8,128)(2,1)} %get-tuple-element.17.pre_ref) | copy-start | bytes 3145732
  32.4 17.7 %copy-start.5 = (bf16[256,256]{1,0:T(8,128)(2,1)S(1)}, bf16[256,256]{1,0:T(8,128)(2,1)}, u32[]{:S(2)}) copy-start(bf16[256,256]{1,0:T(8,128)(2,1)} %state_ref.1) | copy-start | bytes 393220
  32.4 17.7 %copy-start.6 = (bf16[256,256]{1,0:T(8,128)(2,1)S(1)}, bf16[256,256]{1,0:T(8,128)(2,1)}, u32[]{:S(2)}) copy-start(bf16[256,256]{1,0:T(8,128)(2,1)} %w_up_ref.1) | copy-start | bytes 393220
  32.4 17.7 %copy-start.10 = (f32[256]{0:T(256)S(1)}, f32[256]{0:T(256)}, u32[]{:S(2)}) copy-start(f32[256]{0:T(256)} %param.30) | copy-start | bytes 3076
  32.4 22.1 %copy-start.9 = (s32[256]{0:T(256)S(1)}, s32[256]{0:T(256)}, u32[]{:S(2)}) copy-start(s32[256]{0:T(256)} %param.25) | copy-start | bytes 3076
  36.6 31.5 %copy-start.1 = (bf16[256,256]{1,0:T(8,128)(2,1)S(1)}, bf16[256,256]{1,0:T(8,128)(2,1)}, u32[]{:S(2)}) copy-start(bf16[256,256]{1,0:T(8,128)(2,1)} %w1_ref.1) | copy-start | bytes 393220
  36.6 31.5 %copy-start.2 = (bf16[256,256]{1,0:T(8,128)(2,1)S(1)}, bf16[256,256]{1,0:T(8,128)(2,1)}, u32[]{:S(2)}) copy-start(bf16[256,256]{1,0:T(8,128)(2,1)} %w2_ref.1) | copy-start | bytes 393220
  36.7 31.5 %copy-start.3 = (bf16[256,256]{1,0:T(8,128)(2,1)S(1)}, bf16[256,256]{1,0:T(8,128)(2,1)}, u32[]{:S(2)}) copy-start(bf16[256,256]{1,0:T(8,128)(2,1)} %w_down_ref.1) | copy-start | bytes 393220
  36.7 31.5 %copy-start.4 = (bf16[256,256]{1,0:T(8,128)(2,1)S(1)}, bf16[256,256]{1,0:T(8,128)(2,1)}, u32[]{:S(2)}) copy-start(bf16[256,256]{1,0:T(8,128)(2,1)} %w_fine_ref.1) | copy-start | bytes 393220
  36.7 31.5 %copy-start.7 = (bf16[192,256]{1,0:T(8,128)(2,1)S(1)}, bf16[192,256]{1,0:T(8,128)(2,1)}, u32[]{:S(2)}) copy-start(bf16[192,256]{1,0:T(8,128)(2,1)} %get-tuple-element.23.l3_rows_ref) | copy-start | bytes 294916
  36.7 31.5 %copy-start.11 = (f32[256]{0:T(256)S(1)}, f32[256]{0:T(256)}, u32[]{:S(2)}) copy-start(f32[256]{0:T(256)} %param.31) | copy-start | bytes 3076
  36.7 3.3 %collective-permute-start.2 = (bf16[128,256]{1,0:T(8,128)(2,1)S(1)}, bf16[128,256]{1,0:T(8,128)(2,1)S(1)}, u32[]{:S(2)}, u32[]{:S(2)}) collective-permute-start(bf16[128,256]{1,0:T(8,128)(2,1)S(1)} %get-tuple-element.20), channel_id=1, source_target_pairs={{0,1},{1,0},{2,3},{3,2},{4,5},{5,4},{6,7},{7,6},{8,9},{9,8},{10,11... | collective-permute-start | bytes 196616 | tf_op jit(solution)/shard_map/ppermute | solution.py:255
  50.4 4.1 %collective-permute-start.3 = (bf16[128,256]{1,0:T(8,128)(2,1)S(1)}, bf16[128,256]{1,0:T(8,128)(2,1)S(1)}, u32[]{:S(2)}, u32[]{:S(2)}) collective-permute-start(bf16[128,256]{1,0:T(8,128)(2,1)S(1)} %shard_map.190.mine_ref), channel_id=1, source_target_pairs={{0,1},{1,0},{2,3},{3,2},{4,5},{5,4},{6,7},{7,6},{8,9},{9,8},{10,11... | collective-permute-start | bytes 196616 | tf_op jit(solution)/shard_map/ppermute | solution.py:255
  64.2 3.9 %collective-permute-start.4 = (bf16[192,256]{1,0:T(8,128)(2,1)S(1)}, bf16[192,256]{1,0:T(8,128)(2,1)S(1)}, u32[]{:S(2)}, u32[]{:S(2)}) collective-permute-start(bf16[192,256]{1,0:T(8,128)(2,1)S(1)} %shard_map.192.mine_ref), channel_id=1, source_target_pairs={{0,1},{1,0},{2,3},{3,2},{4,5},{5,4},{6,7},{7,6},{8,9},{9,8},{10,11... | collective-permute-start | bytes 294920 | tf_op jit(solution)/shard_map/ppermute | solution.py:255

commit v5 on v4

--- a/solution.py
+++ b/solution.py
@@ -51,28 +51,31 @@
     return jnp.where(high == jnp.asarray(tile, BF16), hot, jnp.zeros_like(hot))
 
 
-def gather_kernel(fs_ref, w_in_ref, send_ref, recv_ref, l3_hbm, pre_ref, l3_rows_ref, proj, hot, sems):
-    nodes, width = fs_ref.shape
-    edges = pre_ref.shape[0]
+def gather_kernel(
+    fs_hbm, w_in_hbm, send_hbm, recv_hbm, l3_hbm, pre_hbm, l3_rows_hbm,
+    fs, w_in, send, recv, proj, hot, pre, sems,
+):
+    nodes, width = fs.shape
+    edges = pre.shape[0]
     wide = lax.axis_index("wide")
     count = lax.axis_size("wide")
-    rows = l3_rows_ref.shape[0] // 3
-    copies = []
+    rows = l3_rows_hbm.shape[0] // 3
+    pairs = [(send_hbm, send), (recv_hbm, recv), (w_in_hbm, w_in), (fs_hbm, fs)]
     for k in range(3):
         block = lax.rem(wide + (k + count - 1), count)
-        copies.append(
-            pltpu.make_async_copy(
-                l3_hbm.at[pl.ds(pl.multiple_of(block * rows, rows), rows)],
-                l3_rows_ref.at[pl.ds(k * rows, rows)],
-                sems.at[k],
-            )
-        )
-    for copy in copies:
+        source = l3_hbm.at[pl.ds(pl.multiple_of(block * rows, rows), rows)]
+        pairs.append((source, l3_rows_hbm.at[pl.ds(k * rows, rows)]))
+    blocks = edges // EDGE_BLOCK
+    for block in range(blocks):
+        span = pl.ds(block * EDGE_BLOCK, EDGE_BLOCK)
+        pairs.append((pre.at[span], pre_hbm.at[span]))
+    copies = [pltpu.make_async_copy(a, b, sems.at[k]) for k, (a, b) in enumerate(pairs)]
+    for copy in copies[:7]:
         copy.start()
-    proj[:nodes] = dot(fs_ref[...], w_in_ref[:width]).astype(BF16)
-    proj[nodes:] = dot(fs_ref[...], w_in_ref[width:]).astype(BF16)
-    columns = [column_parts(send_ref[...]), column_parts(recv_ref[...])]
-    for block in range(edges // EDGE_BLOCK):
+    copies[0].wait()
+    copies[1].wait()
+    columns = [column_parts(send[...]), column_parts(recv[...])]
+    for block in range(blocks):
         for part in range(EDGE_BLOCK // LANES):
             j = block * (EDGE_BLOCK // LANES) + part
             span = slice(j * LANES, (j + 1) * LANES)
@@ -81,9 +84,15 @@
                 for t in range(nodes // LANES):
                     start = side * nodes + t * LANES
                     hot[span, start : start + LANES] = pick(hot_j, high_j, t)
+        if block == 0:
+            copies[2].wait()
+            copies[3].wait()
+            proj[:nodes] = dot(fs[...], w_in[:width]).astype(BF16)
+            proj[nodes:] = dot(fs[...], w_in[width:]).astype(BF16)
         span = slice(block * EDGE_BLOCK, (block + 1) * EDGE_BLOCK)
-        pre_ref[span] = dot(hot[span], proj[...]).astype(BF16)
-    for copy in copies:
+        pre[span] = dot(hot[span], proj[...]).astype(BF16)
+        copies[7 + block].start()
+    for copy in copies[4:]:
         copy.wait()
 
 
@@ -101,15 +110,27 @@
     out_ref[...] = pair_ref[1 - pair_slot()]
 
 
+def prepare_kernel(send_ref, recv_ref, hot_ref, inc_ref):
+    tiles = inc_ref.shape[0] // LANES
+    low, high = column_parts(send_ref[...])
+    for j in range(send_ref.shape[0]):
+        span = slice(j * LANES, (j + 1) * LANES)
+        hot_s, high_s = lane_select(low[:, j : j + 1], high[:, j : j + 1])
+        for t in range(hot_ref.shape[1] // LANES):
+            hot_ref[span, t * LANES : (t + 1) * LANES] = pick(hot_s, high_s, tiles + t)
+        hot_r, high_r = row_select(recv_ref[j : j + 1])
+        for t in range(tiles):
+            inc_ref[t * LANES : (t + 1) * LANES, span] = pick(hot_r, high_r, t)
+
+
 def fine_kernel(
-    pre_ref, pair_ref, far_ref, fs_ref, send_ref, recv_ref, par_ref, w_in_ref, w_out_ref, gain_ref,
-    mid_ref, keep_ref, give_ref, around, hidden, hot, inc, sums,
+    pre_ref, pair_ref, far_ref, fs_ref, hot_ref, inc_ref, par_ref, w_in_ref, w_out_ref, gain_ref,
+    mid_ref, part_ref, around, hidden,
 ):
     nodes, width = fs_ref.shape
     edges = pre_ref.shape[0]
     tiles = nodes // LANES
     bound = far_ref.shape[0]
-    extra = 3 * bound // LANES
     slot = pair_slot()
     ahead = lax.rem(lax.axis_index("wide") + lax.axis_index("core"), 2) == 0
     near_at, far_at = jnp.where(ahead, 2 * bound, 0), jnp.where(ahead, 0, 2 * bound)
@@ -117,52 +138,40 @@
     around[bound : 2 * bound] = pair_ref[slot]
     around[pl.ds(pl.multiple_of(far_at, bound), bound)] = far_ref[...]
     proj = dot(around[...], w_in_ref[:width]).astype(BF16)
-    send_low, send_high = column_parts(send_ref[...])
     for block in range(edges // EDGE_BLOCK):
-        for part in range(EDGE_BLOCK // LANES):
-            j = block * (EDGE_BLOCK // LANES) + part
-            span = slice(j * LANES, (j + 1) * LANES)
-            hot_s, high_s = lane_select(send_low[:, j : j + 1], send_high[:, j : j + 1])
-            for t in range(extra):
-                hot[span, t * LANES : (t + 1) * LANES] = pick(hot_s, high_s, tiles + t)
-            hot_r, high_r = row_select(recv_ref[j : j + 1])
-            for t in range(tiles):
-                inc[t * LANES : (t + 1) * LANES, span] = pick(hot_r, high_r, t)
         span = slice(block * EDGE_BLOCK, (block + 1) * EDGE_BLOCK)
-        hidden[span] = silu(pre_ref[span].astype(F32) + dot(hot[span], proj)).astype(BF16)
+        hidden[span] = silu(pre_ref[span].astype(F32) + dot(hot_ref[span], proj)).astype(BF16)
     for block in range(nodes // EDGE_BLOCK):
         span = slice(block * EDGE_BLOCK, (block + 1) * EDGE_BLOCK)
-        agg = dot(dot(inc[span], hidden[...]).astype(BF16), w_out_ref[...])
+        agg = dot(dot(inc_ref[span], hidden[...]).astype(BF16), w_out_ref[...])
         mid_ref[span] = (fs_ref[span].astype(F32) + rms_scale(agg, gain_ref[...])).astype(BF16)
-    total = jnp.zeros(sums.shape, F32)
+    cores, half, _ = part_ref.shape
+    total = jnp.zeros((cores * half, width), F32)
     for j in range(tiles):
         hot_p, high_p = row_select(par_ref[j : j + 1])
-        upper = jnp.concatenate(
-            [pick(hot_p, high_p, t) for t in range(sums.shape[0] // LANES)], axis=0
-        )
+        upper = jnp.concatenate([pick(hot_p, high_p, t) for t in range(cores * half // LANES)], axis=0)
         total = total + dot(upper, mid_ref[j * LANES : (j + 1) * LANES])
-    sums[...] = total
-    half = keep_ref.shape[0]
-    core = lax.axis_index("core")
-    keep_ref[...] = sums[pl.ds(pl.multiple_of(core * half, half), half)].astype(BF16)
-    give_ref[...] = sums[pl.ds(pl.multiple_of((1 - core) * half, half), half)].astype(BF16)
-
-
-def add_kernel(a_ref, b_ref, out_ref):
-    total = (a_ref[...].astype(F32) + b_ref[...].astype(F32)).astype(BF16)
+    for core in range(cores):
+        part_ref[core] = total[core * half : (core + 1) * half].astype(BF16)
+
+
+def add_kernel(parts_ref, out_ref):
+    total = (parts_ref[0].astype(F32) + parts_ref[1].astype(F32)).astype(BF16)
     for k in range(out_ref.shape[0]):
         out_ref[k] = total
 
 
 def level_two_kernel(parts_ref, state_ref, w_up_ref, gain_ref, out_ref):
-    rows = out_ref.shape[0]
+    rows = out_ref.shape[1]
     total = parts_ref[0].astype(F32)
     for k in range(1, parts_ref.shape[0]):
         total = total + parts_ref[k].astype(F32)
     level = dot(total.astype(BF16), w_up_ref[...])
     start = pl.multiple_of(lax.axis_index("core") * rows, rows)
     state = state_ref[pl.ds(start, rows)].astype(F32)
-    out_ref[...] = (state + rms_scale(level, gain_ref[...])).astype(BF16)
+    mid = (state + rms_scale(level, gain_ref[...])).astype(BF16)
+    for k in range(out_ref.shape[0]):
+        out_ref[k] = mid
 
 
 def coarse_parent(parent_ref, rows, level_three):
@@ -174,18 +183,10 @@
     )
 
 
-def window_kernel(level_three, mine_ref, other_ref, parent_ref, own_ref, pieces_ref, mid_ref, padded):
+def window_kernel(level_three, mid_ref, parent_ref, own_ref, pieces_ref, padded):
     rows = own_ref.shape[0] // 3
     core = lax.axis_index("core")
-    mid = jnp.concatenate(
-        [
-            jnp.where(core == 0, mine_ref[...], other_ref[...]),
-            jnp.where(core == 0, other_ref[...], mine_ref[...]),
-        ],
-        axis=0,
-    )
-    mid_ref[...] = mid
-    own = dot(coarse_parent(parent_ref, rows, level_three).astype(BF16), mid)
+    own = dot(coarse_parent(parent_ref, rows, level_three).astype(BF16), mid_ref[...])
     own_ref[...] = own
     padded[...] = jnp.zeros_like(padded)
     padded[rows : 4 * rows] = own.astype(BF16)
@@ -200,22 +201,23 @@
 
 
 def collect_kernel(pieces_ref, out_ref, sums):
-    rows = out_ref.shape[0] // 3
+    rows = out_ref.shape[1] // 3
     sums[...] = jnp.zeros_like(sums)
     here = quad_slot()
     for there in range(pieces_ref.shape[0]):
         start = pl.multiple_of(jnp.where(there < here, 0, rows), rows)
         sums[pl.ds(start, 2 * rows)] += pieces_ref[there].astype(F32)
-    out_ref[...] = sums[...].astype(BF16)
+    for k in range(out_ref.shape[0]):
+        out_ref[k] = sums[...].astype(BF16)
 
 
 def down_kernel(
-    level_three, own_ref, mine_ref, other_ref, l3_rows_ref, gain_ref,
+    level_three, own_ref, sums_ref, l3_rows_ref, gain_ref,
     w1_ref, w2_ref, w_down_ref, w_fine_ref, parent_ref, mid_ref, par_ref, fine_ref,
     fine_out_ref, down_ref,
 ):
     rows = own_ref.shape[0] // 3
-    total = own_ref[...] + (mine_ref[...].astype(F32) + other_ref[...].astype(F32))
+    total = own_ref[...] + (sums_ref[0].astype(F32) + sums_ref[1].astype(F32))
     mid3 = (l3_rows_ref[...].astype(F32) + rms_scale(total, gain_ref[...])).astype(BF16)
     hidden = silu(dot(mid3, w1_ref[...])).astype(BF16)
     new = (mid3.astype(F32) + dot(hidden, w2_ref[...])).astype(BF16)
@@ -251,20 +253,24 @@
     )
 
 
+def between_cores(value):
+    return lax.all_to_all(value, "core", 0, 0, tiled=True)
+
+
 def core_swapped(value):
     return lax.ppermute(value, "core", [(0, 1), (1, 0)])
 
 
-def call(kernel, out, scratch=(), vmem=24, hbm=(), nargs=0, flops=0, moved=0):
+def call(kernel, out, scratch=(), vmem=24, hbm=(), hbm_outs=False, nargs=0, flops=0, moved=0):
     specs = [
-        pl.BlockSpec(memory_space=pltpu.HBM if k in hbm else pltpu.VMEM) for k in range(nargs)
+        pl.BlockSpec(memory_space=pl.ANY if k in hbm else pltpu.VMEM) for k in range(nargs)
     ]
     outs = [jax.ShapeDtypeStruct(shape, dtype) for shape, dtype in out]
     return pl.pallas_call(
         kernel,
         out_shape=outs,
         in_specs=specs,
-        out_specs=[pl.BlockSpec(memory_space=pltpu.VMEM) for _ in outs],
+        out_specs=[pl.BlockSpec(memory_space=pl.ANY if hbm_outs else pltpu.VMEM) for _ in outs],
         scratch_shapes=list(scratch),
         compiler_params=pltpu.CompilerParams(vmem_limit_bytes=vmem * 2**20),
         cost_estimate=pl.CostEstimate(flops=flops, bytes_accessed=moved, transcendentals=0),
@@ -313,51 +319,58 @@
         gather_kernel,
         [((edges, width), BF16), ((3 * rows, width), BF16)],
         [
+            pltpu.VMEM((nodes, width), BF16),
+            pltpu.VMEM((2 * width, width), BF16),
+            pltpu.VMEM(send.shape, jnp.int32),
+            pltpu.VMEM(recv.shape, jnp.int32),
             pltpu.VMEM((2 * nodes, width), BF16),
             pltpu.VMEM((edges, 2 * nodes), BF16),
-            pltpu.SemaphoreType.DMA((3,)),
+            pltpu.VMEM((edges, width), BF16),
+            pltpu.SemaphoreType.DMA((7 + edges // EDGE_BLOCK,)),
         ],
-        hbm=(4,), nargs=5, vmem=61, flops=5_000_000_000, moved=2_000_000,
+        hbm=range(5), hbm_outs=True, nargs=5, vmem=60, flops=5_000_000_000, moved=2_000_000,
     )(local_state, msg_in, send, recv, l3_state)
     pair, pre = lax.optimization_barrier((pair, pre))
     (near,) = call(neighbour_kernel, [((bound, width), BF16)], nargs=1)(pair)
     far = core_swapped(near)
-
-    half = level_two // 2
-    fine_mid, keep, give = call(
+    near, send_late = lax.optimization_barrier((near, send))
+    hot, incidence = call(
+        prepare_kernel, [((edges, 3 * bound), BF16), ((nodes, edges), BF16)],
+        nargs=2, flops=1_000_000_000, moved=6_000_000,
+    )(send_late, recv)
+    far, hot, incidence = lax.optimization_barrier((far, hot, incidence))
+
+    half = level_two // cores
+    fine_mid, part = call(
         fine_kernel,
-        [((nodes, width), BF16), ((half, width), BF16), ((half, width), BF16)],
-        [
-            pltpu.VMEM((3 * bound, width), BF16),
-            pltpu.VMEM((edges, width), BF16),
-            pltpu.VMEM((edges, 3 * bound), BF16),
-            pltpu.VMEM((nodes, edges), BF16),
-            pltpu.VMEM((level_two, width), F32),
-        ],
+        [((nodes, width), BF16), ((cores, half, width), BF16)],
+        [pltpu.VMEM((3 * bound, width), BF16), pltpu.VMEM((edges, width), BF16)],
         nargs=10, flops=3_000_000_000, moved=4_000_000,
-    )(pre, pair, far, fine_state, send, recv, par, msg_in, msg_out, fine_gain)
-
-    (chip_sums,) = call(add_kernel, [((chips, half, width), BF16)], nargs=2)(keep, core_swapped(give))
+    )(pre, pair, far, fine_state, hot, incidence, par, msg_in, msg_out, fine_gain)
+
+    (chip_sums,) = call(add_kernel, [((chips, half, width), BF16)], nargs=1)(between_cores(part))
     chip_sums = lax.all_to_all(chip_sums, "chip", 0, 0, tiled=True)
-    (half_mid,) = call(level_two_kernel, [((half, width), BF16)], nargs=4)(
+    (half_mid,) = call(level_two_kernel, [((cores, half, width), BF16)], nargs=4)(
         chip_sums, l2_state, up_weight, l2_gain
     )
-    own, pieces, l2_mid = call(
+    l2_mid = between_cores(half_mid).reshape(level_two, width)
+    own, pieces = call(
         functools.partial(window_kernel, level_three),
-        [((3 * rows, width), F32), ((4, 2 * rows, width), BF16), ((level_two, width), BF16)],
+        [((3 * rows, width), F32), ((4, 2 * rows, width), BF16)],
         [pltpu.VMEM((7 * rows, width), BF16)],
-        nargs=3,
-    )(half_mid, core_swapped(half_mid), parent)
-    (mine,) = call(
-        collect_kernel, [((3 * rows, width), BF16)], [pltpu.VMEM((3 * rows, width), F32)], nargs=1
+        nargs=2,
+    )(l2_mid, parent)
+    (sums,) = call(
+        collect_kernel, [((cores, 3 * rows, width), BF16)], [pltpu.VMEM((3 * rows, width), F32)],
+        nargs=1,
     )(exchanged(pieces, quads))
 
     fine_out, l2_down = call(
         functools.partial(down_kernel, level_three),
         [((nodes, width), BF16), ((level_two, width), BF16)],
-        nargs=13,
+        nargs=12,
     )(
-        own, mine, core_swapped(mine), l3_rows, l3_gain, l3_w1, l3_w2, down_weight, fine_down,
+        own, between_cores(sums), l3_rows, l3_gain, l3_w1, l3_w2, down_weight, fine_down,
         parent, l2_mid, par, fine_mid,
     )
     return (fine_out, l2_down)

time: 70.6 us -> 71.7 us (1.016)
  blocking collectives: 19.5 us -> 33 us
  starting transfers between devices: 29.3 us -> 21.1 us
  waiting for transfers between devices: 4.91 us -> 0.81 us
  local copies, waits for them, and re-layouts: 1.31 us -> 0.11 us
  Pallas kernels: 12.9 us -> 14 us
    all_to_all x0 -> x3, blocking collectives: none -> 14 us  [between_cores(): return lax.all_to_all(value, 'core', 0, 0, tiled=True)]
    ppermute x5 -> x2, starting transfers between devices: 19.1 us -> 10.8 us  [core_swapped(): return lax.ppermute(value, 'core', [(0, 1), (1, 0)])]
    ppermute x5 -> x2, waiting for transfers between devices: 4.91 us -> 0.81 us  [core_swapped(): return lax.ppermute(value, 'core', [(0, 1), (1, 0)])]
    pallas_call x4 -> x5, Pallas kernels: 4.59 us -> 5.8 us  [the longest x1 3.77 us: body(): call(fine_kernel, [((nodes, width), BF16), ((cores, half, width), BF16)],...]
    unnamed x36, local copies, waits for them, and re-layouts: 1.31 us -> 0.11 us
  transfers between devices with their start and end apart: 6 -> 3, of which waited for: 5 -> 1; matrix products, arithmetic and copies ran while one was open for 0% -> 0% of each run, Pallas kernels for 8% -> 10%
where the time goes in v5:
time: 71.7 us; the launch traced here: 71.2 us
  blocking collectives  33 us (46%)
  starting transfers between devices  21.1 us (29%)
  Pallas kernels  14 us (20%)
  matrix products  1.27 us (2%)
  between operations  0.94 us (1%)
  waiting for transfers between devices  0.81 us (1%)
    all_to_all x3, blocking collectives, between_cores(): return lax.all_to_all(value, 'core', 0, 0, tiled=True)  14 us
    ppermute x2, starting transfers between devices, core_swapped(): return lax.ppermute(value, 'core', [(0, 1), (1, 0)])  10.8 us
    all_to_all x1, starting transfers between devices, exchanged(): lax.all_to_all(value, ('wide', 'chip', 'core'), 0, 0, tiled=True, axis_in...  10.2 us
    all_to_all x1, blocking collectives, body(): chip_sums = lax.all_to_all(chip_sums, 'chip', 0, 0, tiled=True)  9.58 us
    all_to_all x1, blocking collectives, exchanged(): lax.all_to_all(value, ('wide', 'chip', 'core'), 0, 0, tiled=True, axis_in...  9.43 us
    pallas_call x1, Pallas kernels, body(): call(gather_kernel, [((edges, width), BF16), ((3 * rows, width), BF16)],...  5.32 us
    pallas_call x1, Pallas kernels, body(): call(fine_kernel, [((nodes, width), BF16), ((cores, half, width), BF16)],...  3.77 us
    pallas_call x1, Pallas kernels, body(): call(functools.partial(down_kernel, level_three), [((nodes, width), BF16)...  1.96 us
  transfers between devices with their start and end apart: 3, of which 1 were waited for; matrix products, arithmetic and copies ran while one was open for 0% of the time, Pallas kernels for 10%

profile of v5, /device:TPU:1, one launch (start us, length us, event | category | flops | bytes accessed | tf_op | source)
XLA Modules:
  0.0 71.2 jit_solution(5265489938051154357)
XLA Ops:
  0.6 1.3 %convolution_convert_fusion.mine_ref = bf16[16,256]{1,0:T(8,128)(2,1)S(1)} fusion(bf16[1024,256]{1,0:T(8,128)(2,1)} %fs_ref.1, s32[16]{0:T(128)} %param.21), kind=kOutput, calls=%fused_computation | convolution fusion | flops 8409088 | bytes 532544 | tf_op jit(solution)/shard_map/dot_general | solution.py:17
  1.9 8.8 %collective-permute-start = (bf16[16,256]{1,0:T(8,128)(2,1)S(1)}, bf16[16,256]{1,0:T(8,128)(2,1)S(1)}, u32[]{:S(2)}, u32[]{:S(2)}) collective-permute-start(bf16[16,256]{1,0:T(8,128)(2,1)S(1)} %convolution_convert_fusion.mine_ref), channel_id=1, source_target_pairs={{0,1},{1,0},{2,3},{3,2},{4,5},{5,4},{6,7},{7,6},{8,9},{9,8},{10,11... | collective-permute-start | bytes 24584 | tf_op jit(solution)/shard_map/ppermute | solution.py:261
  10.7 0.8 %collective-permute-done.other_ref = bf16[16,256]{1,0:T(8,128)(2,1)S(1)} collective-permute-done((bf16[16,256]{1,0:T(8,128)(2,1)S(1)}, bf16[16,256]{1,0:T(8,128)(2,1)S(1)}, u32[]{:S(2)}, u32[]{:S(2)}) %collective-permute-start) | collective-permute-done | bytes 8224 | tf_op jit(solution)/shard_map/ppermute | solution.py:261
  11.5 0.7 shard_map.185
  12.2 10.2 %all-to-all-start = ((bf16[8,32,256]{2,1,0:T(8,128)(2,1)}), bf16[8,32,256]{2,1,0:T(8,128)(2,1)S(1)}, u32[]{:S(2)}, u32[]{:S(2)}) async-start(bf16[8,32,256]{2,1,0:T(8,128)(2,1)} %shard_map.185), calls=%async_computation | async-start | bytes 262144 | tf_op jit(solution)/shard_map/all_to_all | solution.py:251
  22.4 5.3 %shard_map.186 = (bf16[2048,256]{1,0:T(8,128)(2,1)}, bf16[192,256]{1,0:T(8,128)(2,1)}) custom-call(bf16[1024,256]{1,0:T(8,128)(2,1)} %fs_ref.1, bf16[512,256]{1,0:T(8,128)(2,1)} %w_in_ref.1, s32[16,128]{1,0:T(8,128)} %bitcast.20, s32[16,128]{1,0:T(8,128)} %bitcast.22, bf16[4096,256]{1,0:T(8,128)(2,1)} %l3_hbm.1), custom_call_target="tpu_custom_call" | custom-call | flops 5000000000 | bytes 2000000 | tf_op jit(solution)/shard_map/pallas_call | solution.py:318
  27.7 0.0 copy-start
  27.7 0.0 copy-start.8
  27.7 0.0 copy-start.12
  27.8 0.0 copy-start.13
  27.8 0.0 copy-start.16
  27.8 0.0 copy-start.17
  27.8 0.0 all-to-all-done
  27.8 2.1 %collective-permute-start.1 = (bf16[128,256]{1,0:T(8,128)(2,1)S(1)}, bf16[128,256]{1,0:T(8,128)(2,1)S(1)}, u32[]{:S(2)}, u32[]{:S(2)}) collective-permute-start(bf16[128,256]{1,0:T(8,128)(2,1)S(1)} %shard_map.187), channel_id=1, source_target_pairs={{0,1},{1,0},{2,3},{3,2},{4,5},{5,4},{6,7},{7,6},{8,9},{9,8},{10,11... | collective-permute-start | bytes 196616 | tf_op jit(solution)/shard_map/ppermute | solution.py:261
  29.9 0.0 copy-done.14
  29.9 0.0 copy-done.15
  29.9 1.7 %shard_map.188 = (bf16[2048,384]{1,0:T(8,128)(2,1)S(1)}, bf16[1024,2048]{1,0:T(8,128)(2,1)S(1)}) custom-call(s32[16,128]{1,0:T(8,128)S(1)} %bitcast.21, s32[16,128]{1,0:T(8,128)S(1)} %bitcast.23), custom_call_target="tpu_custom_call" | custom-call | flops 1000000000 | bytes 6000000 | tf_op jit(solution)/shard_map/pallas_call | solution.py:337
  31.6 0.0 collective-permute-done.1.far_ref
  31.6 0.0 copy-done
  31.6 0.0 copy-done.8
  31.6 0.0 copy-done.12
  31.6 0.0 copy-done.13
  31.6 0.0 copy-done.16
  31.6 0.0 copy-done.17
  31.7 0.0 copy-start.1
  31.7 0.0 copy-start.2
  31.7 0.0 copy-start.10
  31.7 3.8 %shard_map.189 = (bf16[1024,256]{1,0:T(8,128)(2,1)S(1)}, bf16[2,128,256]{2,1,0:T(8,128)(2,1)S(1)}) custom-call(bf16[2048,256]{1,0:T(8,128)(2,1)S(1)} %copy-done.17, bf16[2,128,256]{2,1,0:T(8,128)(2,1)S(1)} %bitcast.13, bf16[128,256]{1,0:T(8,128)(2,1)S(1)} %collective-permute-done.1.far_ref, bf16[1024,256]{1,0:T(8,128)(2,1)S(1)} %copy-done, ...), custom_call_target="tpu_custom_call" | custom-call | flops 3000000000 | bytes 4000000 | tf_op jit(solution)/shard_map/pallas_call | solution.py:344
  35.5 0.0 copy-start.9
  35.5 0.0 copy-start.3
  35.5 0.0 copy-start.4
  35.5 0.0 copy-start.5
  35.5 0.0 copy-start.6
  35.5 0.0 copy-start.7
  35.5 0.0 copy-start.11
  35.6 4.1 %all_to_all.30.parts_ref = bf16[2,128,256]{2,1,0:T(8,128)(2,1)S(1)} all-to-all(bf16[2,128,256]{2,1,0:T(8,128)(2,1)S(1)} %get-tuple-element.29), channel_id=1, replica_groups=mesh['wide'=64,'chip'=4,'core'=2] {'core'}, dimensions={0} | all-to-all | bytes 262144 | tf_op jit(solution)/shard_map/all_to_all | solution.py:257
  39.7 9.6 %all_to_all.31.parts_ref = bf16[4,128,256]{2,1,0:T(8,128)(2,1)S(1)} all-to-all(bf16[4,128,256]{2,1,0:T(8,128)(2,1)S(1)} %shard_map.190), channel_id=1, replica_groups=mesh['wide'=64,'chip'=4,'core'=2] {'chip'}, dimensions={0} | all-to-all | bytes 524288 | tf_op jit(solution)/shard_map/all_to_all | solution.py:352
  49.3 0.0 copy-done.1
  49.3 0.0 copy-done.2
  49.3 0.3 shard_map.191
  49.6 5.3 %all_to_all.32 = bf16[2,128,256]{2,1,0:T(8,128)(2,1)S(1)} all-to-all(bf16[2,128,256]{2,1,0:T(8,128)(2,1)S(1)} %shard_map.191), channel_id=1, replica_groups=mesh['wide'=64,'chip'=4,'core'=2] {'core'}, dimensions={0} | all-to-all | bytes 262144 | tf_op jit(solution)/shard_map/all_to_all | solution.py:257
  54.8 0.2 shard_map.192
  55.1 9.4 %all_to_all.33.pieces_ref = bf16[4,128,256]{2,1,0:T(8,128)(2,1)S(1)} all-to-all(bf16[4,128,256]{2,1,0:T(8,128)(2,1)S(1)} %get-tuple-element.31), channel_id=1, replica_groups={{0,8,16,24},{32,40,48,56},{64,72,80,88},{96,104,112,120},{128,136,144,1..., dimensions={0} | all-to-all | bytes 524288 | tf_op jit(solution)/shard_map/all_to_all | solution.py:251
  64.5 0.1 shard_map.193
  64.6 4.6 %all_to_all.34.sums_ref = bf16[2,192,256]{2,1,0:T(8,128)(2,1)S(1)} all-to-all(bf16[2,192,256]{2,1,0:T(8,128)(2,1)S(1)} %shard_map.193), channel_id=1, replica_groups=mesh['wide'=64,'chip'=4,'core'=2] {'core'}, dimensions={0} | all-to-all | bytes 393216 | tf_op jit(solution)/shard_map/all_to_all | solution.py:257
  69.2 0.0 copy-done.3
  69.2 0.0 copy-done.5
  69.2 2.0 %shard_map.194 = (bf16[1024,256]{1,0:T(8,128)(2,1)}, bf16[256,256]{1,0:T(8,128)(2,1)}) custom-call(f32[192,256]{1,0:T(8,128)S(1)} %get-tuple-element.30.own_ref, bf16[2,192,256]{2,1,0:T(8,128)(2,1)S(1)} %all_to_all.34.sums_ref, bf16[192,256]{1,0:T(8,128)(2,1)S(1)} %copy-done.7, f32[1,256]{1,0:T(1,128)S(1)} %bitcast.19, bf16[256,256]{1,0:T(8,128)(2,1)S(1)} %copy-done.3, ...), custom_call_target="tpu_custom_call" | custom-call | tf_op jit(solution)/shard_map/pallas_call | solution.py:368
  (10 shorter events, 0.1 us)
Async XLA Ops:
  1.9 9.6 %collective-permute-start = (bf16[16,256]{1,0:T(8,128)(2,1)S(1)}, bf16[16,256]{1,0:T(8,128)(2,1)S(1)}, u32[]{:S(2)}, u32[]{:S(2)}) collective-permute-start(bf16[16,256]{1,0:T(8,128)(2,1)S(1)} %convolution_convert_fusion.mine_ref), channel_id=1, source_target_pairs={{0,1},{1,0},{2,3},{3,2},{4,5},{5,4},{6,7},{7,6},{8,9},{9,8},{10,11... | collective-permute-start | bytes 24584 | tf_op jit(solution)/shard_map/ppermute | solution.py:261
  12.2 15.6 %all-to-all-start = ((bf16[8,32,256]{2,1,0:T(8,128)(2,1)}), bf16[8,32,256]{2,1,0:T(8,128)(2,1)S(1)}, u32[]{:S(2)}, u32[]{:S(2)}) async-start(bf16[8,32,256]{2,1,0:T(8,128)(2,1)} %shard_map.185), calls=%async_computation | async-start | bytes 262144 | tf_op jit(solution)/shard_map/all_to_all | solution.py:251
  22.4 7.5 %copy-start.14 = (s32[2048]{0:T(1024)S(1)}, s32[2048]{0:T(1024)}, u32[]{:S(2)}) copy-start(s32[2048]{0:T(1024)} %param.22) | copy-start | bytes 24580
  22.4 7.5 %copy-start.15 = (s32[2048]{0:T(1024)S(1)}, s32[2048]{0:T(1024)}, u32[]{:S(2)}) copy-start(s32[2048]{0:T(1024)} %param.23) | copy-start | bytes 24580
  27.7 3.9 %copy-start = (bf16[1024,256]{1,0:T(8,128)(2,1)S(1)}, bf16[1024,256]{1,0:T(8,128)(2,1)}, u32[]{:S(2)}) copy-start(bf16[1024,256]{1,0:T(8,128)(2,1)} %fs_ref.1) | copy-start | bytes 1572868
  27.7 3.9 %copy-start.8 = (s32[1024]{0:T(1024)S(1)}, s32[1024]{0:T(1024)}, u32[]{:S(2)}) copy-start(s32[1024]{0:T(1024)} %param.24) | copy-start | bytes 12292
  27.7 3.9 %copy-start.12 = (bf16[512,256]{1,0:T(8,128)(2,1)S(1)}, bf16[512,256]{1,0:T(8,128)(2,1)}, u32[]{:S(2)}) copy-start(bf16[512,256]{1,0:T(8,128)(2,1)} %w_in_ref.1) | copy-start | bytes 786436
  27.8 3.9 %copy-start.13 = (bf16[256,256]{1,0:T(8,128)(2,1)S(1)}, bf16[256,256]{1,0:T(8,128)(2,1)}, u32[]{:S(2)}) copy-start(bf16[256,256]{1,0:T(8,128)(2,1)} %w_out_ref.1) | copy-start | bytes 393220
  27.8 3.9 %copy-start.16 = (f32[256]{0:T(256)S(1)}, f32[256]{0:T(256)}, u32[]{:S(2)}) copy-start(f32[256]{0:T(256)} %param.28) | copy-start | bytes 3076
  27.8 3.9 %copy-start.17 = (bf16[2048,256]{1,0:T(8,128)(2,1)S(1)}, bf16[2048,256]{1,0:T(8,128)(2,1)}, u32[]{:S(2)}) copy-start(bf16[2048,256]{1,0:T(8,128)(2,1)} %get-tuple-element.21.pre_ref) | copy-start | bytes 3145732
  27.8 3.8 %collective-permute-start.1 = (bf16[128,256]{1,0:T(8,128)(2,1)S(1)}, bf16[128,256]{1,0:T(8,128)(2,1)S(1)}, u32[]{:S(2)}, u32[]{:S(2)}) collective-permute-start(bf16[128,256]{1,0:T(8,128)(2,1)S(1)} %shard_map.187), channel_id=1, source_target_pairs={{0,1},{1,0},{2,3},{3,2},{4,5},{5,4},{6,7},{7,6},{8,9},{9,8},{10,11... | collective-permute-start | bytes 196616 | tf_op jit(solution)/shard_map/ppermute | solution.py:261
  31.7 17.6 %copy-start.1 = (bf16[256,256]{1,0:T(8,128)(2,1)S(1)}, bf16[256,256]{1,0:T(8,128)(2,1)}, u32[]{:S(2)}) copy-start(bf16[256,256]{1,0:T(8,128)(2,1)} %state_ref.1) | copy-start | bytes 393220
  31.7 17.6 %copy-start.2 = (bf16[256,256]{1,0:T(8,128)(2,1)S(1)}, bf16[256,256]{1,0:T(8,128)(2,1)}, u32[]{:S(2)}) copy-start(bf16[256,256]{1,0:T(8,128)(2,1)} %w_up_ref.1) | copy-start | bytes 393220
  31.7 17.6 %copy-start.10 = (f32[256]{0:T(256)S(1)}, f32[256]{0:T(256)}, u32[]{:S(2)}) copy-start(f32[256]{0:T(256)} %param.30) | copy-start | bytes 3076
  35.5 19.4 %copy-start.9 = (s32[256]{0:T(256)S(1)}, s32[256]{0:T(256)}, u32[]{:S(2)}) copy-start(s32[256]{0:T(256)} %param.25) | copy-start | bytes 3076
  35.5 33.7 %copy-start.3 = (bf16[256,256]{1,0:T(8,128)(2,1)S(1)}, bf16[256,256]{1,0:T(8,128)(2,1)}, u32[]{:S(2)}) copy-start(bf16[256,256]{1,0:T(8,128)(2,1)} %w1_ref.1) | copy-start | bytes 393220
  35.5 33.7 %copy-start.4 = (bf16[256,256]{1,0:T(8,128)(2,1)S(1)}, bf16[256,256]{1,0:T(8,128)(2,1)}, u32[]{:S(2)}) copy-start(bf16[256,256]{1,0:T(8,128)(2,1)} %w2_ref.1) | copy-start | bytes 393220
  35.5 33.7 %copy-start.5 = (bf16[256,256]{1,0:T(8,128)(2,1)S(1)}, bf16[256,256]{1,0:T(8,128)(2,1)}, u32[]{:S(2)}) copy-start(bf16[256,256]{1,0:T(8,128)(2,1)} %w_down_ref.1) | copy-start | bytes 393220
  35.5 33.7 %copy-start.6 = (bf16[256,256]{1,0:T(8,128)(2,1)S(1)}, bf16[256,256]{1,0:T(8,128)(2,1)}, u32[]{:S(2)}) copy-start(bf16[256,256]{1,0:T(8,128)(2,1)} %w_fine_ref.1) | copy-start | bytes 393220
  35.5 33.7 %copy-start.7 = (bf16[192,256]{1,0:T(8,128)(2,1)S(1)}, bf16[192,256]{1,0:T(8,128)(2,1)}, u32[]{:S(2)}) copy-start(bf16[192,256]{1,0:T(8,128)(2,1)} %get-tuple-element.32.l3_rows_ref) | copy-start | bytes 294916
  35.5 33.7 %copy-start.11 = (f32[256]{0:T(256)S(1)}, f32[256]{0:T(256)}, u32[]{:S(2)}) copy-start(f32[256]{0:T(256)} %param.31) | copy-start | bytes 3076

commit v6 on v5

--- a/solution.py
+++ b/solution.py
@@ -125,7 +125,7 @@
 
 def fine_kernel(
     pre_ref, pair_ref, far_ref, fs_ref, hot_ref, inc_ref, par_ref, w_in_ref, w_out_ref, gain_ref,
-    mid_ref, part_ref, around, hidden,
+    mid_ref, keep_ref, give_ref, around, hidden, sums,
 ):
     nodes, width = fs_ref.shape
     edges = pre_ref.shape[0]
@@ -145,33 +145,35 @@
         span = slice(block * EDGE_BLOCK, (block + 1) * EDGE_BLOCK)
         agg = dot(dot(inc_ref[span], hidden[...]).astype(BF16), w_out_ref[...])
         mid_ref[span] = (fs_ref[span].astype(F32) + rms_scale(agg, gain_ref[...])).astype(BF16)
-    cores, half, _ = part_ref.shape
-    total = jnp.zeros((cores * half, width), F32)
+    total = jnp.zeros(sums.shape, F32)
     for j in range(tiles):
         hot_p, high_p = row_select(par_ref[j : j + 1])
-        upper = jnp.concatenate([pick(hot_p, high_p, t) for t in range(cores * half // LANES)], axis=0)
+        upper = jnp.concatenate(
+            [pick(hot_p, high_p, t) for t in range(sums.shape[0] // LANES)], axis=0
+        )
         total = total + dot(upper, mid_ref[j * LANES : (j + 1) * LANES])
-    for core in range(cores):
-        part_ref[core] = total[core * half : (core + 1) * half].astype(BF16)
-
-
-def add_kernel(parts_ref, out_ref):
-    total = (parts_ref[0].astype(F32) + parts_ref[1].astype(F32)).astype(BF16)
+    sums[...] = total
+    half = keep_ref.shape[0]
+    core = lax.axis_index("core")
+    keep_ref[...] = sums[pl.ds(pl.multiple_of(core * half, half), half)].astype(BF16)
+    give_ref[...] = sums[pl.ds(pl.multiple_of((1 - core) * half, half), half)].astype(BF16)
+
+
+def add_kernel(a_ref, b_ref, out_ref):
+    total = (a_ref[...].astype(F32) + b_ref[...].astype(F32)).astype(BF16)
     for k in range(out_ref.shape[0]):
         out_ref[k] = total
 
 
 def level_two_kernel(parts_ref, state_ref, w_up_ref, gain_ref, out_ref):
-    rows = out_ref.shape[1]
+    rows = out_ref.shape[0]
     total = parts_ref[0].astype(F32)
     for k in range(1, parts_ref.shape[0]):
         total = total + parts_ref[k].astype(F32)
     level = dot(total.astype(BF16), w_up_ref[...])
     start = pl.multiple_of(lax.axis_index("core") * rows, rows)
     state = state_ref[pl.ds(start, rows)].astype(F32)
-    mid = (state + rms_scale(level, gain_ref[...])).astype(BF16)
-    for k in range(out_ref.shape[0]):
-        out_ref[k] = mid
+    out_ref[...] = (state + rms_scale(level, gain_ref[...])).astype(BF16)
 
 
 def coarse_parent(parent_ref, rows, level_three):
@@ -183,10 +185,18 @@
     )
 
 
-def window_kernel(level_three, mid_ref, parent_ref, own_ref, pieces_ref, padded):
+def window_kernel(level_three, mine_ref, other_ref, parent_ref, own_ref, pieces_ref, mid_ref, padded):
     rows = own_ref.shape[0] // 3
     core = lax.axis_index("core")
-    own = dot(coarse_parent(parent_ref, rows, level_three).astype(BF16), mid_ref[...])
+    mid = jnp.concatenate(
+        [
+            jnp.where(core == 0, mine_ref[...], other_ref[...]),
+            jnp.where(core == 0, other_ref[...], mine_ref[...]),
+        ],
+        axis=0,
+    )
+    mid_ref[...] = mid
+    own = dot(coarse_parent(parent_ref, rows, level_three).astype(BF16), mid)
     own_ref[...] = own
     padded[...] = jnp.zeros_like(padded)
     padded[rows : 4 * rows] = own.astype(BF16)
@@ -201,23 +211,22 @@
 
 
 def collect_kernel(pieces_ref, out_ref, sums):
-    rows = out_ref.shape[1] // 3
+    rows = out_ref.shape[0] // 3
     sums[...] = jnp.zeros_like(sums)
     here = quad_slot()
     for there in range(pieces_ref.shape[0]):
         start = pl.multiple_of(jnp.where(there < here, 0, rows), rows)
         sums[pl.ds(start, 2 * rows)] += pieces_ref[there].astype(F32)
-    for k in range(out_ref.shape[0]):
-        out_ref[k] = sums[...].astype(BF16)
+    out_ref[...] = sums[...].astype(BF16)
 
 
 def down_kernel(
-    level_three, own_ref, sums_ref, l3_rows_ref, gain_ref,
+    level_three, own_ref, mine_ref, other_ref, l3_rows_ref, gain_ref,
     w1_ref, w2_ref, w_down_ref, w_fine_ref, parent_ref, mid_ref, par_ref, fine_ref,
     fine_out_ref, down_ref,
 ):
     rows = own_ref.shape[0] // 3
-    total = own_ref[...] + (sums_ref[0].astype(F32) + sums_ref[1].astype(F32))
+    total = own_ref[...] + (mine_ref[...].astype(F32) + other_ref[...].astype(F32))
     mid3 = (l3_rows_ref[...].astype(F32) + rms_scale(total, gain_ref[...])).astype(BF16)
     hidden = silu(dot(mid3, w1_ref[...])).astype(BF16)
     new = (mid3.astype(F32) + dot(hidden, w2_ref[...])).astype(BF16)
@@ -251,10 +260,6 @@
     return lax.all_to_all(
         value, ("wide", "chip", "core"), 0, 0, tiled=True, axis_index_groups=groups
     )
-
-
-def between_cores(value):
-    return lax.all_to_all(value, "core", 0, 0, tiled=True)
 
 
 def core_swapped(value):
@@ -341,36 +346,38 @@
     far, hot, incidence = lax.optimization_barrier((far, hot, incidence))
 
     half = level_two // cores
-    fine_mid, part = call(
+    fine_mid, keep, give = call(
         fine_kernel,
-        [((nodes, width), BF16), ((cores, half, width), BF16)],
-        [pltpu.VMEM((3 * bound, width), BF16), pltpu.VMEM((edges, width), BF16)],
+        [((nodes, width), BF16), ((half, width), BF16), ((half, width), BF16)],
+        [
+            pltpu.VMEM((3 * bound, width), BF16),
+            pltpu.VMEM((edges, width), BF16),
+            pltpu.VMEM((level_two, width), F32),
+        ],
         nargs=10, flops=3_000_000_000, moved=4_000_000,
     )(pre, pair, far, fine_state, hot, incidence, par, msg_in, msg_out, fine_gain)
 
-    (chip_sums,) = call(add_kernel, [((chips, half, width), BF16)], nargs=1)(between_cores(part))
+    (chip_sums,) = call(add_kernel, [((chips, half, width), BF16)], nargs=2)(keep, core_swapped(give))
     chip_sums = lax.all_to_all(chip_sums, "chip", 0, 0, tiled=True)
-    (half_mid,) = call(level_two_kernel, [((cores, half, width), BF16)], nargs=4)(
+    (half_mid,) = call(level_two_kernel, [((half, width), BF16)], nargs=4)(
         chip_sums, l2_state, up_weight, l2_gain
     )
-    l2_mid = between_cores(half_mid).reshape(level_two, width)
-    own, pieces = call(
+    own, pieces, l2_mid = call(
         functools.partial(window_kernel, level_three),
-        [((3 * rows, width), F32), ((4, 2 * rows, width), BF16)],
+        [((3 * rows, width), F32), ((4, 2 * rows, width), BF16), ((level_two, width), BF16)],
         [pltpu.VMEM((7 * rows, width), BF16)],
-        nargs=2,
-    )(l2_mid, parent)
-    (sums,) = call(
-        collect_kernel, [((cores, 3 * rows, width), BF16)], [pltpu.VMEM((3 * rows, width), F32)],
-        nargs=1,
+        nargs=3,
+    )(half_mid, core_swapped(half_mid), parent)
+    (mine,) = call(
+        collect_kernel, [((3 * rows, width), BF16)], [pltpu.VMEM((3 * rows, width), F32)], nargs=1
     )(exchanged(pieces, quads))
 
     fine_out, l2_down = call(
         functools.partial(down_kernel, level_three),
         [((nodes, width), BF16), ((level_two, width), BF16)],
-        nargs=12,
+        nargs=13,
     )(
-        own, between_cores(sums), l3_rows, l3_gain, l3_w1, l3_w2, down_weight, fine_down,
+        own, mine, core_swapped(mine), l3_rows, l3_gain, l3_w1, l3_w2, down_weight, fine_down,
         parent, l2_mid, par, fine_mid,
     )
     return (fine_out, l2_down)

time: 71.7 us -> 69.6 us (0.971)
  blocking collectives: 33 us -> 19 us
  starting transfers between devices: 21.1 us -> 30.3 us
  waiting for transfers between devices: 0.81 us -> 3.49 us
    all_to_all x3 -> x0, blocking collectives: 14 us -> none  [between_cores(): return lax.all_to_all(value, 'core', 0, 0, tiled=True)]
    ppermute x2 -> x5, starting transfers between devices: 10.8 us -> 20.1 us  [core_swapped(): return lax.ppermute(value, 'core', [(0, 1), (1, 0)])]
    ppermute x2 -> x5, waiting for transfers between devices: 0.81 us -> 3.49 us  [core_swapped(): return lax.ppermute(value, 'core', [(0, 1), (1, 0)])]
  transfers between devices with their start and end apart: 3 -> 6, of which waited for: 1 -> 4; matrix products, arithmetic and copies ran while one was open for 0% -> 0% of each run, Pallas kernels for 10% -> 10%
where the time goes in v6:
time: 69.6 us; the launch traced here: 69.2 us
  starting transfers between devices  30.3 us (44%)
  blocking collectives  19 us (27%)
  Pallas kernels  14 us (20%)
  waiting for transfers between devices  3.49 us (5%)
  matrix products  1.27 us (2%)
  between operations  0.96 us (1%)
    ppermute x5, starting transfers between devices, core_swapped(): return lax.ppermute(value, 'core', [(0, 1), (1, 0)])  20.1 us
    all_to_all x1, starting transfers between devices, exchanged(): lax.all_to_all(value, ('wide', 'chip', 'core'), 0, 0, tiled=True, axis_in...  10.2 us
    all_to_all x1, blocking collectives, body(): chip_sums = lax.all_to_all(chip_sums, 'chip', 0, 0, tiled=True)  9.58 us
    all_to_all x1, blocking collectives, exchanged(): lax.all_to_all(value, ('wide', 'chip', 'core'), 0, 0, tiled=True, axis_in...  9.43 us
    pallas_call x1, Pallas kernels, body(): call(gather_kernel, [((edges, width), BF16), ((3 * rows, width), BF16)],...  5.34 us
    pallas_call x1, Pallas kernels, body(): call(fine_kernel, [((nodes, width), BF16), ((half, width), BF16), ((half,...  3.82 us
    ppermute x5, waiting for transfers between devices, core_swapped(): return lax.ppermute(value, 'core', [(0, 1), (1, 0)])  3.49 us
    pallas_call x1, Pallas kernels, body(): call(functools.partial(down_kernel, level_three), [((nodes, width), BF16)...  1.97 us
  transfers between devices with their start and end apart: 6, of which 4 were waited for; matrix products, arithmetic and copies ran while one was open for 0% of the time, Pallas kernels for 10%

profile of v6, /device:TPU:1, one launch (start us, length us, event | category | flops | bytes accessed | tf_op | source)
XLA Modules:
  0.0 69.2 jit_solution(15725250703409302889)
XLA Ops:
  0.6 1.3 %convolution_convert_fusion.mine_ref = bf16[16,256]{1,0:T(8,128)(2,1)S(1)} fusion(bf16[1024,256]{1,0:T(8,128)(2,1)} %fs_ref.1, s32[16]{0:T(128)} %param.21), kind=kOutput, calls=%fused_computation | convolution fusion | flops 8409088 | bytes 532544 | tf_op jit(solution)/shard_map/dot_general | solution.py:17
  1.9 8.8 %collective-permute-start = (bf16[16,256]{1,0:T(8,128)(2,1)S(1)}, bf16[16,256]{1,0:T(8,128)(2,1)S(1)}, u32[]{:S(2)}, u32[]{:S(2)}) collective-permute-start(bf16[16,256]{1,0:T(8,128)(2,1)S(1)} %convolution_convert_fusion.mine_ref), channel_id=1, source_target_pairs={{0,1},{1,0},{2,3},{3,2},{4,5},{5,4},{6,7},{7,6},{8,9},{9,8},{10,11... | collective-permute-start | bytes 24584 | tf_op jit(solution)/shard_map/ppermute | solution.py:266
  10.7 0.8 %collective-permute-done.other_ref = bf16[16,256]{1,0:T(8,128)(2,1)S(1)} collective-permute-done((bf16[16,256]{1,0:T(8,128)(2,1)S(1)}, bf16[16,256]{1,0:T(8,128)(2,1)S(1)}, u32[]{:S(2)}, u32[]{:S(2)}) %collective-permute-start) | collective-permute-done | bytes 8224 | tf_op jit(solution)/shard_map/ppermute | solution.py:266
  11.5 0.7 shard_map.185
  12.2 10.2 %all-to-all-start = ((bf16[8,32,256]{2,1,0:T(8,128)(2,1)}), bf16[8,32,256]{2,1,0:T(8,128)(2,1)S(1)}, u32[]{:S(2)}, u32[]{:S(2)}) async-start(bf16[8,32,256]{2,1,0:T(8,128)(2,1)} %shard_map.185), calls=%async_computation | async-start | bytes 262144 | tf_op jit(solution)/shard_map/all_to_all | solution.py:260
  22.4 5.3 %shard_map.186 = (bf16[2048,256]{1,0:T(8,128)(2,1)}, bf16[192,256]{1,0:T(8,128)(2,1)}) custom-call(bf16[1024,256]{1,0:T(8,128)(2,1)} %fs_ref.1, bf16[512,256]{1,0:T(8,128)(2,1)} %w_in_ref.1, s32[16,128]{1,0:T(8,128)} %bitcast.17, s32[16,128]{1,0:T(8,128)} %bitcast.19, bf16[4096,256]{1,0:T(8,128)(2,1)} %l3_hbm.1), custom_call_target="tpu_custom_call" | custom-call | flops 5000000000 | bytes 2000000 | tf_op jit(solution)/shard_map/pallas_call | solution.py:323
  27.7 0.0 copy-start
  27.8 0.0 copy-start.8
  27.8 0.0 copy-start.12
  27.8 0.0 copy-start.13
  27.8 0.0 copy-start.16
  27.8 0.0 copy-start.17
  27.8 0.0 all-to-all-done
  27.8 2.1 %collective-permute-start.1 = (bf16[128,256]{1,0:T(8,128)(2,1)S(1)}, bf16[128,256]{1,0:T(8,128)(2,1)S(1)}, u32[]{:S(2)}, u32[]{:S(2)}) collective-permute-start(bf16[128,256]{1,0:T(8,128)(2,1)S(1)} %shard_map.187), channel_id=1, source_target_pairs={{0,1},{1,0},{2,3},{3,2},{4,5},{5,4},{6,7},{7,6},{8,9},{9,8},{10,11... | collective-permute-start | bytes 196616 | tf_op jit(solution)/shard_map/ppermute | solution.py:266
  29.9 0.0 copy-done.14
  29.9 0.0 copy-done.15
  29.9 1.7 %shard_map.188 = (bf16[2048,384]{1,0:T(8,128)(2,1)S(1)}, bf16[1024,2048]{1,0:T(8,128)(2,1)S(1)}) custom-call(s32[16,128]{1,0:T(8,128)S(1)} %bitcast.18, s32[16,128]{1,0:T(8,128)S(1)} %bitcast.20), custom_call_target="tpu_custom_call" | custom-call | flops 1000000000 | bytes 6000000 | tf_op jit(solution)/shard_map/pallas_call | solution.py:342
  31.6 0.0 collective-permute-done.1.far_ref
  31.6 0.0 copy-done
  31.6 0.0 copy-done.8
  31.6 0.0 copy-done.12
  31.6 0.0 copy-done.13
  31.7 0.0 copy-start.5
  31.7 0.0 copy-start.6
  31.7 0.0 copy-start.10
  31.7 0.0 copy-start.9
  31.7 3.8 %shard_map.189 = (bf16[1024,256]{1,0:T(8,128)(2,1)S(1)}, bf16[128,256]{1,0:T(8,128)(2,1)S(1)}, bf16[128,256]{1,0:T(8,128)(2,1)S(1)}) custom-call(bf16[2048,256]{1,0:T(8,128)(2,1)S(1)} %copy-done.17, bf16[2,128,256]{2,1,0:T(8,128)(2,1)S(1)} %bitcast.10, bf16[128,256]{1,0:T(8,128)(2,1)S(1)} %collective-permute-done.1.far_ref, bf16[1024,256]{1,0:T(8,128)(2,1)S(1)} %copy-done, ...), custom_call_target="tpu_custom_call" | custom-call | flops 3000000000 | bytes 4000000 | tf_op jit(solution)/shard_map/pallas_call | solution.py:349
  35.5 0.0 copy-start.1
  35.6 0.0 copy-start.2
  35.6 0.0 copy-start.3
  35.6 0.0 copy-start.4
  35.6 0.0 copy-start.7
  35.6 0.0 copy-start.11
  35.6 2.5 %collective-permute-start.2 = (bf16[128,256]{1,0:T(8,128)(2,1)S(1)}, bf16[128,256]{1,0:T(8,128)(2,1)S(1)}, u32[]{:S(2)}, u32[]{:S(2)}) collective-permute-start(bf16[128,256]{1,0:T(8,128)(2,1)S(1)} %get-tuple-element.32), channel_id=1, source_target_pairs={{0,1},{1,0},{2,3},{3,2},{4,5},{5,4},{6,7},{7,6},{8,9},{9,8},{10,11... | collective-permute-start | bytes 196616 | tf_op jit(solution)/shard_map/ppermute | solution.py:266
  38.2 0.9 %collective-permute-done.2.b_ref = bf16[128,256]{1,0:T(8,128)(2,1)S(1)} collective-permute-done((bf16[128,256]{1,0:T(8,128)(2,1)S(1)}, bf16[128,256]{1,0:T(8,128)(2,1)S(1)}, u32[]{:S(2)}, u32[]{:S(2)}) %collective-permute-start.2) | collective-permute-done | bytes 65568 | tf_op jit(solution)/shard_map/ppermute | solution.py:266
  39.1 9.6 %all_to_all.15.parts_ref = bf16[4,128,256]{2,1,0:T(8,128)(2,1)S(1)} all-to-all(bf16[4,128,256]{2,1,0:T(8,128)(2,1)S(1)} %shard_map.190), channel_id=1, replica_groups=mesh['wide'=64,'chip'=4,'core'=2] {'chip'}, dimensions={0} | all-to-all | bytes 524288 | tf_op jit(solution)/shard_map/all_to_all | solution.py:361
  48.7 0.0 copy-done.5
  48.7 0.0 copy-done.10
  48.7 0.3 shard_map.191.mine_ref
  48.9 3.7 %collective-permute-start.3 = (bf16[128,256]{1,0:T(8,128)(2,1)S(1)}, bf16[128,256]{1,0:T(8,128)(2,1)S(1)}, u32[]{:S(2)}, u32[]{:S(2)}) collective-permute-start(bf16[128,256]{1,0:T(8,128)(2,1)S(1)} %shard_map.191.mine_ref), channel_id=1, source_target_pairs={{0,1},{1,0},{2,3},{3,2},{4,5},{5,4},{6,7},{7,6},{8,9},{9,8},{10,11... | collective-permute-start | bytes 196616 | tf_op jit(solution)/shard_map/ppermute | solution.py:266
  52.6 0.9 %collective-permute-done.3.other_ref = bf16[128,256]{1,0:T(8,128)(2,1)S(1)} collective-permute-done((bf16[128,256]{1,0:T(8,128)(2,1)S(1)}, bf16[128,256]{1,0:T(8,128)(2,1)S(1)}, u32[]{:S(2)}, u32[]{:S(2)}) %collective-permute-start.3) | collective-permute-done | bytes 65568 | tf_op jit(solution)/shard_map/ppermute | solution.py:266
  53.5 0.2 shard_map.192
  53.7 9.4 %all_to_all.16.pieces_ref = bf16[4,128,256]{2,1,0:T(8,128)(2,1)S(1)} all-to-all(bf16[4,128,256]{2,1,0:T(8,128)(2,1)S(1)} %get-tuple-element.34), channel_id=1, replica_groups={{0,8,16,24},{32,40,48,56},{64,72,80,88},{96,104,112,120},{128,136,144,1..., dimensions={0} | all-to-all | bytes 524288 | tf_op jit(solution)/shard_map/all_to_all | solution.py:260
  63.2 0.1 shard_map.193.mine_ref
  63.3 3.0 %collective-permute-start.4 = (bf16[192,256]{1,0:T(8,128)(2,1)S(1)}, bf16[192,256]{1,0:T(8,128)(2,1)S(1)}, u32[]{:S(2)}, u32[]{:S(2)}) collective-permute-start(bf16[192,256]{1,0:T(8,128)(2,1)S(1)} %shard_map.193.mine_ref), channel_id=1, source_target_pairs={{0,1},{1,0},{2,3},{3,2},{4,5},{5,4},{6,7},{7,6},{8,9},{9,8},{10,11... | collective-permute-start | bytes 294920 | tf_op jit(solution)/shard_map/ppermute | solution.py:266
  66.3 0.9 %collective-permute-done.4.other_ref = bf16[192,256]{1,0:T(8,128)(2,1)S(1)} collective-permute-done((bf16[192,256]{1,0:T(8,128)(2,1)S(1)}, bf16[192,256]{1,0:T(8,128)(2,1)S(1)}, u32[]{:S(2)}, u32[]{:S(2)}) %collective-permute-start.4) | collective-permute-done | bytes 98336 | tf_op jit(solution)/shard_map/ppermute | solution.py:266
  67.2 0.0 copy-done.2
  67.2 2.0 %shard_map.194 = (bf16[1024,256]{1,0:T(8,128)(2,1)}, bf16[256,256]{1,0:T(8,128)(2,1)}) custom-call(f32[192,256]{1,0:T(8,128)S(1)} %get-tuple-element.33.own_ref, bf16[192,256]{1,0:T(8,128)(2,1)S(1)} %shard_map.193.mine_ref, bf16[192,256]{1,0:T(8,128)(2,1)S(1)} %collective-permute-done.4.other_ref, bf16[192,256]{1,0:T(8,128)(2,1)S(1)} %copy-done.7, ...), custom_call_target="tpu_custom_call" | custom-call | tf_op jit(solution)/shard_map/pallas_call | solution.py:375
  (13 shorter events, 0.1 us)
Async XLA Ops:
  1.9 9.6 %collective-permute-start = (bf16[16,256]{1,0:T(8,128)(2,1)S(1)}, bf16[16,256]{1,0:T(8,128)(2,1)S(1)}, u32[]{:S(2)}, u32[]{:S(2)}) collective-permute-start(bf16[16,256]{1,0:T(8,128)(2,1)S(1)} %convolution_convert_fusion.mine_ref), channel_id=1, source_target_pairs={{0,1},{1,0},{2,3},{3,2},{4,5},{5,4},{6,7},{7,6},{8,9},{9,8},{10,11... | collective-permute-start | bytes 24584 | tf_op jit(solution)/shard_map/ppermute | solution.py:266
  12.2 15.6 %all-to-all-start = ((bf16[8,32,256]{2,1,0:T(8,128)(2,1)}), bf16[8,32,256]{2,1,0:T(8,128)(2,1)S(1)}, u32[]{:S(2)}, u32[]{:S(2)}) async-start(bf16[8,32,256]{2,1,0:T(8,128)(2,1)} %shard_map.185), calls=%async_computation | async-start | bytes 262144 | tf_op jit(solution)/shard_map/all_to_all | solution.py:260
  22.4 7.5 %copy-start.14 = (s32[2048]{0:T(1024)S(1)}, s32[2048]{0:T(1024)}, u32[]{:S(2)}) copy-start(s32[2048]{0:T(1024)} %param.22) | copy-start | bytes 24580
  22.4 7.5 %copy-start.15 = (s32[2048]{0:T(1024)S(1)}, s32[2048]{0:T(1024)}, u32[]{:S(2)}) copy-start(s32[2048]{0:T(1024)} %param.23) | copy-start | bytes 24580
  27.7 3.9 %copy-start = (bf16[1024,256]{1,0:T(8,128)(2,1)S(1)}, bf16[1024,256]{1,0:T(8,128)(2,1)}, u32[]{:S(2)}) copy-start(bf16[1024,256]{1,0:T(8,128)(2,1)} %fs_ref.1) | copy-start | bytes 1572868
  27.8 3.9 %copy-start.8 = (s32[1024]{0:T(1024)S(1)}, s32[1024]{0:T(1024)}, u32[]{:S(2)}) copy-start(s32[1024]{0:T(1024)} %param.24) | copy-start | bytes 12292
  27.8 3.9 %copy-start.12 = (bf16[512,256]{1,0:T(8,128)(2,1)S(1)}, bf16[512,256]{1,0:T(8,128)(2,1)}, u32[]{:S(2)}) copy-start(bf16[512,256]{1,0:T(8,128)(2,1)} %w_in_ref.1) | copy-start | bytes 786436
  27.8 3.9 %copy-start.13 = (bf16[256,256]{1,0:T(8,128)(2,1)S(1)}, bf16[256,256]{1,0:T(8,128)(2,1)}, u32[]{:S(2)}) copy-start(bf16[256,256]{1,0:T(8,128)(2,1)} %w_out_ref.1) | copy-start | bytes 393220
  27.8 3.9 %copy-start.16 = (f32[256]{0:T(256)S(1)}, f32[256]{0:T(256)}, u32[]{:S(2)}) copy-start(f32[256]{0:T(256)} %param.28) | copy-start | bytes 3076
  27.8 3.9 %copy-start.17 = (bf16[2048,256]{1,0:T(8,128)(2,1)S(1)}, bf16[2048,256]{1,0:T(8,128)(2,1)}, u32[]{:S(2)}) copy-start(bf16[2048,256]{1,0:T(8,128)(2,1)} %get-tuple-element.23.pre_ref) | copy-start | bytes 3145732
  27.8 3.8 %collective-permute-start.1 = (bf16[128,256]{1,0:T(8,128)(2,1)S(1)}, bf16[128,256]{1,0:T(8,128)(2,1)S(1)}, u32[]{:S(2)}, u32[]{:S(2)}) collective-permute-start(bf16[128,256]{1,0:T(8,128)(2,1)S(1)} %shard_map.187), channel_id=1, source_target_pairs={{0,1},{1,0},{2,3},{3,2},{4,5},{5,4},{6,7},{7,6},{8,9},{9,8},{10,11... | collective-permute-start | bytes 196616 | tf_op jit(solution)/shard_map/ppermute | solution.py:266
  31.7 17.0 %copy-start.5 = (bf16[256,256]{1,0:T(8,128)(2,1)S(1)}, bf16[256,256]{1,0:T(8,128)(2,1)}, u32[]{:S(2)}) copy-start(bf16[256,256]{1,0:T(8,128)(2,1)} %state_ref.1) | copy-start | bytes 393220
  31.7 17.0 %copy-start.6 = (bf16[256,256]{1,0:T(8,128)(2,1)S(1)}, bf16[256,256]{1,0:T(8,128)(2,1)}, u32[]{:S(2)}) copy-start(bf16[256,256]{1,0:T(8,128)(2,1)} %w_up_ref.1) | copy-start | bytes 393220
  31.7 17.0 %copy-start.10 = (f32[256]{0:T(256)S(1)}, f32[256]{0:T(256)}, u32[]{:S(2)}) copy-start(f32[256]{0:T(256)} %param.30) | copy-start | bytes 3076
  31.7 21.8 %copy-start.9 = (s32[256]{0:T(256)S(1)}, s32[256]{0:T(256)}, u32[]{:S(2)}) copy-start(s32[256]{0:T(256)} %param.25) | copy-start | bytes 3076
  35.5 31.7 %copy-start.1 = (bf16[256,256]{1,0:T(8,128)(2,1)S(1)}, bf16[256,256]{1,0:T(8,128)(2,1)}, u32[]{:S(2)}) copy-start(bf16[256,256]{1,0:T(8,128)(2,1)} %w1_ref.1) | copy-start | bytes 393220
  35.6 31.6 %copy-start.2 = (bf16[256,256]{1,0:T(8,128)(2,1)S(1)}, bf16[256,256]{1,0:T(8,128)(2,1)}, u32[]{:S(2)}) copy-start(bf16[256,256]{1,0:T(8,128)(2,1)} %w2_ref.1) | copy-start | bytes 393220
  35.6 31.6 %copy-start.3 = (bf16[256,256]{1,0:T(8,128)(2,1)S(1)}, bf16[256,256]{1,0:T(8,128)(2,1)}, u32[]{:S(2)}) copy-start(bf16[256,256]{1,0:T(8,128)(2,1)} %w_down_ref.1) | copy-start | bytes 393220
  35.6 31.6 %copy-start.4 = (bf16[256,256]{1,0:T(8,128)(2,1)S(1)}, bf16[256,256]{1,0:T(8,128)(2,1)}, u32[]{:S(2)}) copy-start(bf16[256,256]{1,0:T(8,128)(2,1)} %w_fine_ref.1) | copy-start | bytes 393220
  35.6 31.6 %copy-start.7 = (bf16[192,256]{1,0:T(8,128)(2,1)S(1)}, bf16[192,256]{1,0:T(8,128)(2,1)}, u32[]{:S(2)}) copy-start(bf16[192,256]{1,0:T(8,128)(2,1)} %get-tuple-element.35.l3_rows_ref) | copy-start | bytes 294916
  35.6 31.6 %copy-start.11 = (f32[256]{0:T(256)S(1)}, f32[256]{0:T(256)}, u32[]{:S(2)}) copy-start(f32[256]{0:T(256)} %param.31) | copy-start | bytes 3076
  35.6 3.4 %collective-permute-start.2 = (bf16[128,256]{1,0:T(8,128)(2,1)S(1)}, bf16[128,256]{1,0:T(8,128)(2,1)S(1)}, u32[]{:S(2)}, u32[]{:S(2)}) collective-permute-start(bf16[128,256]{1,0:T(8,128)(2,1)S(1)} %get-tuple-element.32), channel_id=1, source_target_pairs={{0,1},{1,0},{2,3},{3,2},{4,5},{5,4},{6,7},{7,6},{8,9},{9,8},{10,11... | collective-permute-start | bytes 196616 | tf_op jit(solution)/shard_map/ppermute | solution.py:266
  48.9 4.6 %collective-permute-start.3 = (bf16[128,256]{1,0:T(8,128)(2,1)S(1)}, bf16[128,256]{1,0:T(8,128)(2,1)S(1)}, u32[]{:S(2)}, u32[]{:S(2)}) collective-permute-start(bf16[128,256]{1,0:T(8,128)(2,1)S(1)} %shard_map.191.mine_ref), channel_id=1, source_target_pairs={{0,1},{1,0},{2,3},{3,2},{4,5},{5,4},{6,7},{7,6},{8,9},{9,8},{10,11... | collective-permute-start | bytes 196616 | tf_op jit(solution)/shard_map/ppermute | solution.py:266
  63.3 3.9 %collective-permute-start.4 = (bf16[192,256]{1,0:T(8,128)(2,1)S(1)}, bf16[192,256]{1,0:T(8,128)(2,1)S(1)}, u32[]{:S(2)}, u32[]{:S(2)}) collective-permute-start(bf16[192,256]{1,0:T(8,128)(2,1)S(1)} %shard_map.193.mine_ref), channel_id=1, source_target_pairs={{0,1},{1,0},{2,3},{3,2},{4,5},{5,4},{6,7},{7,6},{8,9},{9,8},{10,11... | collective-permute-start | bytes 294920 | tf_op jit(solution)/shard_map/ppermute | solution.py:266

commit v7 on v6

--- a/solution.py
+++ b/solution.py
@@ -125,7 +125,7 @@
 
 def fine_kernel(
     pre_ref, pair_ref, far_ref, fs_ref, hot_ref, inc_ref, par_ref, w_in_ref, w_out_ref, gain_ref,
-    mid_ref, keep_ref, give_ref, around, hidden, sums,
+    mid_ref, part_ref, around, agg, upper,
 ):
     nodes, width = fs_ref.shape
     edges = pre_ref.shape[0]
@@ -138,42 +138,28 @@
     around[bound : 2 * bound] = pair_ref[slot]
     around[pl.ds(pl.multiple_of(far_at, bound), bound)] = far_ref[...]
     proj = dot(around[...], w_in_ref[:width]).astype(BF16)
+    for j in range(tiles):
+        hot_p, high_p = row_select(par_ref[j : j + 1])
+        for t in range(upper.shape[0] // LANES):
+            upper[t * LANES : (t + 1) * LANES, j * LANES : (j + 1) * LANES] = pick(hot_p, high_p, t)
     for block in range(edges // EDGE_BLOCK):
         span = slice(block * EDGE_BLOCK, (block + 1) * EDGE_BLOCK)
-        hidden[span] = silu(pre_ref[span].astype(F32) + dot(hot_ref[span], proj)).astype(BF16)
+        hidden = silu(pre_ref[span].astype(F32) + dot(hot_ref[span], proj)).astype(BF16)
+        for part in range(nodes // EDGE_BLOCK):
+            here = slice(part * EDGE_BLOCK, (part + 1) * EDGE_BLOCK)
+            more = dot(inc_ref[here, span], hidden)
+            agg[here] = more if block == 0 else agg[here] + more
     for block in range(nodes // EDGE_BLOCK):
         span = slice(block * EDGE_BLOCK, (block + 1) * EDGE_BLOCK)
-        agg = dot(dot(inc_ref[span], hidden[...]).astype(BF16), w_out_ref[...])
-        mid_ref[span] = (fs_ref[span].astype(F32) + rms_scale(agg, gain_ref[...])).astype(BF16)
-    total = jnp.zeros(sums.shape, F32)
-    for j in range(tiles):
-        hot_p, high_p = row_select(par_ref[j : j + 1])
-        upper = jnp.concatenate(
-            [pick(hot_p, high_p, t) for t in range(sums.shape[0] // LANES)], axis=0
-        )
-        total = total + dot(upper, mid_ref[j * LANES : (j + 1) * LANES])
-    sums[...] = total
-    half = keep_ref.shape[0]
-    core = lax.axis_index("core")
-    keep_ref[...] = sums[pl.ds(pl.multiple_of(core * half, half), half)].astype(BF16)
-    give_ref[...] = sums[pl.ds(pl.multiple_of((1 - core) * half, half), half)].astype(BF16)
+        summed = dot(agg[span].astype(BF16), w_out_ref[...])
+        mid_ref[span] = (fs_ref[span].astype(F32) + rms_scale(summed, gain_ref[...])).astype(BF16)
+    part_ref[...] = dot(upper[...], mid_ref[...]).astype(BF16)
 
 
 def add_kernel(a_ref, b_ref, out_ref):
     total = (a_ref[...].astype(F32) + b_ref[...].astype(F32)).astype(BF16)
     for k in range(out_ref.shape[0]):
         out_ref[k] = total
-
-
-def level_two_kernel(parts_ref, state_ref, w_up_ref, gain_ref, out_ref):
-    rows = out_ref.shape[0]
-    total = parts_ref[0].astype(F32)
-    for k in range(1, parts_ref.shape[0]):
-        total = total + parts_ref[k].astype(F32)
-    level = dot(total.astype(BF16), w_up_ref[...])
-    start = pl.multiple_of(lax.axis_index("core") * rows, rows)
-    state = state_ref[pl.ds(start, rows)].astype(F32)
-    out_ref[...] = (state + rms_scale(level, gain_ref[...])).astype(BF16)
 
 
 def coarse_parent(parent_ref, rows, level_three):
@@ -185,16 +171,17 @@
     )
 
 
-def window_kernel(level_three, mine_ref, other_ref, parent_ref, own_ref, pieces_ref, mid_ref, padded):
+def window_kernel(
+    level_three, parts_ref, state_ref, w_up_ref, gain_ref, parent_ref,
+    own_ref, pieces_ref, mid_ref, padded,
+):
     rows = own_ref.shape[0] // 3
     core = lax.axis_index("core")
-    mid = jnp.concatenate(
-        [
-            jnp.where(core == 0, mine_ref[...], other_ref[...]),
-            jnp.where(core == 0, other_ref[...], mine_ref[...]),
-        ],
-        axis=0,
-    )
+    total = parts_ref[0].astype(F32)
+    for k in range(1, parts_ref.shape[0]):
+        total = total + parts_ref[k].astype(F32)
+    level = dot(total.astype(BF16), w_up_ref[...])
+    mid = (state_ref[...].astype(F32) + rms_scale(level, gain_ref[...])).astype(BF16)
     mid_ref[...] = mid
     own = dot(coarse_parent(parent_ref, rows, level_three).astype(BF16), mid)
     own_ref[...] = own
@@ -345,29 +332,27 @@
     )(send_late, recv)
     far, hot, incidence = lax.optimization_barrier((far, hot, incidence))
 
-    half = level_two // cores
-    fine_mid, keep, give = call(
+    fine_mid, part = call(
         fine_kernel,
-        [((nodes, width), BF16), ((half, width), BF16), ((half, width), BF16)],
+        [((nodes, width), BF16), ((level_two, width), BF16)],
         [
             pltpu.VMEM((3 * bound, width), BF16),
-            pltpu.VMEM((edges, width), BF16),
-            pltpu.VMEM((level_two, width), F32),
+            pltpu.VMEM((nodes, width), F32),
+            pltpu.VMEM((level_two, nodes), BF16),
         ],
         nargs=10, flops=3_000_000_000, moved=4_000_000,
     )(pre, pair, far, fine_state, hot, incidence, par, msg_in, msg_out, fine_gain)
 
-    (chip_sums,) = call(add_kernel, [((chips, half, width), BF16)], nargs=2)(keep, core_swapped(give))
+    (chip_sums,) = call(add_kernel, [((chips, level_two, width), BF16)], nargs=2)(
+        part, core_swapped(part)
+    )
     chip_sums = lax.all_to_all(chip_sums, "chip", 0, 0, tiled=True)
-    (half_mid,) = call(level_two_kernel, [((half, width), BF16)], nargs=4)(
-        chip_sums, l2_state, up_weight, l2_gain
-    )
     own, pieces, l2_mid = call(
         functools.partial(window_kernel, level_three),
         [((3 * rows, width), F32), ((4, 2 * rows, width), BF16), ((level_two, width), BF16)],
         [pltpu.VMEM((7 * rows, width), BF16)],
-        nargs=3,
-    )(half_mid, core_swapped(half_mid), parent)
+        nargs=5,
+    )(chip_sums, l2_state, up_weight, l2_gain, parent)
     (mine,) = call(
         collect_kernel, [((3 * rows, width), BF16)], [pltpu.VMEM((3 * rows, width), F32)], nargs=1
     )(exchanged(pieces, quads))

time: 69.6 us -> 68.1 us (0.978)
  starting transfers between devices: 30.3 us -> 27.6 us
  blocking collectives: 19 us -> 21.4 us
  waiting for transfers between devices: 3.49 us -> 2.7 us
    all_to_all x1, blocking collectives: 9.58 us -> 12.4 us  [body(): chip_sums = lax.all_to_all(chip_sums, 'chip', 0, 0, tiled=True)]
    ppermute x5 -> x4, starting transfers between devices: 20.1 us -> 17.3 us  [core_swapped(): return lax.ppermute(value, 'core', [(0, 1), (1, 0)])]
    ppermute x5 -> x4, waiting for transfers between devices: 3.49 us -> 2.7 us  [core_swapped(): return lax.ppermute(value, 'core', [(0, 1), (1, 0)])]
    pallas_call x3 -> x2, Pallas kernels: 4.1 us -> 3.48 us  [the longest x1 3.44 us: body(): call(fine_kernel, [((nodes, width), BF16), ((level_two, width), BF16)], [...]
  transfers between devices with their start and end apart: 6 -> 5, of which waited for: 4 -> 3; matrix products, arithmetic and copies ran while one was open for 0% -> 0% of each run, Pallas kernels for 10% -> 10%
where the time goes in v7:
time: 68.1 us; the launch traced here: 67.7 us
  starting transfers between devices  27.6 us (41%)
  blocking collectives  21.4 us (31%)
  Pallas kernels  13.7 us (20%)
  waiting for transfers between devices  2.7 us (4%)
  matrix products  1.27 us (2%)
  between operations  0.95 us (1%)
    ppermute x4, starting transfers between devices, core_swapped(): return lax.ppermute(value, 'core', [(0, 1), (1, 0)])  17.3 us
    all_to_all x1, blocking collectives, body(): chip_sums = lax.all_to_all(chip_sums, 'chip', 0, 0, tiled=True)  12.4 us
    all_to_all x1, starting transfers between devices, exchanged(): lax.all_to_all(value, ('wide', 'chip', 'core'), 0, 0, tiled=True, axis_in...  10.2 us
    all_to_all x1, blocking collectives, exchanged(): lax.all_to_all(value, ('wide', 'chip', 'core'), 0, 0, tiled=True, axis_in...  9.05 us
    pallas_call x1, Pallas kernels, body(): call(gather_kernel, [((edges, width), BF16), ((3 * rows, width), BF16)],...  5.33 us
    pallas_call x1, Pallas kernels, body(): call(fine_kernel, [((nodes, width), BF16), ((level_two, width), BF16)], [...  3.44 us
    ppermute x4, waiting for transfers between devices, core_swapped(): return lax.ppermute(value, 'core', [(0, 1), (1, 0)])  2.7 us
    pallas_call x1, Pallas kernels, body(): call(functools.partial(down_kernel, level_three), [((nodes, width), BF16)...  1.97 us
  transfers between devices with their start and end apart: 5, of which 3 were waited for; matrix products, arithmetic and copies ran while one was open for 0% of the time, Pallas kernels for 10%

profile of v7, /device:TPU:1, one launch (start us, length us, event | category | flops | bytes accessed | tf_op | source)
XLA Modules:
  0.0 67.7 jit_solution(2349972782652620552)
XLA Ops:
  0.6 1.3 %convolution_convert_fusion.mine_ref = bf16[16,256]{1,0:T(8,128)(2,1)S(1)} fusion(bf16[1024,256]{1,0:T(8,128)(2,1)} %fs_ref.1, s32[16]{0:T(128)} %param.21), kind=kOutput, calls=%fused_computation | convolution fusion | flops 8409088 | bytes 532544 | tf_op jit(solution)/shard_map/dot_general | solution.py:17
  1.9 8.8 %collective-permute-start = (bf16[16,256]{1,0:T(8,128)(2,1)S(1)}, bf16[16,256]{1,0:T(8,128)(2,1)S(1)}, u32[]{:S(2)}, u32[]{:S(2)}) collective-permute-start(bf16[16,256]{1,0:T(8,128)(2,1)S(1)} %convolution_convert_fusion.mine_ref), channel_id=1, source_target_pairs={{0,1},{1,0},{2,3},{3,2},{4,5},{5,4},{6,7},{7,6},{8,9},{9,8},{10,11... | collective-permute-start | bytes 24584 | tf_op jit(solution)/shard_map/ppermute | solution.py:253
  10.7 0.8 %collective-permute-done.other_ref = bf16[16,256]{1,0:T(8,128)(2,1)S(1)} collective-permute-done((bf16[16,256]{1,0:T(8,128)(2,1)S(1)}, bf16[16,256]{1,0:T(8,128)(2,1)S(1)}, u32[]{:S(2)}, u32[]{:S(2)}) %collective-permute-start) | collective-permute-done | bytes 8224 | tf_op jit(solution)/shard_map/ppermute | solution.py:253
  11.5 0.7 shard_map.185
  12.2 10.2 %all-to-all-start = ((bf16[8,32,256]{2,1,0:T(8,128)(2,1)}), bf16[8,32,256]{2,1,0:T(8,128)(2,1)S(1)}, u32[]{:S(2)}, u32[]{:S(2)}) async-start(bf16[8,32,256]{2,1,0:T(8,128)(2,1)} %shard_map.185), calls=%async_computation | async-start | bytes 262144 | tf_op jit(solution)/shard_map/all_to_all | solution.py:247
  22.4 5.3 %shard_map.186 = (bf16[2048,256]{1,0:T(8,128)(2,1)}, bf16[192,256]{1,0:T(8,128)(2,1)}) custom-call(bf16[1024,256]{1,0:T(8,128)(2,1)} %fs_ref.1, bf16[512,256]{1,0:T(8,128)(2,1)} %w_in_ref.1, s32[16,128]{1,0:T(8,128)} %bitcast.17, s32[16,128]{1,0:T(8,128)} %bitcast.19, bf16[4096,256]{1,0:T(8,128)(2,1)} %l3_hbm.1), custom_call_target="tpu_custom_call" | custom-call | flops 5000000000 | bytes 2000000 | tf_op jit(solution)/shard_map/pallas_call | solution.py:310
  27.7 0.0 copy-start
  27.7 0.0 copy-start.8
  27.8 0.0 copy-start.12
  27.8 0.0 copy-start.13
  27.8 0.0 copy-start.16
  27.8 0.0 copy-start.17
  27.8 0.0 all-to-all-done
  27.8 2.1 %collective-permute-start.1 = (bf16[128,256]{1,0:T(8,128)(2,1)S(1)}, bf16[128,256]{1,0:T(8,128)(2,1)S(1)}, u32[]{:S(2)}, u32[]{:S(2)}) collective-permute-start(bf16[128,256]{1,0:T(8,128)(2,1)S(1)} %shard_map.187), channel_id=1, source_target_pairs={{0,1},{1,0},{2,3},{3,2},{4,5},{5,4},{6,7},{7,6},{8,9},{9,8},{10,11... | collective-permute-start | bytes 196616 | tf_op jit(solution)/shard_map/ppermute | solution.py:253
  29.9 0.0 copy-done.14
  29.9 0.0 copy-done.15
  29.9 1.7 %shard_map.188 = (bf16[2048,384]{1,0:T(8,128)(2,1)S(1)}, bf16[1024,2048]{1,0:T(8,128)(2,1)S(1)}) custom-call(s32[16,128]{1,0:T(8,128)S(1)} %bitcast.18, s32[16,128]{1,0:T(8,128)S(1)} %bitcast.20), custom_call_target="tpu_custom_call" | custom-call | flops 1000000000 | bytes 6000000 | tf_op jit(solution)/shard_map/pallas_call | solution.py:329
  31.6 0.0 collective-permute-done.1.far_ref
  31.6 0.0 copy-done
  31.6 0.0 copy-done.8
  31.6 0.0 copy-done.12
  31.6 0.0 copy-done.13
  31.6 0.0 copy-done.16
  31.7 0.0 copy-done.17
  31.7 0.0 copy-start.5
  31.7 0.0 copy-start.6
  31.7 0.0 copy-start.9
  31.7 0.0 copy-start.10
  31.7 3.4 %shard_map.189 = (bf16[1024,256]{1,0:T(8,128)(2,1)S(1)}, bf16[256,256]{1,0:T(8,128)(2,1)S(1)}) custom-call(bf16[2048,256]{1,0:T(8,128)(2,1)S(1)} %copy-done.17, bf16[2,128,256]{2,1,0:T(8,128)(2,1)S(1)} %bitcast.10, bf16[128,256]{1,0:T(8,128)(2,1)S(1)} %collective-permute-done.1.far_ref, bf16[1024,256]{1,0:T(8,128)(2,1)S(1)} %copy-done, ...), custom_call_target="tpu_custom_call" | custom-call | flops 3000000000 | bytes 4000000 | tf_op jit(solution)/shard_map/pallas_call | solution.py:335
  35.2 0.0 copy-start.1
  35.2 0.0 copy-start.2
  35.2 0.0 copy-start.3
  35.2 0.0 copy-start.4
  35.2 0.0 copy-start.7
  35.2 0.0 copy-start.11
  35.2 2.5 %collective-permute-start.2 = (bf16[256,256]{1,0:T(8,128)(2,1)S(1)}, bf16[256,256]{1,0:T(8,128)(2,1)S(1)}, u32[]{:S(2)}, u32[]{:S(2)}) collective-permute-start(bf16[256,256]{1,0:T(8,128)(2,1)S(1)} %get-tuple-element.30.a_ref), channel_id=1, source_target_pairs={{0,1},{1,0},{2,3},{3,2},{4,5},{5,4},{6,7},{7,6},{8,9},{9,8},{10,11... | collective-permute-start | bytes 393224 | tf_op jit(solution)/shard_map/ppermute | solution.py:253
  37.8 1.0 %collective-permute-done.2.b_ref = bf16[256,256]{1,0:T(8,128)(2,1)S(1)} collective-permute-done((bf16[256,256]{1,0:T(8,128)(2,1)S(1)}, bf16[256,256]{1,0:T(8,128)(2,1)S(1)}, u32[]{:S(2)}, u32[]{:S(2)}) %collective-permute-start.2) | collective-permute-done | bytes 131104 | tf_op jit(solution)/shard_map/ppermute | solution.py:253
  38.8 12.4 %all_to_all.15.parts_ref = bf16[4,256,256]{2,1,0:T(8,128)(2,1)S(1)} all-to-all(bf16[4,256,256]{2,1,0:T(8,128)(2,1)S(1)} %shard_map.190), channel_id=1, replica_groups=mesh['wide'=64,'chip'=4,'core'=2] {'chip'}, dimensions={0} | all-to-all | bytes 1048576 | tf_op jit(solution)/shard_map/all_to_all | solution.py:349
  51.2 0.0 copy-done.10
  51.2 0.5 shard_map.191
  51.7 9.0 %all_to_all.16.pieces_ref = bf16[4,128,256]{2,1,0:T(8,128)(2,1)S(1)} all-to-all(bf16[4,128,256]{2,1,0:T(8,128)(2,1)S(1)} %get-tuple-element.32), channel_id=1, replica_groups={{0,8,16,24},{32,40,48,56},{64,72,80,88},{96,104,112,120},{128,136,144,1..., dimensions={0} | all-to-all | bytes 524288 | tf_op jit(solution)/shard_map/all_to_all | solution.py:247
  60.7 0.1 shard_map.192.mine_ref
  60.8 3.9 %collective-permute-start.3 = (bf16[192,256]{1,0:T(8,128)(2,1)S(1)}, bf16[192,256]{1,0:T(8,128)(2,1)S(1)}, u32[]{:S(2)}, u32[]{:S(2)}) collective-permute-start(bf16[192,256]{1,0:T(8,128)(2,1)S(1)} %shard_map.192.mine_ref), channel_id=1, source_target_pairs={{0,1},{1,0},{2,3},{3,2},{4,5},{5,4},{6,7},{7,6},{8,9},{9,8},{10,11... | collective-permute-start | bytes 294920 | tf_op jit(solution)/shard_map/ppermute | solution.py:253
  64.8 0.9 %collective-permute-done.3.other_ref = bf16[192,256]{1,0:T(8,128)(2,1)S(1)} collective-permute-done((bf16[192,256]{1,0:T(8,128)(2,1)S(1)}, bf16[192,256]{1,0:T(8,128)(2,1)S(1)}, u32[]{:S(2)}, u32[]{:S(2)}) %collective-permute-start.3) | collective-permute-done | bytes 98336 | tf_op jit(solution)/shard_map/ppermute | solution.py:253
  65.7 0.0 copy-done.4
  65.7 0.0 copy-done.7
  65.7 0.0 copy-done.11
  65.7 2.0 %shard_map.193 = (bf16[1024,256]{1,0:T(8,128)(2,1)}, bf16[256,256]{1,0:T(8,128)(2,1)}) custom-call(f32[192,256]{1,0:T(8,128)S(1)} %get-tuple-element.31.own_ref, bf16[192,256]{1,0:T(8,128)(2,1)S(1)} %shard_map.192.mine_ref, bf16[192,256]{1,0:T(8,128)(2,1)S(1)} %collective-permute-done.3.other_ref, bf16[192,256]{1,0:T(8,128)(2,1)S(1)} %copy-done.7, ...), custom_call_target="tpu_custom_call" | custom-call | tf_op jit(solution)/shard_map/pallas_call | solution.py:360
  (10 shorter events, 0.1 us)
Async XLA Ops:
  1.9 9.6 %collective-permute-start = (bf16[16,256]{1,0:T(8,128)(2,1)S(1)}, bf16[16,256]{1,0:T(8,128)(2,1)S(1)}, u32[]{:S(2)}, u32[]{:S(2)}) collective-permute-start(bf16[16,256]{1,0:T(8,128)(2,1)S(1)} %convolution_convert_fusion.mine_ref), channel_id=1, source_target_pairs={{0,1},{1,0},{2,3},{3,2},{4,5},{5,4},{6,7},{7,6},{8,9},{9,8},{10,11... | collective-permute-start | bytes 24584 | tf_op jit(solution)/shard_map/ppermute | solution.py:253
  12.2 15.6 %all-to-all-start = ((bf16[8,32,256]{2,1,0:T(8,128)(2,1)}), bf16[8,32,256]{2,1,0:T(8,128)(2,1)S(1)}, u32[]{:S(2)}, u32[]{:S(2)}) async-start(bf16[8,32,256]{2,1,0:T(8,128)(2,1)} %shard_map.185), calls=%async_computation | async-start | bytes 262144 | tf_op jit(solution)/shard_map/all_to_all | solution.py:247
  22.4 7.5 %copy-start.14 = (s32[2048]{0:T(1024)S(1)}, s32[2048]{0:T(1024)}, u32[]{:S(2)}) copy-start(s32[2048]{0:T(1024)} %param.22) | copy-start | bytes 24580
  22.4 7.5 %copy-start.15 = (s32[2048]{0:T(1024)S(1)}, s32[2048]{0:T(1024)}, u32[]{:S(2)}) copy-start(s32[2048]{0:T(1024)} %param.23) | copy-start | bytes 24580
  27.7 3.9 %copy-start = (bf16[1024,256]{1,0:T(8,128)(2,1)S(1)}, bf16[1024,256]{1,0:T(8,128)(2,1)}, u32[]{:S(2)}) copy-start(bf16[1024,256]{1,0:T(8,128)(2,1)} %fs_ref.1) | copy-start | bytes 1572868
  27.7 3.9 %copy-start.8 = (s32[1024]{0:T(1024)S(1)}, s32[1024]{0:T(1024)}, u32[]{:S(2)}) copy-start(s32[1024]{0:T(1024)} %param.24) | copy-start | bytes 12292
  27.8 3.9 %copy-start.12 = (bf16[512,256]{1,0:T(8,128)(2,1)S(1)}, bf16[512,256]{1,0:T(8,128)(2,1)}, u32[]{:S(2)}) copy-start(bf16[512,256]{1,0:T(8,128)(2,1)} %w_in_ref.1) | copy-start | bytes 786436
  27.8 3.9 %copy-start.13 = (bf16[256,256]{1,0:T(8,128)(2,1)S(1)}, bf16[256,256]{1,0:T(8,128)(2,1)}, u32[]{:S(2)}) copy-start(bf16[256,256]{1,0:T(8,128)(2,1)} %w_out_ref.1) | copy-start | bytes 393220
  27.8 3.9 %copy-start.16 = (f32[256]{0:T(256)S(1)}, f32[256]{0:T(256)}, u32[]{:S(2)}) copy-start(f32[256]{0:T(256)} %param.28) | copy-start | bytes 3076
  27.8 3.9 %copy-start.17 = (bf16[2048,256]{1,0:T(8,128)(2,1)S(1)}, bf16[2048,256]{1,0:T(8,128)(2,1)}, u32[]{:S(2)}) copy-start(bf16[2048,256]{1,0:T(8,128)(2,1)} %get-tuple-element.22.pre_ref) | copy-start | bytes 3145732
  27.8 3.8 %collective-permute-start.1 = (bf16[128,256]{1,0:T(8,128)(2,1)S(1)}, bf16[128,256]{1,0:T(8,128)(2,1)S(1)}, u32[]{:S(2)}, u32[]{:S(2)}) collective-permute-start(bf16[128,256]{1,0:T(8,128)(2,1)S(1)} %shard_map.187), channel_id=1, source_target_pairs={{0,1},{1,0},{2,3},{3,2},{4,5},{5,4},{6,7},{7,6},{8,9},{9,8},{10,11... | collective-permute-start | bytes 196616 | tf_op jit(solution)/shard_map/ppermute | solution.py:253
  31.7 19.5 %copy-start.5 = (bf16[256,256]{1,0:T(8,128)(2,1)S(1)}, bf16[256,256]{1,0:T(8,128)(2,1)}, u32[]{:S(2)}) copy-start(bf16[256,256]{1,0:T(8,128)(2,1)} %state_ref.1) | copy-start | bytes 393220
  31.7 19.5 %copy-start.6 = (bf16[256,256]{1,0:T(8,128)(2,1)S(1)}, bf16[256,256]{1,0:T(8,128)(2,1)}, u32[]{:S(2)}) copy-start(bf16[256,256]{1,0:T(8,128)(2,1)} %w_up_ref.1) | copy-start | bytes 393220
  31.7 19.5 %copy-start.9 = (s32[256]{0:T(256)S(1)}, s32[256]{0:T(256)}, u32[]{:S(2)}) copy-start(s32[256]{0:T(256)} %param.25) | copy-start | bytes 3076
  31.7 19.5 %copy-start.10 = (f32[256]{0:T(256)S(1)}, f32[256]{0:T(256)}, u32[]{:S(2)}) copy-start(f32[256]{0:T(256)} %param.30) | copy-start | bytes 3076
  35.2 30.5 %copy-start.1 = (bf16[256,256]{1,0:T(8,128)(2,1)S(1)}, bf16[256,256]{1,0:T(8,128)(2,1)}, u32[]{:S(2)}) copy-start(bf16[256,256]{1,0:T(8,128)(2,1)} %w1_ref.1) | copy-start | bytes 393220
  35.2 30.5 %copy-start.2 = (bf16[256,256]{1,0:T(8,128)(2,1)S(1)}, bf16[256,256]{1,0:T(8,128)(2,1)}, u32[]{:S(2)}) copy-start(bf16[256,256]{1,0:T(8,128)(2,1)} %w2_ref.1) | copy-start | bytes 393220
  35.2 30.5 %copy-start.3 = (bf16[256,256]{1,0:T(8,128)(2,1)S(1)}, bf16[256,256]{1,0:T(8,128)(2,1)}, u32[]{:S(2)}) copy-start(bf16[256,256]{1,0:T(8,128)(2,1)} %w_down_ref.1) | copy-start | bytes 393220
  35.2 30.5 %copy-start.4 = (bf16[256,256]{1,0:T(8,128)(2,1)S(1)}, bf16[256,256]{1,0:T(8,128)(2,1)}, u32[]{:S(2)}) copy-start(bf16[256,256]{1,0:T(8,128)(2,1)} %w_fine_ref.1) | copy-start | bytes 393220
  35.2 30.5 %copy-start.7 = (bf16[192,256]{1,0:T(8,128)(2,1)S(1)}, bf16[192,256]{1,0:T(8,128)(2,1)}, u32[]{:S(2)}) copy-start(bf16[192,256]{1,0:T(8,128)(2,1)} %get-tuple-element.33.l3_rows_ref) | copy-start | bytes 294916
  35.2 30.5 %copy-start.11 = (f32[256]{0:T(256)S(1)}, f32[256]{0:T(256)}, u32[]{:S(2)}) copy-start(f32[256]{0:T(256)} %param.31) | copy-start | bytes 3076
  35.2 3.5 %collective-permute-start.2 = (bf16[256,256]{1,0:T(8,128)(2,1)S(1)}, bf16[256,256]{1,0:T(8,128)(2,1)S(1)}, u32[]{:S(2)}, u32[]{:S(2)}) collective-permute-start(bf16[256,256]{1,0:T(8,128)(2,1)S(1)} %get-tuple-element.30.a_ref), channel_id=1, source_target_pairs={{0,1},{1,0},{2,3},{3,2},{4,5},{5,4},{6,7},{7,6},{8,9},{9,8},{10,11... | collective-permute-start | bytes 393224 | tf_op jit(solution)/shard_map/ppermute | solution.py:253
  60.8 4.9 %collective-permute-start.3 = (bf16[192,256]{1,0:T(8,128)(2,1)S(1)}, bf16[192,256]{1,0:T(8,128)(2,1)S(1)}, u32[]{:S(2)}, u32[]{:S(2)}) collective-permute-start(bf16[192,256]{1,0:T(8,128)(2,1)S(1)} %shard_map.192.mine_ref), channel_id=1, source_target_pairs={{0,1},{1,0},{2,3},{3,2},{4,5},{5,4},{6,7},{7,6},{8,9},{9,8},{10,11... | collective-permute-start | bytes 294920 | tf_op jit(solution)/shard_map/ppermute | solution.py:253

commit v8 on v7

--- a/solution.py
+++ b/solution.py
@@ -26,10 +26,18 @@
     return half + half * jnp.tanh(half)
 
 
-def column_parts(index):
-    low = (index & (LANES - 1)).astype(F32)
-    high = (index >> 7).astype(F32)
-    return low.T, high.T
+def column_parts(*indices):
+    parts = []
+    for index in indices:
+        parts.append((index & (LANES - 1)).astype(F32))
+        parts.append((index >> 7).astype(F32))
+    columns = jnp.concatenate(parts, axis=0).T
+    out, start = [], 0
+    for index in indices:
+        k = index.shape[0]
+        out.append((columns[:, start : start + k], columns[:, start + k : start + 2 * k]))
+        start += 2 * k
+    return out
 
 
 def lane_select(low_col, high_col):
@@ -60,7 +68,10 @@
     wide = lax.axis_index("wide")
     count = lax.axis_size("wide")
     rows = l3_rows_hbm.shape[0] // 3
-    pairs = [(send_hbm, send), (recv_hbm, recv), (w_in_hbm, w_in), (fs_hbm, fs)]
+    pairs = [(send_hbm, send), (recv_hbm, recv), (w_in_hbm, w_in)]
+    quarter = nodes // 4
+    for k in range(4):
+        pairs.append((fs_hbm.at[pl.ds(k * quarter, quarter)], fs.at[pl.ds(k * quarter, quarter)]))
     for k in range(3):
         block = lax.rem(wide + (k + count - 1), count)
         source = l3_hbm.at[pl.ds(pl.multiple_of(block * rows, rows), rows)]
@@ -70,11 +81,11 @@
         span = pl.ds(block * EDGE_BLOCK, EDGE_BLOCK)
         pairs.append((pre.at[span], pre_hbm.at[span]))
     copies = [pltpu.make_async_copy(a, b, sems.at[k]) for k, (a, b) in enumerate(pairs)]
-    for copy in copies[:7]:
+    for copy in copies[:10]:
         copy.start()
     copies[0].wait()
     copies[1].wait()
-    columns = [column_parts(send[...]), column_parts(recv[...])]
+    columns = column_parts(send[...], recv[...])
     for block in range(blocks):
         for part in range(EDGE_BLOCK // LANES):
             j = block * (EDGE_BLOCK // LANES) + part
@@ -86,13 +97,18 @@
                     hot[span, start : start + LANES] = pick(hot_j, high_j, t)
         if block == 0:
             copies[2].wait()
-            copies[3].wait()
-            proj[:nodes] = dot(fs[...], w_in[:width]).astype(BF16)
-            proj[nodes:] = dot(fs[...], w_in[width:]).astype(BF16)
+            for k in range(4):
+                copies[3 + k].wait()
+                rows_in = fs[k * quarter : (k + 1) * quarter]
+                for side in range(2):
+                    start = side * nodes + k * quarter
+                    proj[start : start + quarter] = dot(
+                        rows_in, w_in[side * width : (side + 1) * width]
+                    ).astype(BF16)
         span = slice(block * EDGE_BLOCK, (block + 1) * EDGE_BLOCK)
         pre[span] = dot(hot[span], proj[...]).astype(BF16)
-        copies[7 + block].start()
-    for copy in copies[4:]:
+        copies[10 + block].start()
+    for copy in copies[7:]:
         copy.wait()
 
 
@@ -110,22 +126,16 @@
     out_ref[...] = pair_ref[1 - pair_slot()]
 
 
-def prepare_kernel(send_ref, recv_ref, hot_ref, inc_ref):
-    tiles = inc_ref.shape[0] // LANES
-    low, high = column_parts(send_ref[...])
-    for j in range(send_ref.shape[0]):
-        span = slice(j * LANES, (j + 1) * LANES)
-        hot_s, high_s = lane_select(low[:, j : j + 1], high[:, j : j + 1])
-        for t in range(hot_ref.shape[1] // LANES):
-            hot_ref[span, t * LANES : (t + 1) * LANES] = pick(hot_s, high_s, tiles + t)
-        hot_r, high_r = row_select(recv_ref[j : j + 1])
-        for t in range(tiles):
-            inc_ref[t * LANES : (t + 1) * LANES, span] = pick(hot_r, high_r, t)
+def incidence_kernel(recv_ref, inc_ref):
+    for j in range(recv_ref.shape[0]):
+        hot, high = row_select(recv_ref[j : j + 1])
+        for t in range(inc_ref.shape[0] // LANES):
+            inc_ref[t * LANES : (t + 1) * LANES, j * LANES : (j + 1) * LANES] = pick(hot, high, t)
 
 
 def fine_kernel(
-    pre_ref, pair_ref, far_ref, fs_ref, hot_ref, inc_ref, par_ref, w_in_ref, w_out_ref, gain_ref,
-    mid_ref, part_ref, around, agg, upper,
+    pre_ref, pair_ref, far_ref, fs_ref, send_ref, inc_ref, par_ref, w_in_ref, w_out_ref, gain_ref,
+    mid_ref, part_ref, around, agg, upper, hot,
 ):
     nodes, width = fs_ref.shape
     edges = pre_ref.shape[0]
@@ -138,13 +148,20 @@
     around[bound : 2 * bound] = pair_ref[slot]
     around[pl.ds(pl.multiple_of(far_at, bound), bound)] = far_ref[...]
     proj = dot(around[...], w_in_ref[:width]).astype(BF16)
+    ((low, high),) = column_parts(send_ref[...])
     for j in range(tiles):
         hot_p, high_p = row_select(par_ref[j : j + 1])
         for t in range(upper.shape[0] // LANES):
             upper[t * LANES : (t + 1) * LANES, j * LANES : (j + 1) * LANES] = pick(hot_p, high_p, t)
     for block in range(edges // EDGE_BLOCK):
         span = slice(block * EDGE_BLOCK, (block + 1) * EDGE_BLOCK)
-        hidden = silu(pre_ref[span].astype(F32) + dot(hot_ref[span], proj)).astype(BF16)
+        for j in range(block * EDGE_BLOCK // LANES, (block + 1) * EDGE_BLOCK // LANES):
+            hot_s, high_s = lane_select(low[:, j : j + 1], high[:, j : j + 1])
+            for t in range(hot.shape[1] // LANES):
+                hot[j * LANES : (j + 1) * LANES, t * LANES : (t + 1) * LANES] = pick(
+                    hot_s, high_s, tiles + t
+                )
+        hidden = silu(pre_ref[span].astype(F32) + dot(hot[span], proj)).astype(BF16)
         for part in range(nodes // EDGE_BLOCK):
             here = slice(part * EDGE_BLOCK, (part + 1) * EDGE_BLOCK)
             more = dot(inc_ref[here, span], hidden)
@@ -210,7 +227,7 @@
 def down_kernel(
     level_three, own_ref, mine_ref, other_ref, l3_rows_ref, gain_ref,
     w1_ref, w2_ref, w_down_ref, w_fine_ref, parent_ref, mid_ref, par_ref, fine_ref,
-    fine_out_ref, down_ref,
+    fine_out_hbm, down_hbm, fine_out, down_out, sems,
 ):
     rows = own_ref.shape[0] // 3
     total = own_ref[...] + (mine_ref[...].astype(F32) + other_ref[...].astype(F32))
@@ -220,14 +237,24 @@
     lower = coarse_parent(parent_ref, rows, level_three).T.astype(BF16)
     picked = dot(lower, new).astype(BF16)
     down = (mid_ref[...].astype(F32) + dot(picked, w_down_ref[...])).astype(BF16)
-    down_ref[...] = down
+    down_out[...] = down
+    copies = [pltpu.make_async_copy(down_out, down_hbm, sems.at[0])]
+    copies[0].start()
     fine = dot(down, w_fine_ref[...]).astype(BF16)
-    par_low, par_high = column_parts(par_ref[...])
+    ((par_low, par_high),) = column_parts(par_ref[...])
     for j in range(par_ref.shape[0]):
         hot, high = lane_select(par_low[:, j : j + 1], par_high[:, j : j + 1])
         lower = jnp.concatenate([pick(hot, high, t) for t in range(fine.shape[0] // LANES)], axis=1)
         span = slice(j * LANES, (j + 1) * LANES)
-        fine_out_ref[span] = (fine_ref[span].astype(F32) + dot(lower, fine)).astype(BF16)
+        fine_out[span] = (fine_ref[span].astype(F32) + dot(lower, fine)).astype(BF16)
+        if j % 2 == 1:
+            part = pl.ds((j - 1) * LANES, 2 * LANES)
+            copies.append(
+                pltpu.make_async_copy(fine_out.at[part], fine_out_hbm.at[part], sems.at[(j + 1) // 2])
+            )
+            copies[-1].start()
+    for copy in copies:
+        copy.wait()
 
 
 def pair_slot():
@@ -318,19 +345,19 @@
             pltpu.VMEM((2 * nodes, width), BF16),
             pltpu.VMEM((edges, 2 * nodes), BF16),
             pltpu.VMEM((edges, width), BF16),
-            pltpu.SemaphoreType.DMA((7 + edges // EDGE_BLOCK,)),
+            pltpu.SemaphoreType.DMA((10 + edges // EDGE_BLOCK,)),
         ],
         hbm=range(5), hbm_outs=True, nargs=5, vmem=60, flops=5_000_000_000, moved=2_000_000,
     )(local_state, msg_in, send, recv, l3_state)
     pair, pre = lax.optimization_barrier((pair, pre))
     (near,) = call(neighbour_kernel, [((bound, width), BF16)], nargs=1)(pair)
     far = core_swapped(near)
-    near, send_late = lax.optimization_barrier((near, send))
-    hot, incidence = call(
-        prepare_kernel, [((edges, 3 * bound), BF16), ((nodes, edges), BF16)],
-        nargs=2, flops=1_000_000_000, moved=6_000_000,
-    )(send_late, recv)
-    far, hot, incidence = lax.optimization_barrier((far, hot, incidence))
+    near, recv_late = lax.optimization_barrier((near, recv))
+    (incidence,) = call(
+        incidence_kernel, [((nodes, edges), BF16)],
+        nargs=1, flops=1_000_000_000, moved=4_000_000,
+    )(recv_late)
+    far, incidence = lax.optimization_barrier((far, incidence))
 
     fine_mid, part = call(
         fine_kernel,
@@ -339,9 +366,10 @@
             pltpu.VMEM((3 * bound, width), BF16),
             pltpu.VMEM((nodes, width), F32),
             pltpu.VMEM((level_two, nodes), BF16),
+            pltpu.VMEM((edges, 3 * bound), BF16),
         ],
         nargs=10, flops=3_000_000_000, moved=4_000_000,
-    )(pre, pair, far, fine_state, hot, incidence, par, msg_in, msg_out, fine_gain)
+    )(pre, pair, far, fine_state, send, incidence, par, msg_in, msg_out, fine_gain)
 
     (chip_sums,) = call(add_kernel, [((chips, level_two, width), BF16)], nargs=2)(
         part, core_swapped(part)
@@ -360,7 +388,12 @@
     fine_out, l2_down = call(
         functools.partial(down_kernel, level_three),
         [((nodes, width), BF16), ((level_two, width), BF16)],
-        nargs=13,
+        [
+            pltpu.VMEM((nodes, width), BF16),
+            pltpu.VMEM((level_two, width), BF16),
+            pltpu.SemaphoreType.DMA((1 + nodes // (2 * LANES),)),
+        ],
+        nargs=13, hbm_outs=True,
     )(
         own, mine, core_swapped(mine), l3_rows, l3_gain, l3_w1, l3_w2, down_weight, fine_down,
         parent, l2_mid, par, fine_mid,

time: 68.1 us -> 67.7 us (level)
  transfers between devices with their start and end apart: 5 -> 5, of which waited for: 3 -> 4; matrix products, arithmetic and copies ran while one was open for 0% -> 0% of each run, Pallas kernels for 10% -> 10%
where the time goes in v8:
time: 67.7 us; the launch traced here: 67.2 us
  starting transfers between devices  27.3 us (40%)
  blocking collectives  21.4 us (32%)
  Pallas kernels  13.3 us (20%)
  waiting for transfers between devices  2.85 us (4%)
  matrix products  1.27 us (2%)
  between operations  0.93 us (1%)
    ppermute x4, starting transfers between devices, core_swapped(): return lax.ppermute(value, 'core', [(0, 1), (1, 0)])  17.1 us
    all_to_all x1, blocking collectives, body(): chip_sums = lax.all_to_all(chip_sums, 'chip', 0, 0, tiled=True)  12.4 us
    all_to_all x1, starting transfers between devices, exchanged(): lax.all_to_all(value, ('wide', 'chip', 'core'), 0, 0, tiled=True, axis_in...  10.2 us
    all_to_all x1, blocking collectives, exchanged(): lax.all_to_all(value, ('wide', 'chip', 'core'), 0, 0, tiled=True, axis_in...  9.05 us
    pallas_call x1, Pallas kernels, body(): call(gather_kernel, [((edges, width), BF16), ((3 * rows, width), BF16)],...  5.54 us
    pallas_call x1, Pallas kernels, body(): call(fine_kernel, [((nodes, width), BF16), ((level_two, width), BF16)], [...  3.59 us
    ppermute x4, waiting for transfers between devices, core_swapped(): return lax.ppermute(value, 'core', [(0, 1), (1, 0)])  2.85 us
    pallas_call x1, Pallas kernels, body(): call(functools.partial(down_kernel, level_three), [((nodes, width), BF16)...  1.88 us
  transfers between devices with their start and end apart: 5, of which 4 were waited for; matrix products, arithmetic and copies ran while one was open for 0% of the time, Pallas kernels for 10%

profile of v8, /device:TPU:1, one launch (start us, length us, event | category | flops | bytes accessed | tf_op | source)
XLA Modules:
  0.0 67.2 jit_solution(18423800342747737906)
XLA Ops:
  0.6 1.3 %convolution_convert_fusion.mine_ref = bf16[16,256]{1,0:T(8,128)(2,1)S(1)} fusion(bf16[1024,256]{1,0:T(8,128)(2,1)} %fs_ref.1, s32[16]{0:T(128)} %param.21), kind=kOutput, calls=%fused_computation | convolution fusion | flops 8409088 | bytes 532544 | tf_op jit(solution)/shard_map/dot_general | solution.py:17
  1.9 8.8 %collective-permute-start = (bf16[16,256]{1,0:T(8,128)(2,1)S(1)}, bf16[16,256]{1,0:T(8,128)(2,1)S(1)}, u32[]{:S(2)}, u32[]{:S(2)}) collective-permute-start(bf16[16,256]{1,0:T(8,128)(2,1)S(1)} %convolution_convert_fusion.mine_ref), channel_id=1, source_target_pairs={{0,1},{1,0},{2,3},{3,2},{4,5},{5,4},{6,7},{7,6},{8,9},{9,8},{10,11... | collective-permute-start | bytes 24584 | tf_op jit(solution)/shard_map/ppermute | solution.py:280
  10.7 0.8 %collective-permute-done.other_ref = bf16[16,256]{1,0:T(8,128)(2,1)S(1)} collective-permute-done((bf16[16,256]{1,0:T(8,128)(2,1)S(1)}, bf16[16,256]{1,0:T(8,128)(2,1)S(1)}, u32[]{:S(2)}, u32[]{:S(2)}) %collective-permute-start) | collective-permute-done | bytes 8224 | tf_op jit(solution)/shard_map/ppermute | solution.py:280
  11.5 0.7 shard_map.185
  12.2 10.2 %all-to-all-start = ((bf16[8,32,256]{2,1,0:T(8,128)(2,1)}), bf16[8,32,256]{2,1,0:T(8,128)(2,1)S(1)}, u32[]{:S(2)}, u32[]{:S(2)}) async-start(bf16[8,32,256]{2,1,0:T(8,128)(2,1)} %shard_map.185), calls=%async_computation | async-start | bytes 262144 | tf_op jit(solution)/shard_map/all_to_all | solution.py:274
  22.4 5.5 %shard_map.186 = (bf16[2048,256]{1,0:T(8,128)(2,1)}, bf16[192,256]{1,0:T(8,128)(2,1)}) custom-call(bf16[1024,256]{1,0:T(8,128)(2,1)} %fs_ref.1, bf16[512,256]{1,0:T(8,128)(2,1)} %w_in_ref.1, s32[16,128]{1,0:T(8,128)} %bitcast.19, s32[16,128]{1,0:T(8,128)} %bitcast.11, bf16[4096,256]{1,0:T(8,128)(2,1)} %l3_hbm.1), custom_call_target="tpu_custom_call" | custom-call | flops 5000000000 | bytes 2000000 | tf_op jit(solution)/shard_map/pallas_call | solution.py:337
  27.9 0.0 copy-start
  28.0 0.0 copy-start.9
  28.0 0.0 copy-start.13
  28.0 0.0 copy-start.14
  28.0 0.0 copy-start.15
  28.0 0.0 copy-start.16
  28.0 0.0 copy-start.17
  28.0 0.0 all-to-all-done
  28.1 2.1 %collective-permute-start.1 = (bf16[128,256]{1,0:T(8,128)(2,1)S(1)}, bf16[128,256]{1,0:T(8,128)(2,1)S(1)}, u32[]{:S(2)}, u32[]{:S(2)}) collective-permute-start(bf16[128,256]{1,0:T(8,128)(2,1)S(1)} %shard_map.187), channel_id=1, source_target_pairs={{0,1},{1,0},{2,3},{3,2},{4,5},{5,4},{6,7},{7,6},{8,9},{9,8},{10,11... | collective-permute-start | bytes 196616 | tf_op jit(solution)/shard_map/ppermute | solution.py:280
  30.1 0.0 copy-done.8
  30.1 1.0 %shard_map.188.inc_ref = bf16[1024,2048]{1,0:T(8,128)(2,1)S(1)} custom-call(s32[16,128]{1,0:T(8,128)S(1)} %bitcast.12), custom_call_target="tpu_custom_call" | custom-call | flops 1000000000 | bytes 4000000 | tf_op jit(solution)/shard_map/pallas_call | solution.py:356
  31.2 0.2 collective-permute-done.1.far_ref
  31.3 0.0 copy-done
  31.3 0.0 copy-done.9
  31.3 0.0 copy-done.13
  31.4 0.0 copy-done.14
  31.4 0.0 copy-done.15
  31.4 0.0 copy-done.16
  31.4 0.0 copy-start.5
  31.4 0.0 copy-start.6
  31.4 0.0 copy-start.10
  31.4 0.0 copy-start.11
  31.4 0.0 copy-start.1
  31.5 0.0 copy-start.2
  31.5 0.0 copy-start.3
  31.5 0.0 copy-start.4
  31.5 0.0 copy-start.7
  31.5 0.0 copy-start.12
  31.5 3.6 %shard_map.189 = (bf16[1024,256]{1,0:T(8,128)(2,1)S(1)}, bf16[256,256]{1,0:T(8,128)(2,1)S(1)}) custom-call(bf16[2048,256]{1,0:T(8,128)(2,1)S(1)} %copy-done.17, bf16[2,128,256]{2,1,0:T(8,128)(2,1)S(1)} %bitcast.10, bf16[128,256]{1,0:T(8,128)(2,1)S(1)} %collective-permute-done.1.far_ref, bf16[1024,256]{1,0:T(8,128)(2,1)S(1)} %copy-done, ...), custom_call_target="tpu_custom_call" | custom-call | flops 3000000000 | bytes 4000000 | tf_op jit(solution)/shard_map/pallas_call | solution.py:362
  35.1 2.3 %collective-permute-start.2 = (bf16[256,256]{1,0:T(8,128)(2,1)S(1)}, bf16[256,256]{1,0:T(8,128)(2,1)S(1)}, u32[]{:S(2)}, u32[]{:S(2)}) collective-permute-start(bf16[256,256]{1,0:T(8,128)(2,1)S(1)} %get-tuple-element.24.a_ref), channel_id=1, source_target_pairs={{0,1},{1,0},{2,3},{3,2},{4,5},{5,4},{6,7},{7,6},{8,9},{9,8},{10,11... | collective-permute-start | bytes 393224 | tf_op jit(solution)/shard_map/ppermute | solution.py:280
  37.4 1.0 %collective-permute-done.2.b_ref = bf16[256,256]{1,0:T(8,128)(2,1)S(1)} collective-permute-done((bf16[256,256]{1,0:T(8,128)(2,1)S(1)}, bf16[256,256]{1,0:T(8,128)(2,1)S(1)}, u32[]{:S(2)}, u32[]{:S(2)}) %collective-permute-start.2) | collective-permute-done | bytes 131104 | tf_op jit(solution)/shard_map/ppermute | solution.py:280
  38.4 12.4 %all_to_all.15.parts_ref = bf16[4,256,256]{2,1,0:T(8,128)(2,1)S(1)} all-to-all(bf16[4,256,256]{2,1,0:T(8,128)(2,1)S(1)} %shard_map.190), channel_id=1, replica_groups=mesh['wide'=64,'chip'=4,'core'=2] {'chip'}, dimensions={0} | all-to-all | bytes 1048576 | tf_op jit(solution)/shard_map/all_to_all | solution.py:377
  50.8 0.0 copy-done.6
  50.8 0.5 shard_map.191
  51.3 9.0 %all_to_all.16.pieces_ref = bf16[4,128,256]{2,1,0:T(8,128)(2,1)S(1)} all-to-all(bf16[4,128,256]{2,1,0:T(8,128)(2,1)S(1)} %get-tuple-element.26), channel_id=1, replica_groups={{0,8,16,24},{32,40,48,56},{64,72,80,88},{96,104,112,120},{128,136,144,1..., dimensions={0} | all-to-all | bytes 524288 | tf_op jit(solution)/shard_map/all_to_all | solution.py:274
  60.4 0.1 shard_map.192.mine_ref
  60.4 3.9 %collective-permute-start.3 = (bf16[192,256]{1,0:T(8,128)(2,1)S(1)}, bf16[192,256]{1,0:T(8,128)(2,1)S(1)}, u32[]{:S(2)}, u32[]{:S(2)}) collective-permute-start(bf16[192,256]{1,0:T(8,128)(2,1)S(1)} %shard_map.192.mine_ref), channel_id=1, source_target_pairs={{0,1},{1,0},{2,3},{3,2},{4,5},{5,4},{6,7},{7,6},{8,9},{9,8},{10,11... | collective-permute-start | bytes 294920 | tf_op jit(solution)/shard_map/ppermute | solution.py:280
  64.4 0.9 %collective-permute-done.3.other_ref = bf16[192,256]{1,0:T(8,128)(2,1)S(1)} collective-permute-done((bf16[192,256]{1,0:T(8,128)(2,1)S(1)}, bf16[192,256]{1,0:T(8,128)(2,1)S(1)}, u32[]{:S(2)}, u32[]{:S(2)}) %collective-permute-start.3) | collective-permute-done | bytes 98336 | tf_op jit(solution)/shard_map/ppermute | solution.py:280
  65.3 0.0 copy-done.1
  65.3 0.0 copy-done.7
  65.3 0.0 copy-done.12
  65.4 1.9 %shard_map.193 = (bf16[1024,256]{1,0:T(8,128)(2,1)}, bf16[256,256]{1,0:T(8,128)(2,1)}) custom-call(f32[192,256]{1,0:T(8,128)S(1)} %get-tuple-element.25.own_ref, bf16[192,256]{1,0:T(8,128)(2,1)S(1)} %shard_map.192.mine_ref, bf16[192,256]{1,0:T(8,128)(2,1)S(1)} %collective-permute-done.3.other_ref, bf16[192,256]{1,0:T(8,128)(2,1)S(1)} %copy-done.7, ...), custom_call_target="tpu_custom_call" | custom-call | tf_op jit(solution)/shard_map/pallas_call | solution.py:388
  (10 shorter events, 0.1 us)
Async XLA Ops:
  1.9 9.6 %collective-permute-start = (bf16[16,256]{1,0:T(8,128)(2,1)S(1)}, bf16[16,256]{1,0:T(8,128)(2,1)S(1)}, u32[]{:S(2)}, u32[]{:S(2)}) collective-permute-start(bf16[16,256]{1,0:T(8,128)(2,1)S(1)} %convolution_convert_fusion.mine_ref), channel_id=1, source_target_pairs={{0,1},{1,0},{2,3},{3,2},{4,5},{5,4},{6,7},{7,6},{8,9},{9,8},{10,11... | collective-permute-start | bytes 24584 | tf_op jit(solution)/shard_map/ppermute | solution.py:280
  12.2 15.9 %all-to-all-start = ((bf16[8,32,256]{2,1,0:T(8,128)(2,1)}), bf16[8,32,256]{2,1,0:T(8,128)(2,1)S(1)}, u32[]{:S(2)}, u32[]{:S(2)}) async-start(bf16[8,32,256]{2,1,0:T(8,128)(2,1)} %shard_map.185), calls=%async_computation | async-start | bytes 262144 | tf_op jit(solution)/shard_map/all_to_all | solution.py:274
  22.4 7.7 %copy-start.8 = (s32[2048]{0:T(1024)S(1)}, s32[2048]{0:T(1024)}, u32[]{:S(2)}) copy-start(s32[2048]{0:T(1024)} %param.23) | copy-start | bytes 24580
  27.9 3.4 %copy-start = (bf16[1024,256]{1,0:T(8,128)(2,1)S(1)}, bf16[1024,256]{1,0:T(8,128)(2,1)}, u32[]{:S(2)}) copy-start(bf16[1024,256]{1,0:T(8,128)(2,1)} %fs_ref.1) | copy-start | bytes 1572868
  28.0 3.4 %copy-start.9 = (s32[1024]{0:T(1024)S(1)}, s32[1024]{0:T(1024)}, u32[]{:S(2)}) copy-start(s32[1024]{0:T(1024)} %param.24) | copy-start | bytes 12292
  28.0 3.4 %copy-start.13 = (bf16[512,256]{1,0:T(8,128)(2,1)S(1)}, bf16[512,256]{1,0:T(8,128)(2,1)}, u32[]{:S(2)}) copy-start(bf16[512,256]{1,0:T(8,128)(2,1)} %w_in_ref.1) | copy-start | bytes 786436
  28.0 3.4 %copy-start.14 = (bf16[256,256]{1,0:T(8,128)(2,1)S(1)}, bf16[256,256]{1,0:T(8,128)(2,1)}, u32[]{:S(2)}) copy-start(bf16[256,256]{1,0:T(8,128)(2,1)} %w_out_ref.1) | copy-start | bytes 393220
  28.0 3.4 %copy-start.15 = (s32[2048]{0:T(1024)S(1)}, s32[2048]{0:T(1024)}, u32[]{:S(2)}) copy-start(s32[2048]{0:T(1024)} %param.22) | copy-start | bytes 24580
  28.0 3.4 %copy-start.16 = (f32[256]{0:T(256)S(1)}, f32[256]{0:T(256)}, u32[]{:S(2)}) copy-start(f32[256]{0:T(256)} %param.28) | copy-start | bytes 3076
  28.0 3.4 %copy-start.17 = (bf16[2048,256]{1,0:T(8,128)(2,1)S(1)}, bf16[2048,256]{1,0:T(8,128)(2,1)}, u32[]{:S(2)}) copy-start(bf16[2048,256]{1,0:T(8,128)(2,1)} %get-tuple-element.19.pre_ref) | copy-start | bytes 3145732
  28.1 3.3 %collective-permute-start.1 = (bf16[128,256]{1,0:T(8,128)(2,1)S(1)}, bf16[128,256]{1,0:T(8,128)(2,1)S(1)}, u32[]{:S(2)}, u32[]{:S(2)}) collective-permute-start(bf16[128,256]{1,0:T(8,128)(2,1)S(1)} %shard_map.187), channel_id=1, source_target_pairs={{0,1},{1,0},{2,3},{3,2},{4,5},{5,4},{6,7},{7,6},{8,9},{9,8},{10,11... | collective-permute-start | bytes 196616 | tf_op jit(solution)/shard_map/ppermute | solution.py:280
  31.4 19.4 %copy-start.5 = (bf16[256,256]{1,0:T(8,128)(2,1)S(1)}, bf16[256,256]{1,0:T(8,128)(2,1)}, u32[]{:S(2)}) copy-start(bf16[256,256]{1,0:T(8,128)(2,1)} %state_ref.1) | copy-start | bytes 393220
  31.4 19.4 %copy-start.6 = (bf16[256,256]{1,0:T(8,128)(2,1)S(1)}, bf16[256,256]{1,0:T(8,128)(2,1)}, u32[]{:S(2)}) copy-start(bf16[256,256]{1,0:T(8,128)(2,1)} %w_up_ref.1) | copy-start | bytes 393220
  31.4 19.4 %copy-start.10 = (s32[256]{0:T(256)S(1)}, s32[256]{0:T(256)}, u32[]{:S(2)}) copy-start(s32[256]{0:T(256)} %param.25) | copy-start | bytes 3076
  31.4 19.4 %copy-start.11 = (f32[256]{0:T(256)S(1)}, f32[256]{0:T(256)}, u32[]{:S(2)}) copy-start(f32[256]{0:T(256)} %param.30) | copy-start | bytes 3076
  31.4 33.9 %copy-start.1 = (bf16[256,256]{1,0:T(8,128)(2,1)S(1)}, bf16[256,256]{1,0:T(8,128)(2,1)}, u32[]{:S(2)}) copy-start(bf16[256,256]{1,0:T(8,128)(2,1)} %w1_ref.1) | copy-start | bytes 393220
  31.5 33.9 %copy-start.2 = (bf16[256,256]{1,0:T(8,128)(2,1)S(1)}, bf16[256,256]{1,0:T(8,128)(2,1)}, u32[]{:S(2)}) copy-start(bf16[256,256]{1,0:T(8,128)(2,1)} %w2_ref.1) | copy-start | bytes 393220
  31.5 33.9 %copy-start.3 = (bf16[256,256]{1,0:T(8,128)(2,1)S(1)}, bf16[256,256]{1,0:T(8,128)(2,1)}, u32[]{:S(2)}) copy-start(bf16[256,256]{1,0:T(8,128)(2,1)} %w_down_ref.1) | copy-start | bytes 393220
  31.5 33.9 %copy-start.4 = (bf16[256,256]{1,0:T(8,128)(2,1)S(1)}, bf16[256,256]{1,0:T(8,128)(2,1)}, u32[]{:S(2)}) copy-start(bf16[256,256]{1,0:T(8,128)(2,1)} %w_fine_ref.1) | copy-start | bytes 393220
  31.5 33.8 %copy-start.7 = (bf16[192,256]{1,0:T(8,128)(2,1)S(1)}, bf16[192,256]{1,0:T(8,128)(2,1)}, u32[]{:S(2)}) copy-start(bf16[192,256]{1,0:T(8,128)(2,1)} %get-tuple-element.27.l3_rows_ref) | copy-start | bytes 294916
  31.5 33.8 %copy-start.12 = (f32[256]{0:T(256)S(1)}, f32[256]{0:T(256)}, u32[]{:S(2)}) copy-start(f32[256]{0:T(256)} %param.31) | copy-start | bytes 3076
  35.1 3.2 %collective-permute-start.2 = (bf16[256,256]{1,0:T(8,128)(2,1)S(1)}, bf16[256,256]{1,0:T(8,128)(2,1)S(1)}, u32[]{:S(2)}, u32[]{:S(2)}) collective-permute-start(bf16[256,256]{1,0:T(8,128)(2,1)S(1)} %get-tuple-element.24.a_ref), channel_id=1, source_target_pairs={{0,1},{1,0},{2,3},{3,2},{4,5},{5,4},{6,7},{7,6},{8,9},{9,8},{10,11... | collective-permute-start | bytes 393224 | tf_op jit(solution)/shard_map/ppermute | solution.py:280
  60.4 4.9 %collective-permute-start.3 = (bf16[192,256]{1,0:T(8,128)(2,1)S(1)}, bf16[192,256]{1,0:T(8,128)(2,1)S(1)}, u32[]{:S(2)}, u32[]{:S(2)}) collective-permute-start(bf16[192,256]{1,0:T(8,128)(2,1)S(1)} %shard_map.192.mine_ref), channel_id=1, source_target_pairs={{0,1},{1,0},{2,3},{3,2},{4,5},{5,4},{6,7},{7,6},{8,9},{9,8},{10,11... | collective-permute-start | bytes 294920 | tf_op jit(solution)/shard_map/ppermute | solution.py:280

commit v9 on v8

--- a/solution.py
+++ b/solution.py
@@ -59,34 +59,13 @@
     return jnp.where(high == jnp.asarray(tile, BF16), hot, jnp.zeros_like(hot))
 
 
-def gather_kernel(
-    fs_hbm, w_in_hbm, send_hbm, recv_hbm, l3_hbm, pre_hbm, l3_rows_hbm,
-    fs, w_in, send, recv, proj, hot, pre, sems,
-):
-    nodes, width = fs.shape
-    edges = pre.shape[0]
-    wide = lax.axis_index("wide")
-    count = lax.axis_size("wide")
-    rows = l3_rows_hbm.shape[0] // 3
-    pairs = [(send_hbm, send), (recv_hbm, recv), (w_in_hbm, w_in)]
-    quarter = nodes // 4
-    for k in range(4):
-        pairs.append((fs_hbm.at[pl.ds(k * quarter, quarter)], fs.at[pl.ds(k * quarter, quarter)]))
-    for k in range(3):
-        block = lax.rem(wide + (k + count - 1), count)
-        source = l3_hbm.at[pl.ds(pl.multiple_of(block * rows, rows), rows)]
-        pairs.append((source, l3_rows_hbm.at[pl.ds(k * rows, rows)]))
-    blocks = edges // EDGE_BLOCK
-    for block in range(blocks):
-        span = pl.ds(block * EDGE_BLOCK, EDGE_BLOCK)
-        pairs.append((pre.at[span], pre_hbm.at[span]))
-    copies = [pltpu.make_async_copy(a, b, sems.at[k]) for k, (a, b) in enumerate(pairs)]
-    for copy in copies[:10]:
-        copy.start()
-    copies[0].wait()
-    copies[1].wait()
-    columns = column_parts(send[...], recv[...])
-    for block in range(blocks):
+def gather_kernel(fs_ref, w_in_ref, send_ref, recv_ref, pre_ref, proj, hot):
+    nodes, width = fs_ref.shape
+    edges = pre_ref.shape[0]
+    proj[:nodes] = dot(fs_ref[...], w_in_ref[:width]).astype(BF16)
+    proj[nodes:] = dot(fs_ref[...], w_in_ref[width:]).astype(BF16)
+    columns = column_parts(send_ref[...], recv_ref[...])
+    for block in range(edges // EDGE_BLOCK):
         for part in range(EDGE_BLOCK // LANES):
             j = block * (EDGE_BLOCK // LANES) + part
             span = slice(j * LANES, (j + 1) * LANES)
@@ -95,21 +74,8 @@
                 for t in range(nodes // LANES):
                     start = side * nodes + t * LANES
                     hot[span, start : start + LANES] = pick(hot_j, high_j, t)
-        if block == 0:
-            copies[2].wait()
-            for k in range(4):
-                copies[3 + k].wait()
-                rows_in = fs[k * quarter : (k + 1) * quarter]
-                for side in range(2):
-                    start = side * nodes + k * quarter
-                    proj[start : start + quarter] = dot(
-                        rows_in, w_in[side * width : (side + 1) * width]
-                    ).astype(BF16)
         span = slice(block * EDGE_BLOCK, (block + 1) * EDGE_BLOCK)
-        pre[span] = dot(hot[span], proj[...]).astype(BF16)
-        copies[10 + block].start()
-    for copy in copies[7:]:
-        copy.wait()
+        pre_ref[span] = dot(hot[span], proj[...]).astype(BF16)
 
 
 def chip_rows_kernel(mine_ref, other_ref, out_ref):
@@ -189,11 +155,25 @@
 
 
 def window_kernel(
-    level_three, parts_ref, state_ref, w_up_ref, gain_ref, parent_ref,
-    own_ref, pieces_ref, mid_ref, padded,
+    level_three, parts_ref, state_ref, w_up_ref, gain_ref, parent_ref, l3_hbm,
+    own_ref, pieces_ref, mid_ref, l3_rows_ref, padded, sems,
 ):
     rows = own_ref.shape[0] // 3
     core = lax.axis_index("core")
+    wide = lax.axis_index("wide")
+    count = lax.axis_size("wide")
+    copies = []
+    for k in range(3):
+        block = lax.rem(wide + (k + count - 1), count)
+        copies.append(
+            pltpu.make_async_copy(
+                l3_hbm.at[pl.ds(pl.multiple_of(block * rows, rows), rows)],
+                l3_rows_ref.at[pl.ds(k * rows, rows)],
+                sems.at[k],
+            )
+        )
+    for copy in copies:
+        copy.start()
     total = parts_ref[0].astype(F32)
     for k in range(1, parts_ref.shape[0]):
         total = total + parts_ref[k].astype(F32)
@@ -212,6 +192,8 @@
         )
         start = jnp.where((core == 1) & ((here >= 2) == (there >= 2)), 5, start)
         pieces_ref[there] = padded[pl.ds(pl.multiple_of(start * rows, rows), 2 * rows)]
+    for copy in copies:
+        copy.wait()
 
 
 def collect_kernel(pieces_ref, out_ref, sums):
@@ -329,26 +311,18 @@
     ]
 
     (chip_rows,) = call(
-        chip_rows_kernel, [((2 * chips, cores * boundary.shape[0], width), BF16)], nargs=2
+        chip_rows_kernel, [((2 * chips, cores * boundary.shape[0], width), BF16)], nargs=2,
+        flops=6_000_000_000,
     )(exported, core_swapped(exported))
     chip_rows, local_state = lax.optimization_barrier((chip_rows, fine_state))
     pair = exchanged(chip_rows, pairs).reshape(2, bound, width)
 
-    pre, l3_rows = call(
+    (pre,) = call(
         gather_kernel,
-        [((edges, width), BF16), ((3 * rows, width), BF16)],
-        [
-            pltpu.VMEM((nodes, width), BF16),
-            pltpu.VMEM((2 * width, width), BF16),
-            pltpu.VMEM(send.shape, jnp.int32),
-            pltpu.VMEM(recv.shape, jnp.int32),
-            pltpu.VMEM((2 * nodes, width), BF16),
-            pltpu.VMEM((edges, 2 * nodes), BF16),
-            pltpu.VMEM((edges, width), BF16),
-            pltpu.SemaphoreType.DMA((10 + edges // EDGE_BLOCK,)),
-        ],
-        hbm=range(5), hbm_outs=True, nargs=5, vmem=60, flops=5_000_000_000, moved=2_000_000,
-    )(local_state, msg_in, send, recv, l3_state)
+        [((edges, width), BF16)],
+        [pltpu.VMEM((2 * nodes, width), BF16), pltpu.VMEM((edges, 2 * nodes), BF16)],
+        nargs=4, flops=5_000_000_000, moved=2_000_000,
+    )(local_state, msg_in, send, recv)
     pair, pre = lax.optimization_barrier((pair, pre))
     (near,) = call(neighbour_kernel, [((bound, width), BF16)], nargs=1)(pair)
     far = core_swapped(near)
@@ -375,12 +349,17 @@
         part, core_swapped(part)
     )
     chip_sums = lax.all_to_all(chip_sums, "chip", 0, 0, tiled=True)
-    own, pieces, l2_mid = call(
+    own, pieces, l2_mid, l3_rows = call(
         functools.partial(window_kernel, level_three),
-        [((3 * rows, width), F32), ((4, 2 * rows, width), BF16), ((level_two, width), BF16)],
-        [pltpu.VMEM((7 * rows, width), BF16)],
-        nargs=5,
-    )(chip_sums, l2_state, up_weight, l2_gain, parent)
+        [
+            ((3 * rows, width), F32),
+            ((4, 2 * rows, width), BF16),
+            ((level_two, width), BF16),
+            ((3 * rows, width), BF16),
+        ],
+        [pltpu.VMEM((7 * rows, width), BF16), pltpu.SemaphoreType.DMA((3,))],
+        hbm=(5,), nargs=6,
+    )(chip_sums, l2_state, up_weight, l2_gain, parent, l3_state)
     (mine,) = call(
         collect_kernel, [((3 * rows, width), BF16)], [pltpu.VMEM((3 * rows, width), F32)], nargs=1
     )(exchanged(pieces, quads))

time: 67.7 us -> 66.4 us (0.981)
  Pallas kernels: 13.3 us -> 11.1 us
  waiting for transfers between devices: 2.85 us -> 4 us
    pallas_call x1, Pallas kernels: 5.54 us -> 3.17 us  [body(): call(gather_kernel, [((edges, width), BF16)], [pltpu.VMEM((2 * nodes, wid...]
    all_to_all x1, waiting for transfers between devices: 0.01 us -> 1.13 us  [exchanged(): lax.all_to_all(value, ('wide', 'chip', 'core'), 0, 0, tiled=True, axis_in...]
    all_to_all x1, blocking collectives: 12.4 us -> 11.4 us  [body(): chip_sums = lax.all_to_all(chip_sums, 'chip', 0, 0, tiled=True)]
    all_to_all x1, blocking collectives: 9.05 us -> 9.84 us  [exchanged(): lax.all_to_all(value, ('wide', 'chip', 'core'), 0, 0, tiled=True, axis_in...]
  transfers between devices with their start and end apart: 5 -> 5, of which waited for: 4 -> 5; matrix products, arithmetic and copies ran while one was open for 0% -> 0% of each run, Pallas kernels for 10% -> 6%
where the time goes in v9:
time: 66.4 us; the launch traced here: 66 us
  starting transfers between devices  27.3 us (41%)
  blocking collectives  21.3 us (32%)
  Pallas kernels  11.1 us (17%)
  waiting for transfers between devices  4 us (6%)
  matrix products  1.27 us (2%)
  between operations  0.89 us (1%)
    ppermute x4, starting transfers between devices, core_swapped(): return lax.ppermute(value, 'core', [(0, 1), (1, 0)])  17.1 us
    all_to_all x1, blocking collectives, body(): chip_sums = lax.all_to_all(chip_sums, 'chip', 0, 0, tiled=True)  11.4 us
    all_to_all x1, starting transfers between devices, exchanged(): lax.all_to_all(value, ('wide', 'chip', 'core'), 0, 0, tiled=True, axis_in...  10.2 us
    all_to_all x1, blocking collectives, exchanged(): lax.all_to_all(value, ('wide', 'chip', 'core'), 0, 0, tiled=True, axis_in...  9.84 us
    pallas_call x1, Pallas kernels, body(): call(fine_kernel, [((nodes, width), BF16), ((level_two, width), BF16)], [...  3.59 us
    pallas_call x1, Pallas kernels, body(): call(gather_kernel, [((edges, width), BF16)], [pltpu.VMEM((2 * nodes, wid...  3.17 us
    ppermute x4, waiting for transfers between devices, core_swapped(): return lax.ppermute(value, 'core', [(0, 1), (1, 0)])  2.87 us
    pallas_call x1, Pallas kernels, body(): call(functools.partial(down_kernel, level_three), [((nodes, width), BF16)...  1.88 us
  transfers between devices with their start and end apart: 5, of which 5 were waited for; matrix products, arithmetic and copies ran while one was open for 0% of the time, Pallas kernels for 6%

profile of v9, /device:TPU:1, one launch (start us, length us, event | category | flops | bytes accessed | tf_op | source)
XLA Modules:
  0.0 66.0 jit_solution(14808460029486990221)
XLA Ops:
  0.6 1.3 %convolution_convert_fusion.mine_ref = bf16[16,256]{1,0:T(8,128)(2,1)S(1)} fusion(bf16[1024,256]{1,0:T(8,128)(2,1)} %fs_ref.2, s32[16]{0:T(128)} %param.21), kind=kOutput, calls=%fused_computation | convolution fusion | flops 8409088 | bytes 532544 | tf_op jit(solution)/shard_map/dot_general | solution.py:17
  1.9 0.0 copy-start.13
  1.9 0.0 copy-start.15
  1.9 8.9 %collective-permute-start = (bf16[16,256]{1,0:T(8,128)(2,1)S(1)}, bf16[16,256]{1,0:T(8,128)(2,1)S(1)}, u32[]{:S(2)}, u32[]{:S(2)}) collective-permute-start(bf16[16,256]{1,0:T(8,128)(2,1)S(1)} %convolution_convert_fusion.mine_ref), channel_id=1, source_target_pairs={{0,1},{1,0},{2,3},{3,2},{4,5},{5,4},{6,7},{7,6},{8,9},{9,8},{10,11... | collective-permute-start | bytes 24584 | tf_op jit(solution)/shard_map/ppermute | solution.py:262
  10.9 0.8 %collective-permute-done.other_ref = bf16[16,256]{1,0:T(8,128)(2,1)S(1)} collective-permute-done((bf16[16,256]{1,0:T(8,128)(2,1)S(1)}, bf16[16,256]{1,0:T(8,128)(2,1)S(1)}, u32[]{:S(2)}, u32[]{:S(2)}) %collective-permute-start) | collective-permute-done | bytes 8224 | tf_op jit(solution)/shard_map/ppermute | solution.py:262
  11.7 0.7 %shard_map.185 = bf16[8,32,256]{2,1,0:T(8,128)(2,1)} custom-call(bf16[16,256]{1,0:T(8,128)(2,1)S(1)} %convolution_convert_fusion.mine_ref, bf16[16,256]{1,0:T(8,128)(2,1)S(1)} %collective-permute-done.other_ref), custom_call_target="tpu_custom_call" | custom-call | flops 6000000000 | tf_op jit(solution)/shard_map/pallas_call | solution.py:313
  12.3 10.2 %all-to-all-start = ((bf16[8,32,256]{2,1,0:T(8,128)(2,1)}), bf16[8,32,256]{2,1,0:T(8,128)(2,1)S(1)}, u32[]{:S(2)}, u32[]{:S(2)}) async-start(bf16[8,32,256]{2,1,0:T(8,128)(2,1)} %shard_map.185), calls=%async_computation | async-start | bytes 262144 | tf_op jit(solution)/shard_map/all_to_all | solution.py:256
  22.6 0.0 copy-done.1
  22.6 0.0 copy-done.8
  22.6 0.0 copy-done.13
  22.6 0.0 copy-done.15
  22.6 3.2 %shard_map.186.pre_ref = bf16[2048,256]{1,0:T(8,128)(2,1)S(1)} custom-call(bf16[1024,256]{1,0:T(8,128)(2,1)S(1)} %copy-done.1, bf16[512,256]{1,0:T(8,128)(2,1)S(1)} %copy-done.13, s32[16,128]{1,0:T(8,128)S(1)} %bitcast.19, s32[16,128]{1,0:T(8,128)S(1)} %bitcast.11), custom_call_target="tpu_custom_call" | custom-call | flops 5000000000 | bytes 2000000 | tf_op jit(solution)/shard_map/pallas_call | solution.py:320
  25.8 0.0 copy-start.10
  25.8 0.0 copy-start.14
  25.8 0.0 copy-start.16
  25.8 1.1 %all-to-all-done = bf16[8,32,256]{2,1,0:T(8,128)(2,1)S(1)} async-done(((bf16[8,32,256]{2,1,0:T(8,128)(2,1)}), bf16[8,32,256]{2,1,0:T(8,128)(2,1)S(1)}, u32[]{:S(2)}, u32[]{:S(2)}) %all-to-all-start) | async-done | bytes 131104 | tf_op jit(solution)/shard_map/all_to_all | solution.py:256
  26.9 1.9 %collective-permute-start.1 = (bf16[128,256]{1,0:T(8,128)(2,1)S(1)}, bf16[128,256]{1,0:T(8,128)(2,1)S(1)}, u32[]{:S(2)}, u32[]{:S(2)}) collective-permute-start(bf16[128,256]{1,0:T(8,128)(2,1)S(1)} %shard_map.187), channel_id=1, source_target_pairs={{0,1},{1,0},{2,3},{3,2},{4,5},{5,4},{6,7},{7,6},{8,9},{9,8},{10,11... | collective-permute-start | bytes 196616 | tf_op jit(solution)/shard_map/ppermute | solution.py:262
  28.9 1.0 %shard_map.188.inc_ref = bf16[1024,2048]{1,0:T(8,128)(2,1)S(1)} custom-call(s32[16,128]{1,0:T(8,128)S(1)} %bitcast.12), custom_call_target="tpu_custom_call" | custom-call | flops 1000000000 | bytes 4000000 | tf_op jit(solution)/shard_map/pallas_call | solution.py:330
  29.9 0.2 collective-permute-done.1.far_ref
  30.1 0.0 copy-done.10
  30.1 0.0 copy-done.14
  30.1 0.0 copy-done.16
  30.1 0.0 copy-start
  30.1 0.0 copy-start.2
  30.1 0.0 copy-start.3
  30.1 0.0 copy-start.9
  30.1 0.0 copy-start.11
  30.1 3.6 %shard_map.189 = (bf16[1024,256]{1,0:T(8,128)(2,1)S(1)}, bf16[256,256]{1,0:T(8,128)(2,1)S(1)}) custom-call(bf16[2048,256]{1,0:T(8,128)(2,1)S(1)} %shard_map.186.pre_ref, bf16[2,128,256]{2,1,0:T(8,128)(2,1)S(1)} %bitcast.10, bf16[128,256]{1,0:T(8,128)(2,1)S(1)} %collective-permute-done.1.far_ref, bf16[1024,256]{1,0:T(8,128)(2,1)S(1)} %copy-done.1, ...), custom_call_target="tpu_custom_call" | custom-call | flops 3000000000 | bytes 4000000 | tf_op jit(solution)/shard_map/pallas_call | solution.py:336
  33.7 0.0 copy-start.4
  33.8 0.0 copy-start.5
  33.8 0.0 copy-start.6
  33.8 0.0 copy-start.7
  33.8 0.0 copy-start.12
  33.8 2.4 %collective-permute-start.2 = (bf16[256,256]{1,0:T(8,128)(2,1)S(1)}, bf16[256,256]{1,0:T(8,128)(2,1)S(1)}, u32[]{:S(2)}, u32[]{:S(2)}) collective-permute-start(bf16[256,256]{1,0:T(8,128)(2,1)S(1)} %get-tuple-element.22.a_ref), channel_id=1, source_target_pairs={{0,1},{1,0},{2,3},{3,2},{4,5},{5,4},{6,7},{7,6},{8,9},{9,8},{10,11... | collective-permute-start | bytes 393224 | tf_op jit(solution)/shard_map/ppermute | solution.py:262
  36.2 1.0 %collective-permute-done.2.b_ref = bf16[256,256]{1,0:T(8,128)(2,1)S(1)} collective-permute-done((bf16[256,256]{1,0:T(8,128)(2,1)S(1)}, bf16[256,256]{1,0:T(8,128)(2,1)S(1)}, u32[]{:S(2)}, u32[]{:S(2)}) %collective-permute-start.2) | collective-permute-done | bytes 131104 | tf_op jit(solution)/shard_map/ppermute | solution.py:262
  37.2 11.4 %all_to_all.15.parts_ref = bf16[4,256,256]{2,1,0:T(8,128)(2,1)S(1)} all-to-all(bf16[4,256,256]{2,1,0:T(8,128)(2,1)S(1)} %shard_map.190), channel_id=1, replica_groups=mesh['wide'=64,'chip'=4,'core'=2] {'chip'}, dimensions={0} | all-to-all | bytes 1048576 | tf_op jit(solution)/shard_map/all_to_all | solution.py:351
  48.6 0.0 copy-done
  48.6 0.0 copy-done.2
  48.7 0.0 copy-done.3
  48.7 0.0 copy-done.9
  48.7 0.7 %shard_map.191 = (f32[192,256]{1,0:T(8,128)S(1)}, bf16[4,128,256]{2,1,0:T(8,128)(2,1)S(1)}, bf16[256,256]{1,0:T(8,128)(2,1)S(1)}, bf16[192,256]{1,0:T(8,128)(2,1)S(1)}) custom-call(bf16[4,256,256]{2,1,0:T(8,128)(2,1)S(1)} %all_to_all.15.parts_ref, bf16[256,256]{1,0:T(8,128)(2,1)S(1)} %copy-done.2, bf16[256,256]{1,0:T(8,128)(2,1)S(1)} %copy-done.3, ...), custom_call_target="tpu_custom_call" | custom-call | tf_op jit(solution)/shard_map/pallas_call | solution.py:352
  49.4 9.8 %all_to_all.16.pieces_ref = bf16[4,128,256]{2,1,0:T(8,128)(2,1)S(1)} all-to-all(bf16[4,128,256]{2,1,0:T(8,128)(2,1)S(1)} %get-tuple-element.24), channel_id=1, replica_groups={{0,8,16,24},{32,40,48,56},{64,72,80,88},{96,104,112,120},{128,136,144,1..., dimensions={0} | all-to-all | bytes 524288 | tf_op jit(solution)/shard_map/all_to_all | solution.py:256
  59.2 0.1 shard_map.192.mine_ref
  59.3 3.9 %collective-permute-start.3 = (bf16[192,256]{1,0:T(8,128)(2,1)S(1)}, bf16[192,256]{1,0:T(8,128)(2,1)S(1)}, u32[]{:S(2)}, u32[]{:S(2)}) collective-permute-start(bf16[192,256]{1,0:T(8,128)(2,1)S(1)} %shard_map.192.mine_ref), channel_id=1, source_target_pairs={{0,1},{1,0},{2,3},{3,2},{4,5},{5,4},{6,7},{7,6},{8,9},{9,8},{10,11... | collective-permute-start | bytes 294920 | tf_op jit(solution)/shard_map/ppermute | solution.py:262
  63.1 0.9 %collective-permute-done.3.other_ref = bf16[192,256]{1,0:T(8,128)(2,1)S(1)} collective-permute-done((bf16[192,256]{1,0:T(8,128)(2,1)S(1)}, bf16[192,256]{1,0:T(8,128)(2,1)S(1)}, u32[]{:S(2)}, u32[]{:S(2)}) %collective-permute-start.3) | collective-permute-done | bytes 98336 | tf_op jit(solution)/shard_map/ppermute | solution.py:262
  64.1 0.0 copy-done.4
  64.1 0.0 copy-done.12
  64.1 1.9 %shard_map.193 = (bf16[1024,256]{1,0:T(8,128)(2,1)}, bf16[256,256]{1,0:T(8,128)(2,1)}) custom-call(f32[192,256]{1,0:T(8,128)S(1)} %get-tuple-element.23.own_ref, bf16[192,256]{1,0:T(8,128)(2,1)S(1)} %shard_map.192.mine_ref, bf16[192,256]{1,0:T(8,128)(2,1)S(1)} %collective-permute-done.3.other_ref, bf16[192,256]{1,0:T(8,128)(2,1)S(1)} %get-tuple-element.25.l3_rows_ref, ...), custom_call_target="tpu_custom_call" | custom-call | tf_op jit(solution)/shard_map/pallas_call | solution.py:367
  (8 shorter events, 0.1 us)
Async XLA Ops:
  1.9 20.7 %copy-start.1 = (bf16[1024,256]{1,0:T(8,128)(2,1)S(1)}, bf16[1024,256]{1,0:T(8,128)(2,1)}, u32[]{:S(2)}) copy-start(bf16[1024,256]{1,0:T(8,128)(2,1)} %fs_ref.2) | copy-start | bytes 1572868
  1.9 20.7 %copy-start.8 = (s32[2048]{0:T(1024)S(1)}, s32[2048]{0:T(1024)}, u32[]{:S(2)}) copy-start(s32[2048]{0:T(1024)} %param.23) | copy-start | bytes 24580
  1.9 20.7 %copy-start.13 = (bf16[512,256]{1,0:T(8,128)(2,1)S(1)}, bf16[512,256]{1,0:T(8,128)(2,1)}, u32[]{:S(2)}) copy-start(bf16[512,256]{1,0:T(8,128)(2,1)} %w_in_ref.3) | copy-start | bytes 786436
  1.9 20.7 %copy-start.15 = (s32[2048]{0:T(1024)S(1)}, s32[2048]{0:T(1024)}, u32[]{:S(2)}) copy-start(s32[2048]{0:T(1024)} %param.22) | copy-start | bytes 24580
  1.9 9.7 %collective-permute-start = (bf16[16,256]{1,0:T(8,128)(2,1)S(1)}, bf16[16,256]{1,0:T(8,128)(2,1)S(1)}, u32[]{:S(2)}, u32[]{:S(2)}) collective-permute-start(bf16[16,256]{1,0:T(8,128)(2,1)S(1)} %convolution_convert_fusion.mine_ref), channel_id=1, source_target_pairs={{0,1},{1,0},{2,3},{3,2},{4,5},{5,4},{6,7},{7,6},{8,9},{9,8},{10,11... | collective-permute-start | bytes 24584 | tf_op jit(solution)/shard_map/ppermute | solution.py:262
  12.3 14.6 %all-to-all-start = ((bf16[8,32,256]{2,1,0:T(8,128)(2,1)}), bf16[8,32,256]{2,1,0:T(8,128)(2,1)S(1)}, u32[]{:S(2)}, u32[]{:S(2)}) async-start(bf16[8,32,256]{2,1,0:T(8,128)(2,1)} %shard_map.185), calls=%async_computation | async-start | bytes 262144 | tf_op jit(solution)/shard_map/all_to_all | solution.py:256
  25.8 4.3 %copy-start.10 = (s32[1024]{0:T(1024)S(1)}, s32[1024]{0:T(1024)}, u32[]{:S(2)}) copy-start(s32[1024]{0:T(1024)} %param.24) | copy-start | bytes 12292
  25.8 4.3 %copy-start.14 = (bf16[256,256]{1,0:T(8,128)(2,1)S(1)}, bf16[256,256]{1,0:T(8,128)(2,1)}, u32[]{:S(2)}) copy-start(bf16[256,256]{1,0:T(8,128)(2,1)} %w_out_ref.1) | copy-start | bytes 393220
  25.8 4.3 %copy-start.16 = (f32[256]{0:T(256)S(1)}, f32[256]{0:T(256)}, u32[]{:S(2)}) copy-start(f32[256]{0:T(256)} %param.28) | copy-start | bytes 3076
  26.9 3.1 %collective-permute-start.1 = (bf16[128,256]{1,0:T(8,128)(2,1)S(1)}, bf16[128,256]{1,0:T(8,128)(2,1)S(1)}, u32[]{:S(2)}, u32[]{:S(2)}) collective-permute-start(bf16[128,256]{1,0:T(8,128)(2,1)S(1)} %shard_map.187), channel_id=1, source_target_pairs={{0,1},{1,0},{2,3},{3,2},{4,5},{5,4},{6,7},{7,6},{8,9},{9,8},{10,11... | collective-permute-start | bytes 196616 | tf_op jit(solution)/shard_map/ppermute | solution.py:262
  30.1 18.6 %copy-start = (bf16[4096,256]{1,0:T(8,128)(2,1)S(1)}, bf16[4096,256]{1,0:T(8,128)(2,1)}, u32[]{:S(2)}) copy-start(bf16[4096,256]{1,0:T(8,128)(2,1)} %l3_hbm.1) | copy-start | bytes 6291460
  30.1 18.6 %copy-start.2 = (bf16[256,256]{1,0:T(8,128)(2,1)S(1)}, bf16[256,256]{1,0:T(8,128)(2,1)}, u32[]{:S(2)}) copy-start(bf16[256,256]{1,0:T(8,128)(2,1)} %state_ref.1) | copy-start | bytes 393220
  30.1 18.5 %copy-start.3 = (bf16[256,256]{1,0:T(8,128)(2,1)S(1)}, bf16[256,256]{1,0:T(8,128)(2,1)}, u32[]{:S(2)}) copy-start(bf16[256,256]{1,0:T(8,128)(2,1)} %w_up_ref.1) | copy-start | bytes 393220
  30.1 18.5 %copy-start.9 = (s32[256]{0:T(256)S(1)}, s32[256]{0:T(256)}, u32[]{:S(2)}) copy-start(s32[256]{0:T(256)} %param.25) | copy-start | bytes 3076
  30.1 18.5 %copy-start.11 = (f32[256]{0:T(256)S(1)}, f32[256]{0:T(256)}, u32[]{:S(2)}) copy-start(f32[256]{0:T(256)} %param.30) | copy-start | bytes 3076
  33.7 30.3 %copy-start.4 = (bf16[256,256]{1,0:T(8,128)(2,1)S(1)}, bf16[256,256]{1,0:T(8,128)(2,1)}, u32[]{:S(2)}) copy-start(bf16[256,256]{1,0:T(8,128)(2,1)} %w1_ref.1) | copy-start | bytes 393220
  33.8 30.3 %copy-start.5 = (bf16[256,256]{1,0:T(8,128)(2,1)S(1)}, bf16[256,256]{1,0:T(8,128)(2,1)}, u32[]{:S(2)}) copy-start(bf16[256,256]{1,0:T(8,128)(2,1)} %w2_ref.1) | copy-start | bytes 393220
  33.8 30.3 %copy-start.6 = (bf16[256,256]{1,0:T(8,128)(2,1)S(1)}, bf16[256,256]{1,0:T(8,128)(2,1)}, u32[]{:S(2)}) copy-start(bf16[256,256]{1,0:T(8,128)(2,1)} %w_down_ref.1) | copy-start | bytes 393220
  33.8 30.3 %copy-start.7 = (bf16[256,256]{1,0:T(8,128)(2,1)S(1)}, bf16[256,256]{1,0:T(8,128)(2,1)}, u32[]{:S(2)}) copy-start(bf16[256,256]{1,0:T(8,128)(2,1)} %w_fine_ref.1) | copy-start | bytes 393220
  33.8 30.3 %copy-start.12 = (f32[256]{0:T(256)S(1)}, f32[256]{0:T(256)}, u32[]{:S(2)}) copy-start(f32[256]{0:T(256)} %param.31) | copy-start | bytes 3076
  33.8 3.4 %collective-permute-start.2 = (bf16[256,256]{1,0:T(8,128)(2,1)S(1)}, bf16[256,256]{1,0:T(8,128)(2,1)S(1)}, u32[]{:S(2)}, u32[]{:S(2)}) collective-permute-start(bf16[256,256]{1,0:T(8,128)(2,1)S(1)} %get-tuple-element.22.a_ref), channel_id=1, source_target_pairs={{0,1},{1,0},{2,3},{3,2},{4,5},{5,4},{6,7},{7,6},{8,9},{9,8},{10,11... | collective-permute-start | bytes 393224 | tf_op jit(solution)/shard_map/ppermute | solution.py:262
  59.3 4.8 %collective-permute-start.3 = (bf16[192,256]{1,0:T(8,128)(2,1)S(1)}, bf16[192,256]{1,0:T(8,128)(2,1)S(1)}, u32[]{:S(2)}, u32[]{:S(2)}) collective-permute-start(bf16[192,256]{1,0:T(8,128)(2,1)S(1)} %shard_map.192.mine_ref), channel_id=1, source_target_pairs={{0,1},{1,0},{2,3},{3,2},{4,5},{5,4},{6,7},{7,6},{8,9},{9,8},{10,11... | collective-permute-start | bytes 294920 | tf_op jit(solution)/shard_map/ppermute | solution.py:262

commit v10 on v9

--- a/solution.py
+++ b/solution.py
@@ -128,10 +128,8 @@
                     hot_s, high_s, tiles + t
                 )
         hidden = silu(pre_ref[span].astype(F32) + dot(hot[span], proj)).astype(BF16)
-        for part in range(nodes // EDGE_BLOCK):
-            here = slice(part * EDGE_BLOCK, (part + 1) * EDGE_BLOCK)
-            more = dot(inc_ref[here, span], hidden)
-            agg[here] = more if block == 0 else agg[here] + more
+        more = dot(inc_ref[:, span], hidden)
+        agg[...] = more if block == 0 else agg[...] + more
     for block in range(nodes // EDGE_BLOCK):
         span = slice(block * EDGE_BLOCK, (block + 1) * EDGE_BLOCK)
         summed = dot(agg[span].astype(BF16), w_out_ref[...])
@@ -155,25 +153,11 @@
 
 
 def window_kernel(
-    level_three, parts_ref, state_ref, w_up_ref, gain_ref, parent_ref, l3_hbm,
-    own_ref, pieces_ref, mid_ref, l3_rows_ref, padded, sems,
+    level_three, parts_ref, state_ref, w_up_ref, gain_ref, parent_ref,
+    own_ref, pieces_ref, mid_ref, padded,
 ):
     rows = own_ref.shape[0] // 3
     core = lax.axis_index("core")
-    wide = lax.axis_index("wide")
-    count = lax.axis_size("wide")
-    copies = []
-    for k in range(3):
-        block = lax.rem(wide + (k + count - 1), count)
-        copies.append(
-            pltpu.make_async_copy(
-                l3_hbm.at[pl.ds(pl.multiple_of(block * rows, rows), rows)],
-                l3_rows_ref.at[pl.ds(k * rows, rows)],
-                sems.at[k],
-            )
-        )
-    for copy in copies:
-        copy.start()
     total = parts_ref[0].astype(F32)
     for k in range(1, parts_ref.shape[0]):
         total = total + parts_ref[k].astype(F32)
@@ -192,8 +176,6 @@
         )
         start = jnp.where((core == 1) & ((here >= 2) == (there >= 2)), 5, start)
         pieces_ref[there] = padded[pl.ds(pl.multiple_of(start * rows, rows), 2 * rows)]
-    for copy in copies:
-        copy.wait()
 
 
 def collect_kernel(pieces_ref, out_ref, sums):
@@ -207,13 +189,19 @@
 
 
 def down_kernel(
-    level_three, own_ref, mine_ref, other_ref, l3_rows_ref, gain_ref,
+    level_three, own_ref, mine_ref, other_ref, l3_ref, gain_ref,
     w1_ref, w2_ref, w_down_ref, w_fine_ref, parent_ref, mid_ref, par_ref, fine_ref,
-    fine_out_hbm, down_hbm, fine_out, down_out, sems,
+    fine_out_hbm, down_hbm, fine_out, down_out, lower_fine, sems,
 ):
     rows = own_ref.shape[0] // 3
     total = own_ref[...] + (mine_ref[...].astype(F32) + other_ref[...].astype(F32))
-    mid3 = (l3_rows_ref[...].astype(F32) + rms_scale(total, gain_ref[...])).astype(BF16)
+    wide = lax.axis_index("wide")
+    count = lax.axis_size("wide")
+    state = []
+    for k in range(3):
+        block = lax.rem(wide + (k + count - 1), count)
+        state.append(l3_ref[pl.ds(pl.multiple_of(block * rows, rows), rows)])
+    mid3 = (jnp.concatenate(state, axis=0).astype(F32) + rms_scale(total, gain_ref[...])).astype(BF16)
     hidden = silu(dot(mid3, w1_ref[...])).astype(BF16)
     new = (mid3.astype(F32) + dot(hidden, w2_ref[...])).astype(BF16)
     lower = coarse_parent(parent_ref, rows, level_three).T.astype(BF16)
@@ -226,15 +214,16 @@
     ((par_low, par_high),) = column_parts(par_ref[...])
     for j in range(par_ref.shape[0]):
         hot, high = lane_select(par_low[:, j : j + 1], par_high[:, j : j + 1])
-        lower = jnp.concatenate([pick(hot, high, t) for t in range(fine.shape[0] // LANES)], axis=1)
-        span = slice(j * LANES, (j + 1) * LANES)
-        fine_out[span] = (fine_ref[span].astype(F32) + dot(lower, fine)).astype(BF16)
-        if j % 2 == 1:
-            part = pl.ds((j - 1) * LANES, 2 * LANES)
-            copies.append(
-                pltpu.make_async_copy(fine_out.at[part], fine_out_hbm.at[part], sems.at[(j + 1) // 2])
-            )
-            copies[-1].start()
+        for t in range(fine.shape[0] // LANES):
+            lower_fine[j * LANES : (j + 1) * LANES, t * LANES : (t + 1) * LANES] = pick(hot, high, t)
+    for block in range(fine_out.shape[0] // EDGE_BLOCK):
+        span = slice(block * EDGE_BLOCK, (block + 1) * EDGE_BLOCK)
+        fine_out[span] = (fine_ref[span].astype(F32) + dot(lower_fine[span], fine)).astype(BF16)
+        part = pl.ds(block * EDGE_BLOCK, EDGE_BLOCK)
+        copies.append(
+            pltpu.make_async_copy(fine_out.at[part], fine_out_hbm.at[part], sems.at[block + 1])
+        )
+        copies[-1].start()
     for copy in copies:
         copy.wait()
 
@@ -349,17 +338,16 @@
         part, core_swapped(part)
     )
     chip_sums = lax.all_to_all(chip_sums, "chip", 0, 0, tiled=True)
-    own, pieces, l2_mid, l3_rows = call(
+    own, pieces, l2_mid = call(
         functools.partial(window_kernel, level_three),
         [
             ((3 * rows, width), F32),
             ((4, 2 * rows, width), BF16),
             ((level_two, width), BF16),
-            ((3 * rows, width), BF16),
         ],
-        [pltpu.VMEM((7 * rows, width), BF16), pltpu.SemaphoreType.DMA((3,))],
-        hbm=(5,), nargs=6,
-    )(chip_sums, l2_state, up_weight, l2_gain, parent, l3_state)
+        [pltpu.VMEM((7 * rows, width), BF16)],
+        nargs=5,
+    )(chip_sums, l2_state, up_weight, l2_gain, parent)
     (mine,) = call(
         collect_kernel, [((3 * rows, width), BF16)], [pltpu.VMEM((3 * rows, width), F32)], nargs=1
     )(exchanged(pieces, quads))
@@ -370,11 +358,12 @@
         [
             pltpu.VMEM((nodes, width), BF16),
             pltpu.VMEM((level_two, width), BF16),
-            pltpu.SemaphoreType.DMA((1 + nodes // (2 * LANES),)),
+            pltpu.VMEM((nodes, level_two), BF16),
+            pltpu.SemaphoreType.DMA((1 + nodes // EDGE_BLOCK,)),
         ],
         nargs=13, hbm_outs=True,
     )(
-        own, mine, core_swapped(mine), l3_rows, l3_gain, l3_w1, l3_w2, down_weight, fine_down,
+        own, mine, core_swapped(mine), l3_state, l3_gain, l3_w1, l3_w2, down_weight, fine_down,
         parent, l2_mid, par, fine_mid,
     )
     return (fine_out, l2_down)

time: 66.4 us -> 66.3 us (level)
  no operation moved by 1% of the time
where the time goes in v10:
time: 66.3 us; the launch traced here: 65.9 us
  starting transfers between devices  27.3 us (41%)
  blocking collectives  21.3 us (32%)
  Pallas kernels  11.1 us (17%)
  waiting for transfers between devices  4 us (6%)
  matrix products  1.27 us (2%)
  between operations  0.89 us (1%)
    ppermute x4, starting transfers between devices, core_swapped(): return lax.ppermute(value, 'core', [(0, 1), (1, 0)])  17.1 us
    all_to_all x1, blocking collectives, body(): chip_sums = lax.all_to_all(chip_sums, 'chip', 0, 0, tiled=True)  11.4 us
    all_to_all x1, starting transfers between devices, exchanged(): lax.all_to_all(value, ('wide', 'chip', 'core'), 0, 0, tiled=True, axis_in...  10.2 us
    all_to_all x1, blocking collectives, exchanged(): lax.all_to_all(value, ('wide', 'chip', 'core'), 0, 0, tiled=True, axis_in...  9.83 us
    pallas_call x1, Pallas kernels, body(): call(fine_kernel, [((nodes, width), BF16), ((level_two, width), BF16)], [...  3.64 us
    pallas_call x1, Pallas kernels, body(): call(gather_kernel, [((edges, width), BF16)], [pltpu.VMEM((2 * nodes, wid...  3.17 us
    ppermute x4, waiting for transfers between devices, core_swapped(): return lax.ppermute(value, 'core', [(0, 1), (1, 0)])  2.86 us
    pallas_call x1, Pallas kernels, body(): call(functools.partial(down_kernel, level_three), [((nodes, width), BF16)...  1.93 us
  transfers between devices with their start and end apart: 5, of which 5 were waited for; matrix products, arithmetic and copies ran while one was open for 0% of the time, Pallas kernels for 6%

profile of v10, /device:TPU:1, one launch (start us, length us, event | category | flops | bytes accessed | tf_op | source)
XLA Modules:
  0.0 65.9 jit_solution(5306457266959147173)
XLA Ops:
  0.6 1.3 %convolution_convert_fusion.mine_ref = bf16[16,256]{1,0:T(8,128)(2,1)S(1)} fusion(bf16[1024,256]{1,0:T(8,128)(2,1)} %fs_ref.2, s32[16]{0:T(128)} %param.21), kind=kOutput, calls=%fused_computation | convolution fusion | flops 8409088 | bytes 532544 | tf_op jit(solution)/shard_map/dot_general | solution.py:17
  1.9 0.0 copy-start.13
  1.9 0.0 copy-start.15
  1.9 8.9 %collective-permute-start = (bf16[16,256]{1,0:T(8,128)(2,1)S(1)}, bf16[16,256]{1,0:T(8,128)(2,1)S(1)}, u32[]{:S(2)}, u32[]{:S(2)}) collective-permute-start(bf16[16,256]{1,0:T(8,128)(2,1)S(1)} %convolution_convert_fusion.mine_ref), channel_id=1, source_target_pairs={{0,1},{1,0},{2,3},{3,2},{4,5},{5,4},{6,7},{7,6},{8,9},{9,8},{10,11... | collective-permute-start | bytes 24584 | tf_op jit(solution)/shard_map/ppermute | solution.py:251
  10.9 0.8 %collective-permute-done.other_ref = bf16[16,256]{1,0:T(8,128)(2,1)S(1)} collective-permute-done((bf16[16,256]{1,0:T(8,128)(2,1)S(1)}, bf16[16,256]{1,0:T(8,128)(2,1)S(1)}, u32[]{:S(2)}, u32[]{:S(2)}) %collective-permute-start) | collective-permute-done | bytes 8224 | tf_op jit(solution)/shard_map/ppermute | solution.py:251
  11.7 0.7 %shard_map.185 = bf16[8,32,256]{2,1,0:T(8,128)(2,1)} custom-call(bf16[16,256]{1,0:T(8,128)(2,1)S(1)} %convolution_convert_fusion.mine_ref, bf16[16,256]{1,0:T(8,128)(2,1)S(1)} %collective-permute-done.other_ref), custom_call_target="tpu_custom_call" | custom-call | flops 6000000000 | tf_op jit(solution)/shard_map/pallas_call | solution.py:302
  12.3 10.2 %all-to-all-start = ((bf16[8,32,256]{2,1,0:T(8,128)(2,1)}), bf16[8,32,256]{2,1,0:T(8,128)(2,1)S(1)}, u32[]{:S(2)}, u32[]{:S(2)}) async-start(bf16[8,32,256]{2,1,0:T(8,128)(2,1)} %shard_map.185), calls=%async_computation | async-start | bytes 262144 | tf_op jit(solution)/shard_map/all_to_all | solution.py:245
  22.6 0.0 copy-done.1
  22.6 0.0 copy-done.8
  22.6 0.0 copy-done.13
  22.6 0.0 copy-done.15
  22.6 3.2 %shard_map.186.pre_ref = bf16[2048,256]{1,0:T(8,128)(2,1)S(1)} custom-call(bf16[1024,256]{1,0:T(8,128)(2,1)S(1)} %copy-done.1, bf16[512,256]{1,0:T(8,128)(2,1)S(1)} %copy-done.13, s32[16,128]{1,0:T(8,128)S(1)} %bitcast.19, s32[16,128]{1,0:T(8,128)S(1)} %bitcast.11), custom_call_target="tpu_custom_call" | custom-call | flops 5000000000 | bytes 2000000 | tf_op jit(solution)/shard_map/pallas_call | solution.py:309
  25.8 0.0 copy-start.9
  25.8 0.0 copy-start.14
  25.8 0.0 copy-start.16
  25.8 1.1 %all-to-all-done = bf16[8,32,256]{2,1,0:T(8,128)(2,1)S(1)} async-done(((bf16[8,32,256]{2,1,0:T(8,128)(2,1)}), bf16[8,32,256]{2,1,0:T(8,128)(2,1)S(1)}, u32[]{:S(2)}, u32[]{:S(2)}) %all-to-all-start) | async-done | bytes 131104 | tf_op jit(solution)/shard_map/all_to_all | solution.py:245
  26.9 1.9 %collective-permute-start.1 = (bf16[128,256]{1,0:T(8,128)(2,1)S(1)}, bf16[128,256]{1,0:T(8,128)(2,1)S(1)}, u32[]{:S(2)}, u32[]{:S(2)}) collective-permute-start(bf16[128,256]{1,0:T(8,128)(2,1)S(1)} %shard_map.187), channel_id=1, source_target_pairs={{0,1},{1,0},{2,3},{3,2},{4,5},{5,4},{6,7},{7,6},{8,9},{9,8},{10,11... | collective-permute-start | bytes 196616 | tf_op jit(solution)/shard_map/ppermute | solution.py:251
  28.9 1.0 %shard_map.188.inc_ref = bf16[1024,2048]{1,0:T(8,128)(2,1)S(1)} custom-call(s32[16,128]{1,0:T(8,128)S(1)} %bitcast.12), custom_call_target="tpu_custom_call" | custom-call | flops 1000000000 | bytes 4000000 | tf_op jit(solution)/shard_map/pallas_call | solution.py:319
  29.9 0.2 collective-permute-done.1.far_ref
  30.1 0.0 copy-done.9
  30.1 0.0 copy-done.14
  30.1 0.0 copy-done.16
  30.1 0.0 copy-start.6
  30.1 0.0 copy-start.7
  30.1 0.0 copy-start.10
  30.1 0.0 copy-start.11
  30.1 0.0 copy-start.2
  30.1 0.0 copy-start.3
  30.2 0.0 copy-start.4
  30.2 0.0 copy-start.5
  30.2 0.0 copy-start.12
  30.2 3.6 %shard_map.189 = (bf16[1024,256]{1,0:T(8,128)(2,1)S(1)}, bf16[256,256]{1,0:T(8,128)(2,1)S(1)}) custom-call(bf16[2048,256]{1,0:T(8,128)(2,1)S(1)} %shard_map.186.pre_ref, bf16[2,128,256]{2,1,0:T(8,128)(2,1)S(1)} %bitcast.10, bf16[128,256]{1,0:T(8,128)(2,1)S(1)} %collective-permute-done.1.far_ref, bf16[1024,256]{1,0:T(8,128)(2,1)S(1)} %copy-done.1, ...), custom_call_target="tpu_custom_call" | custom-call | flops 3000000000 | bytes 4000000 | tf_op jit(solution)/shard_map/pallas_call | solution.py:325
  33.8 0.0 copy-start
  33.9 2.4 %collective-permute-start.2 = (bf16[256,256]{1,0:T(8,128)(2,1)S(1)}, bf16[256,256]{1,0:T(8,128)(2,1)S(1)}, u32[]{:S(2)}, u32[]{:S(2)}) collective-permute-start(bf16[256,256]{1,0:T(8,128)(2,1)S(1)} %get-tuple-element.21.a_ref), channel_id=1, source_target_pairs={{0,1},{1,0},{2,3},{3,2},{4,5},{5,4},{6,7},{7,6},{8,9},{9,8},{10,11... | collective-permute-start | bytes 393224 | tf_op jit(solution)/shard_map/ppermute | solution.py:251
  36.3 1.0 %collective-permute-done.2.b_ref = bf16[256,256]{1,0:T(8,128)(2,1)S(1)} collective-permute-done((bf16[256,256]{1,0:T(8,128)(2,1)S(1)}, bf16[256,256]{1,0:T(8,128)(2,1)S(1)}, u32[]{:S(2)}, u32[]{:S(2)}) %collective-permute-start.2) | collective-permute-done | bytes 131104 | tf_op jit(solution)/shard_map/ppermute | solution.py:251
  37.3 11.4 %all_to_all.15.parts_ref = bf16[4,256,256]{2,1,0:T(8,128)(2,1)S(1)} all-to-all(bf16[4,256,256]{2,1,0:T(8,128)(2,1)S(1)} %shard_map.190), channel_id=1, replica_groups=mesh['wide'=64,'chip'=4,'core'=2] {'chip'}, dimensions={0} | all-to-all | bytes 1048576 | tf_op jit(solution)/shard_map/all_to_all | solution.py:340
  48.7 0.0 copy-done.6
  48.7 0.0 copy-done.7
  48.7 0.0 copy-done.11
  48.7 0.5 shard_map.191
  49.2 9.8 %all_to_all.16.pieces_ref = bf16[4,128,256]{2,1,0:T(8,128)(2,1)S(1)} all-to-all(bf16[4,128,256]{2,1,0:T(8,128)(2,1)S(1)} %get-tuple-element.23), channel_id=1, replica_groups={{0,8,16,24},{32,40,48,56},{64,72,80,88},{96,104,112,120},{128,136,144,1..., dimensions={0} | all-to-all | bytes 524288 | tf_op jit(solution)/shard_map/all_to_all | solution.py:245
  59.0 0.1 shard_map.192.mine_ref
  59.1 3.9 %collective-permute-start.3 = (bf16[192,256]{1,0:T(8,128)(2,1)S(1)}, bf16[192,256]{1,0:T(8,128)(2,1)S(1)}, u32[]{:S(2)}, u32[]{:S(2)}) collective-permute-start(bf16[192,256]{1,0:T(8,128)(2,1)S(1)} %shard_map.192.mine_ref), channel_id=1, source_target_pairs={{0,1},{1,0},{2,3},{3,2},{4,5},{5,4},{6,7},{7,6},{8,9},{9,8},{10,11... | collective-permute-start | bytes 294920 | tf_op jit(solution)/shard_map/ppermute | solution.py:251
  63.0 0.9 %collective-permute-done.3.other_ref = bf16[192,256]{1,0:T(8,128)(2,1)S(1)} collective-permute-done((bf16[192,256]{1,0:T(8,128)(2,1)S(1)}, bf16[192,256]{1,0:T(8,128)(2,1)S(1)}, u32[]{:S(2)}, u32[]{:S(2)}) %collective-permute-start.3) | collective-permute-done | bytes 98336 | tf_op jit(solution)/shard_map/ppermute | solution.py:251
  63.9 0.0 copy-done.2
  63.9 0.0 copy-done.12
  63.9 0.0 copy-done
  64.0 1.9 %shard_map.193 = (bf16[1024,256]{1,0:T(8,128)(2,1)}, bf16[256,256]{1,0:T(8,128)(2,1)}) custom-call(f32[192,256]{1,0:T(8,128)S(1)} %get-tuple-element.22.own_ref, bf16[192,256]{1,0:T(8,128)(2,1)S(1)} %shard_map.192.mine_ref, bf16[192,256]{1,0:T(8,128)(2,1)S(1)} %collective-permute-done.3.other_ref, bf16[4096,256]{1,0:T(8,128)(2,1)S(1)} %copy-done, ...), custom_call_target="tpu_custom_call" | custom-call | tf_op jit(solution)/shard_map/pallas_call | solution.py:355
  (8 shorter events, 0.1 us)
Async XLA Ops:
  1.9 20.7 %copy-start.1 = (bf16[1024,256]{1,0:T(8,128)(2,1)S(1)}, bf16[1024,256]{1,0:T(8,128)(2,1)}, u32[]{:S(2)}) copy-start(bf16[1024,256]{1,0:T(8,128)(2,1)} %fs_ref.2) | copy-start | bytes 1572868
  1.9 20.7 %copy-start.8 = (s32[2048]{0:T(1024)S(1)}, s32[2048]{0:T(1024)}, u32[]{:S(2)}) copy-start(s32[2048]{0:T(1024)} %param.23) | copy-start | bytes 24580
  1.9 20.7 %copy-start.13 = (bf16[512,256]{1,0:T(8,128)(2,1)S(1)}, bf16[512,256]{1,0:T(8,128)(2,1)}, u32[]{:S(2)}) copy-start(bf16[512,256]{1,0:T(8,128)(2,1)} %w_in_ref.3) | copy-start | bytes 786436
  1.9 20.7 %copy-start.15 = (s32[2048]{0:T(1024)S(1)}, s32[2048]{0:T(1024)}, u32[]{:S(2)}) copy-start(s32[2048]{0:T(1024)} %param.22) | copy-start | bytes 24580
  1.9 9.7 %collective-permute-start = (bf16[16,256]{1,0:T(8,128)(2,1)S(1)}, bf16[16,256]{1,0:T(8,128)(2,1)S(1)}, u32[]{:S(2)}, u32[]{:S(2)}) collective-permute-start(bf16[16,256]{1,0:T(8,128)(2,1)S(1)} %convolution_convert_fusion.mine_ref), channel_id=1, source_target_pairs={{0,1},{1,0},{2,3},{3,2},{4,5},{5,4},{6,7},{7,6},{8,9},{9,8},{10,11... | collective-permute-start | bytes 24584 | tf_op jit(solution)/shard_map/ppermute | solution.py:251
  12.3 14.6 %all-to-all-start = ((bf16[8,32,256]{2,1,0:T(8,128)(2,1)}), bf16[8,32,256]{2,1,0:T(8,128)(2,1)S(1)}, u32[]{:S(2)}, u32[]{:S(2)}) async-start(bf16[8,32,256]{2,1,0:T(8,128)(2,1)} %shard_map.185), calls=%async_computation | async-start | bytes 262144 | tf_op jit(solution)/shard_map/all_to_all | solution.py:245
  25.8 4.3 %copy-start.9 = (s32[1024]{0:T(1024)S(1)}, s32[1024]{0:T(1024)}, u32[]{:S(2)}) copy-start(s32[1024]{0:T(1024)} %param.24) | copy-start | bytes 12292
  25.8 4.3 %copy-start.14 = (bf16[256,256]{1,0:T(8,128)(2,1)S(1)}, bf16[256,256]{1,0:T(8,128)(2,1)}, u32[]{:S(2)}) copy-start(bf16[256,256]{1,0:T(8,128)(2,1)} %w_out_ref.1) | copy-start | bytes 393220
  25.8 4.3 %copy-start.16 = (f32[256]{0:T(256)S(1)}, f32[256]{0:T(256)}, u32[]{:S(2)}) copy-start(f32[256]{0:T(256)} %param.28) | copy-start | bytes 3076
  26.9 3.1 %collective-permute-start.1 = (bf16[128,256]{1,0:T(8,128)(2,1)S(1)}, bf16[128,256]{1,0:T(8,128)(2,1)S(1)}, u32[]{:S(2)}, u32[]{:S(2)}) collective-permute-start(bf16[128,256]{1,0:T(8,128)(2,1)S(1)} %shard_map.187), channel_id=1, source_target_pairs={{0,1},{1,0},{2,3},{3,2},{4,5},{5,4},{6,7},{7,6},{8,9},{9,8},{10,11... | collective-permute-start | bytes 196616 | tf_op jit(solution)/shard_map/ppermute | solution.py:251
  30.1 18.6 %copy-start.6 = (bf16[256,256]{1,0:T(8,128)(2,1)S(1)}, bf16[256,256]{1,0:T(8,128)(2,1)}, u32[]{:S(2)}) copy-start(bf16[256,256]{1,0:T(8,128)(2,1)} %state_ref.1) | copy-start | bytes 393220
  30.1 18.6 %copy-start.7 = (bf16[256,256]{1,0:T(8,128)(2,1)S(1)}, bf16[256,256]{1,0:T(8,128)(2,1)}, u32[]{:S(2)}) copy-start(bf16[256,256]{1,0:T(8,128)(2,1)} %w_up_ref.1) | copy-start | bytes 393220
  30.1 18.6 %copy-start.10 = (s32[256]{0:T(256)S(1)}, s32[256]{0:T(256)}, u32[]{:S(2)}) copy-start(s32[256]{0:T(256)} %param.25) | copy-start | bytes 3076
  30.1 18.6 %copy-start.11 = (f32[256]{0:T(256)S(1)}, f32[256]{0:T(256)}, u32[]{:S(2)}) copy-start(f32[256]{0:T(256)} %param.30) | copy-start | bytes 3076
  30.1 33.8 %copy-start.2 = (bf16[256,256]{1,0:T(8,128)(2,1)S(1)}, bf16[256,256]{1,0:T(8,128)(2,1)}, u32[]{:S(2)}) copy-start(bf16[256,256]{1,0:T(8,128)(2,1)} %w1_ref.1) | copy-start | bytes 393220
  30.1 33.8 %copy-start.3 = (bf16[256,256]{1,0:T(8,128)(2,1)S(1)}, bf16[256,256]{1,0:T(8,128)(2,1)}, u32[]{:S(2)}) copy-start(bf16[256,256]{1,0:T(8,128)(2,1)} %w2_ref.1) | copy-start | bytes 393220
  30.2 33.8 %copy-start.4 = (bf16[256,256]{1,0:T(8,128)(2,1)S(1)}, bf16[256,256]{1,0:T(8,128)(2,1)}, u32[]{:S(2)}) copy-start(bf16[256,256]{1,0:T(8,128)(2,1)} %w_down_ref.1) | copy-start | bytes 393220
  30.2 33.8 %copy-start.5 = (bf16[256,256]{1,0:T(8,128)(2,1)S(1)}, bf16[256,256]{1,0:T(8,128)(2,1)}, u32[]{:S(2)}) copy-start(bf16[256,256]{1,0:T(8,128)(2,1)} %w_fine_ref.1) | copy-start | bytes 393220
  30.2 33.8 %copy-start.12 = (f32[256]{0:T(256)S(1)}, f32[256]{0:T(256)}, u32[]{:S(2)}) copy-start(f32[256]{0:T(256)} %param.31) | copy-start | bytes 3076
  33.8 30.1 %copy-start = (bf16[4096,256]{1,0:T(8,128)(2,1)S(1)}, bf16[4096,256]{1,0:T(8,128)(2,1)}, u32[]{:S(2)}) copy-start(bf16[4096,256]{1,0:T(8,128)(2,1)} %l3_ref.1) | copy-start | bytes 6291460
  33.9 3.4 %collective-permute-start.2 = (bf16[256,256]{1,0:T(8,128)(2,1)S(1)}, bf16[256,256]{1,0:T(8,128)(2,1)S(1)}, u32[]{:S(2)}, u32[]{:S(2)}) collective-permute-start(bf16[256,256]{1,0:T(8,128)(2,1)S(1)} %get-tuple-element.21.a_ref), channel_id=1, source_target_pairs={{0,1},{1,0},{2,3},{3,2},{4,5},{5,4},{6,7},{7,6},{8,9},{9,8},{10,11... | collective-permute-start | bytes 393224 | tf_op jit(solution)/shard_map/ppermute | solution.py:251
  59.1 4.8 %collective-permute-start.3 = (bf16[192,256]{1,0:T(8,128)(2,1)S(1)}, bf16[192,256]{1,0:T(8,128)(2,1)S(1)}, u32[]{:S(2)}, u32[]{:S(2)}) collective-permute-start(bf16[192,256]{1,0:T(8,128)(2,1)S(1)} %shard_map.192.mine_ref), channel_id=1, source_target_pairs={{0,1},{1,0},{2,3},{3,2},{4,5},{5,4},{6,7},{7,6},{8,9},{9,8},{10,11... | collective-permute-start | bytes 294920 | tf_op jit(solution)/shard_map/ppermute | solution.py:251

commit v11 on v10

--- a/solution.py
+++ b/solution.py
@@ -11,6 +11,7 @@
 BF16 = jnp.bfloat16
 LANES = 128
 EDGE_BLOCK = 512
+FINE_BLOCK = 1024
 
 
 def dot(a, b):
@@ -119,9 +120,9 @@
         hot_p, high_p = row_select(par_ref[j : j + 1])
         for t in range(upper.shape[0] // LANES):
             upper[t * LANES : (t + 1) * LANES, j * LANES : (j + 1) * LANES] = pick(hot_p, high_p, t)
-    for block in range(edges // EDGE_BLOCK):
-        span = slice(block * EDGE_BLOCK, (block + 1) * EDGE_BLOCK)
-        for j in range(block * EDGE_BLOCK // LANES, (block + 1) * EDGE_BLOCK // LANES):
+    for block in range(edges // FINE_BLOCK):
+        span = slice(block * FINE_BLOCK, (block + 1) * FINE_BLOCK)
+        for j in range(block * FINE_BLOCK // LANES, (block + 1) * FINE_BLOCK // LANES):
             hot_s, high_s = lane_select(low[:, j : j + 1], high[:, j : j + 1])
             for t in range(hot.shape[1] // LANES):
                 hot[j * LANES : (j + 1) * LANES, t * LANES : (t + 1) * LANES] = pick(

time: 66.3 us -> 66.1 us (level)
  no operation moved by 1% of the time
where the time goes in v11:
time: 66.1 us; the launch traced here: 65.7 us
  starting transfers between devices  27.3 us (41%)
  blocking collectives  21.3 us (32%)
  Pallas kernels  10.9 us (16%)
  waiting for transfers between devices  4.01 us (6%)
  matrix products  1.27 us (2%)
  between operations  0.89 us (1%)
    ppermute x4, starting transfers between devices, core_swapped(): return lax.ppermute(value, 'core', [(0, 1), (1, 0)])  17.1 us
    all_to_all x1, blocking collectives, body(): chip_sums = lax.all_to_all(chip_sums, 'chip', 0, 0, tiled=True)  11.4 us
    all_to_all x1, starting transfers between devices, exchanged(): lax.all_to_all(value, ('wide', 'chip', 'core'), 0, 0, tiled=True, axis_in...  10.2 us
    all_to_all x1, blocking collectives, exchanged(): lax.all_to_all(value, ('wide', 'chip', 'core'), 0, 0, tiled=True, axis_in...  9.85 us
    pallas_call x1, Pallas kernels, body(): call(fine_kernel, [((nodes, width), BF16), ((level_two, width), BF16)], [...  3.5 us
    pallas_call x1, Pallas kernels, body(): call(gather_kernel, [((edges, width), BF16)], [pltpu.VMEM((2 * nodes, wid...  3.17 us
    ppermute x4, waiting for transfers between devices, core_swapped(): return lax.ppermute(value, 'core', [(0, 1), (1, 0)])  2.88 us
    pallas_call x1, Pallas kernels, body(): call(functools.partial(down_kernel, level_three), [((nodes, width), BF16)...  1.92 us
  transfers between devices with their start and end apart: 5, of which 5 were waited for; matrix products, arithmetic and copies ran while one was open for 0% of the time, Pallas kernels for 6%

profile of v11, /device:TPU:1, one launch (start us, length us, event | category | flops | bytes accessed | tf_op | source)
XLA Modules:
  0.0 65.7 jit_solution(12795067750664279423)
XLA Ops:
  0.6 1.3 %convolution_convert_fusion.mine_ref = bf16[16,256]{1,0:T(8,128)(2,1)S(1)} fusion(bf16[1024,256]{1,0:T(8,128)(2,1)} %fs_ref.2, s32[16]{0:T(128)} %param.21), kind=kOutput, calls=%fused_computation | convolution fusion | flops 8409088 | bytes 532544 | tf_op jit(solution)/shard_map/dot_general | solution.py:18
  1.9 0.0 copy-start.13
  1.9 0.0 copy-start.15
  1.9 8.9 %collective-permute-start = (bf16[16,256]{1,0:T(8,128)(2,1)S(1)}, bf16[16,256]{1,0:T(8,128)(2,1)S(1)}, u32[]{:S(2)}, u32[]{:S(2)}) collective-permute-start(bf16[16,256]{1,0:T(8,128)(2,1)S(1)} %convolution_convert_fusion.mine_ref), channel_id=1, source_target_pairs={{0,1},{1,0},{2,3},{3,2},{4,5},{5,4},{6,7},{7,6},{8,9},{9,8},{10,11... | collective-permute-start | bytes 24584 | tf_op jit(solution)/shard_map/ppermute | solution.py:252
  10.9 0.8 %collective-permute-done.other_ref = bf16[16,256]{1,0:T(8,128)(2,1)S(1)} collective-permute-done((bf16[16,256]{1,0:T(8,128)(2,1)S(1)}, bf16[16,256]{1,0:T(8,128)(2,1)S(1)}, u32[]{:S(2)}, u32[]{:S(2)}) %collective-permute-start) | collective-permute-done | bytes 8224 | tf_op jit(solution)/shard_map/ppermute | solution.py:252
  11.7 0.7 %shard_map.185 = bf16[8,32,256]{2,1,0:T(8,128)(2,1)} custom-call(bf16[16,256]{1,0:T(8,128)(2,1)S(1)} %convolution_convert_fusion.mine_ref, bf16[16,256]{1,0:T(8,128)(2,1)S(1)} %collective-permute-done.other_ref), custom_call_target="tpu_custom_call" | custom-call | flops 6000000000 | tf_op jit(solution)/shard_map/pallas_call | solution.py:303
  12.3 10.2 %all-to-all-start = ((bf16[8,32,256]{2,1,0:T(8,128)(2,1)}), bf16[8,32,256]{2,1,0:T(8,128)(2,1)S(1)}, u32[]{:S(2)}, u32[]{:S(2)}) async-start(bf16[8,32,256]{2,1,0:T(8,128)(2,1)} %shard_map.185), calls=%async_computation | async-start | bytes 262144 | tf_op jit(solution)/shard_map/all_to_all | solution.py:246
  22.6 0.0 copy-done.1
  22.6 0.0 copy-done.8
  22.6 0.0 copy-done.13
  22.6 0.0 copy-done.15
  22.6 3.2 %shard_map.186.pre_ref = bf16[2048,256]{1,0:T(8,128)(2,1)S(1)} custom-call(bf16[1024,256]{1,0:T(8,128)(2,1)S(1)} %copy-done.1, bf16[512,256]{1,0:T(8,128)(2,1)S(1)} %copy-done.13, s32[16,128]{1,0:T(8,128)S(1)} %bitcast.19, s32[16,128]{1,0:T(8,128)S(1)} %bitcast.11), custom_call_target="tpu_custom_call" | custom-call | flops 5000000000 | bytes 2000000 | tf_op jit(solution)/shard_map/pallas_call | solution.py:310
  25.8 0.0 copy-start.9
  25.8 0.0 copy-start.14
  25.8 0.0 copy-start.16
  25.8 1.1 %all-to-all-done = bf16[8,32,256]{2,1,0:T(8,128)(2,1)S(1)} async-done(((bf16[8,32,256]{2,1,0:T(8,128)(2,1)}), bf16[8,32,256]{2,1,0:T(8,128)(2,1)S(1)}, u32[]{:S(2)}, u32[]{:S(2)}) %all-to-all-start) | async-done | bytes 131104 | tf_op jit(solution)/shard_map/all_to_all | solution.py:246
  26.9 1.9 %collective-permute-start.1 = (bf16[128,256]{1,0:T(8,128)(2,1)S(1)}, bf16[128,256]{1,0:T(8,128)(2,1)S(1)}, u32[]{:S(2)}, u32[]{:S(2)}) collective-permute-start(bf16[128,256]{1,0:T(8,128)(2,1)S(1)} %shard_map.187), channel_id=1, source_target_pairs={{0,1},{1,0},{2,3},{3,2},{4,5},{5,4},{6,7},{7,6},{8,9},{9,8},{10,11... | collective-permute-start | bytes 196616 | tf_op jit(solution)/shard_map/ppermute | solution.py:252
  28.9 1.0 %shard_map.188.inc_ref = bf16[1024,2048]{1,0:T(8,128)(2,1)S(1)} custom-call(s32[16,128]{1,0:T(8,128)S(1)} %bitcast.12), custom_call_target="tpu_custom_call" | custom-call | flops 1000000000 | bytes 4000000 | tf_op jit(solution)/shard_map/pallas_call | solution.py:320
  29.9 0.2 collective-permute-done.1.far_ref
  30.1 0.0 copy-done.9
  30.1 0.0 copy-done.14
  30.1 0.0 copy-done.16
  30.1 0.0 copy-start.6
  30.1 0.0 copy-start.7
  30.1 0.0 copy-start.10
  30.1 0.0 copy-start.11
  30.1 0.0 copy-start.2
  30.1 0.0 copy-start.3
  30.2 0.0 copy-start.4
  30.2 0.0 copy-start.5
  30.2 0.0 copy-start.12
  30.2 3.5 %shard_map.189 = (bf16[1024,256]{1,0:T(8,128)(2,1)S(1)}, bf16[256,256]{1,0:T(8,128)(2,1)S(1)}) custom-call(bf16[2048,256]{1,0:T(8,128)(2,1)S(1)} %shard_map.186.pre_ref, bf16[2,128,256]{2,1,0:T(8,128)(2,1)S(1)} %bitcast.10, bf16[128,256]{1,0:T(8,128)(2,1)S(1)} %collective-permute-done.1.far_ref, bf16[1024,256]{1,0:T(8,128)(2,1)S(1)} %copy-done.1, ...), custom_call_target="tpu_custom_call" | custom-call | flops 3000000000 | bytes 4000000 | tf_op jit(solution)/shard_map/pallas_call | solution.py:326
  33.7 0.0 copy-start
  33.7 2.4 %collective-permute-start.2 = (bf16[256,256]{1,0:T(8,128)(2,1)S(1)}, bf16[256,256]{1,0:T(8,128)(2,1)S(1)}, u32[]{:S(2)}, u32[]{:S(2)}) collective-permute-start(bf16[256,256]{1,0:T(8,128)(2,1)S(1)} %get-tuple-element.21.a_ref), channel_id=1, source_target_pairs={{0,1},{1,0},{2,3},{3,2},{4,5},{5,4},{6,7},{7,6},{8,9},{9,8},{10,11... | collective-permute-start | bytes 393224 | tf_op jit(solution)/shard_map/ppermute | solution.py:252
  36.1 1.0 %collective-permute-done.2.b_ref = bf16[256,256]{1,0:T(8,128)(2,1)S(1)} collective-permute-done((bf16[256,256]{1,0:T(8,128)(2,1)S(1)}, bf16[256,256]{1,0:T(8,128)(2,1)S(1)}, u32[]{:S(2)}, u32[]{:S(2)}) %collective-permute-start.2) | collective-permute-done | bytes 131104 | tf_op jit(solution)/shard_map/ppermute | solution.py:252
  37.1 11.4 %all_to_all.15.parts_ref = bf16[4,256,256]{2,1,0:T(8,128)(2,1)S(1)} all-to-all(bf16[4,256,256]{2,1,0:T(8,128)(2,1)S(1)} %shard_map.190), channel_id=1, replica_groups=mesh['wide'=64,'chip'=4,'core'=2] {'chip'}, dimensions={0} | all-to-all | bytes 1048576 | tf_op jit(solution)/shard_map/all_to_all | solution.py:341
  48.5 0.0 copy-done.6
  48.5 0.0 copy-done.7
  48.6 0.0 copy-done.10
  48.6 0.0 copy-done.11
  48.6 0.5 shard_map.191
  49.1 9.8 %all_to_all.16.pieces_ref = bf16[4,128,256]{2,1,0:T(8,128)(2,1)S(1)} all-to-all(bf16[4,128,256]{2,1,0:T(8,128)(2,1)S(1)} %get-tuple-element.23), channel_id=1, replica_groups={{0,8,16,24},{32,40,48,56},{64,72,80,88},{96,104,112,120},{128,136,144,1..., dimensions={0} | all-to-all | bytes 524288 | tf_op jit(solution)/shard_map/all_to_all | solution.py:246
  58.9 0.1 shard_map.192.mine_ref
  59.0 3.9 %collective-permute-start.3 = (bf16[192,256]{1,0:T(8,128)(2,1)S(1)}, bf16[192,256]{1,0:T(8,128)(2,1)S(1)}, u32[]{:S(2)}, u32[]{:S(2)}) collective-permute-start(bf16[192,256]{1,0:T(8,128)(2,1)S(1)} %shard_map.192.mine_ref), channel_id=1, source_target_pairs={{0,1},{1,0},{2,3},{3,2},{4,5},{5,4},{6,7},{7,6},{8,9},{9,8},{10,11... | collective-permute-start | bytes 294920 | tf_op jit(solution)/shard_map/ppermute | solution.py:252
  62.9 0.9 %collective-permute-done.3.other_ref = bf16[192,256]{1,0:T(8,128)(2,1)S(1)} collective-permute-done((bf16[192,256]{1,0:T(8,128)(2,1)S(1)}, bf16[192,256]{1,0:T(8,128)(2,1)S(1)}, u32[]{:S(2)}, u32[]{:S(2)}) %collective-permute-start.3) | collective-permute-done | bytes 98336 | tf_op jit(solution)/shard_map/ppermute | solution.py:252
  63.8 0.0 copy-done.2
  63.8 0.0 copy-done.3
  63.8 1.9 %shard_map.193 = (bf16[1024,256]{1,0:T(8,128)(2,1)}, bf16[256,256]{1,0:T(8,128)(2,1)}) custom-call(f32[192,256]{1,0:T(8,128)S(1)} %get-tuple-element.22.own_ref, bf16[192,256]{1,0:T(8,128)(2,1)S(1)} %shard_map.192.mine_ref, bf16[192,256]{1,0:T(8,128)(2,1)S(1)} %collective-permute-done.3.other_ref, bf16[4096,256]{1,0:T(8,128)(2,1)S(1)} %copy-done, ...), custom_call_target="tpu_custom_call" | custom-call | tf_op jit(solution)/shard_map/pallas_call | solution.py:356
  (8 shorter events, 0.1 us)
Async XLA Ops:
  1.9 20.7 %copy-start.1 = (bf16[1024,256]{1,0:T(8,128)(2,1)S(1)}, bf16[1024,256]{1,0:T(8,128)(2,1)}, u32[]{:S(2)}) copy-start(bf16[1024,256]{1,0:T(8,128)(2,1)} %fs_ref.2) | copy-start | bytes 1572868
  1.9 20.7 %copy-start.8 = (s32[2048]{0:T(1024)S(1)}, s32[2048]{0:T(1024)}, u32[]{:S(2)}) copy-start(s32[2048]{0:T(1024)} %param.23) | copy-start | bytes 24580
  1.9 20.7 %copy-start.13 = (bf16[512,256]{1,0:T(8,128)(2,1)S(1)}, bf16[512,256]{1,0:T(8,128)(2,1)}, u32[]{:S(2)}) copy-start(bf16[512,256]{1,0:T(8,128)(2,1)} %w_in_ref.3) | copy-start | bytes 786436
  1.9 20.7 %copy-start.15 = (s32[2048]{0:T(1024)S(1)}, s32[2048]{0:T(1024)}, u32[]{:S(2)}) copy-start(s32[2048]{0:T(1024)} %param.22) | copy-start | bytes 24580
  1.9 9.7 %collective-permute-start = (bf16[16,256]{1,0:T(8,128)(2,1)S(1)}, bf16[16,256]{1,0:T(8,128)(2,1)S(1)}, u32[]{:S(2)}, u32[]{:S(2)}) collective-permute-start(bf16[16,256]{1,0:T(8,128)(2,1)S(1)} %convolution_convert_fusion.mine_ref), channel_id=1, source_target_pairs={{0,1},{1,0},{2,3},{3,2},{4,5},{5,4},{6,7},{7,6},{8,9},{9,8},{10,11... | collective-permute-start | bytes 24584 | tf_op jit(solution)/shard_map/ppermute | solution.py:252
  12.3 14.6 %all-to-all-start = ((bf16[8,32,256]{2,1,0:T(8,128)(2,1)}), bf16[8,32,256]{2,1,0:T(8,128)(2,1)S(1)}, u32[]{:S(2)}, u32[]{:S(2)}) async-start(bf16[8,32,256]{2,1,0:T(8,128)(2,1)} %shard_map.185), calls=%async_computation | async-start | bytes 262144 | tf_op jit(solution)/shard_map/all_to_all | solution.py:246
  25.8 4.3 %copy-start.9 = (s32[1024]{0:T(1024)S(1)}, s32[1024]{0:T(1024)}, u32[]{:S(2)}) copy-start(s32[1024]{0:T(1024)} %param.24) | copy-start | bytes 12292
  25.8 4.3 %copy-start.14 = (bf16[256,256]{1,0:T(8,128)(2,1)S(1)}, bf16[256,256]{1,0:T(8,128)(2,1)}, u32[]{:S(2)}) copy-start(bf16[256,256]{1,0:T(8,128)(2,1)} %w_out_ref.1) | copy-start | bytes 393220
  25.8 4.3 %copy-start.16 = (f32[256]{0:T(256)S(1)}, f32[256]{0:T(256)}, u32[]{:S(2)}) copy-start(f32[256]{0:T(256)} %param.28) | copy-start | bytes 3076
  26.9 3.1 %collective-permute-start.1 = (bf16[128,256]{1,0:T(8,128)(2,1)S(1)}, bf16[128,256]{1,0:T(8,128)(2,1)S(1)}, u32[]{:S(2)}, u32[]{:S(2)}) collective-permute-start(bf16[128,256]{1,0:T(8,128)(2,1)S(1)} %shard_map.187), channel_id=1, source_target_pairs={{0,1},{1,0},{2,3},{3,2},{4,5},{5,4},{6,7},{7,6},{8,9},{9,8},{10,11... | collective-permute-start | bytes 196616 | tf_op jit(solution)/shard_map/ppermute | solution.py:252
  30.1 18.5 %copy-start.6 = (bf16[256,256]{1,0:T(8,128)(2,1)S(1)}, bf16[256,256]{1,0:T(8,128)(2,1)}, u32[]{:S(2)}) copy-start(bf16[256,256]{1,0:T(8,128)(2,1)} %state_ref.1) | copy-start | bytes 393220
  30.1 18.5 %copy-start.7 = (bf16[256,256]{1,0:T(8,128)(2,1)S(1)}, bf16[256,256]{1,0:T(8,128)(2,1)}, u32[]{:S(2)}) copy-start(bf16[256,256]{1,0:T(8,128)(2,1)} %w_up_ref.1) | copy-start | bytes 393220
  30.1 18.4 %copy-start.10 = (s32[256]{0:T(256)S(1)}, s32[256]{0:T(256)}, u32[]{:S(2)}) copy-start(s32[256]{0:T(256)} %param.25) | copy-start | bytes 3076
  30.1 18.4 %copy-start.11 = (f32[256]{0:T(256)S(1)}, f32[256]{0:T(256)}, u32[]{:S(2)}) copy-start(f32[256]{0:T(256)} %param.30) | copy-start | bytes 3076
  30.1 33.7 %copy-start.2 = (bf16[256,256]{1,0:T(8,128)(2,1)S(1)}, bf16[256,256]{1,0:T(8,128)(2,1)}, u32[]{:S(2)}) copy-start(bf16[256,256]{1,0:T(8,128)(2,1)} %w1_ref.1) | copy-start | bytes 393220
  30.1 33.6 %copy-start.3 = (bf16[256,256]{1,0:T(8,128)(2,1)S(1)}, bf16[256,256]{1,0:T(8,128)(2,1)}, u32[]{:S(2)}) copy-start(bf16[256,256]{1,0:T(8,128)(2,1)} %w2_ref.1) | copy-start | bytes 393220
  30.2 33.6 %copy-start.4 = (bf16[256,256]{1,0:T(8,128)(2,1)S(1)}, bf16[256,256]{1,0:T(8,128)(2,1)}, u32[]{:S(2)}) copy-start(bf16[256,256]{1,0:T(8,128)(2,1)} %w_down_ref.1) | copy-start | bytes 393220
  30.2 33.6 %copy-start.5 = (bf16[256,256]{1,0:T(8,128)(2,1)S(1)}, bf16[256,256]{1,0:T(8,128)(2,1)}, u32[]{:S(2)}) copy-start(bf16[256,256]{1,0:T(8,128)(2,1)} %w_fine_ref.1) | copy-start | bytes 393220
  30.2 33.6 %copy-start.12 = (f32[256]{0:T(256)S(1)}, f32[256]{0:T(256)}, u32[]{:S(2)}) copy-start(f32[256]{0:T(256)} %param.31) | copy-start | bytes 3076
  33.7 30.1 %copy-start = (bf16[4096,256]{1,0:T(8,128)(2,1)S(1)}, bf16[4096,256]{1,0:T(8,128)(2,1)}, u32[]{:S(2)}) copy-start(bf16[4096,256]{1,0:T(8,128)(2,1)} %l3_ref.1) | copy-start | bytes 6291460
  33.7 3.4 %collective-permute-start.2 = (bf16[256,256]{1,0:T(8,128)(2,1)S(1)}, bf16[256,256]{1,0:T(8,128)(2,1)S(1)}, u32[]{:S(2)}, u32[]{:S(2)}) collective-permute-start(bf16[256,256]{1,0:T(8,128)(2,1)S(1)} %get-tuple-element.21.a_ref), channel_id=1, source_target_pairs={{0,1},{1,0},{2,3},{3,2},{4,5},{5,4},{6,7},{7,6},{8,9},{9,8},{10,11... | collective-permute-start | bytes 393224 | tf_op jit(solution)/shard_map/ppermute | solution.py:252
  59.0 4.8 %collective-permute-start.3 = (bf16[192,256]{1,0:T(8,128)(2,1)S(1)}, bf16[192,256]{1,0:T(8,128)(2,1)S(1)}, u32[]{:S(2)}, u32[]{:S(2)}) collective-permute-start(bf16[192,256]{1,0:T(8,128)(2,1)S(1)} %shard_map.192.mine_ref), channel_id=1, source_target_pairs={{0,1},{1,0},{2,3},{3,2},{4,5},{5,4},{6,7},{7,6},{8,9},{9,8},{10,11... | collective-permute-start | bytes 294920 | tf_op jit(solution)/shard_map/ppermute | solution.py:252
